TPU v7x, 128 devices: a whole 4x4x4 slice. The times are simulated.
128 devices in a mesh: comp: 2 (over y_lo), lat: 8 (over y_hi, z), lon: 8 (over x, core).
Axes of the slice: x: 4, y: 4 (y_hi: 2, y_lo: 2; y = y_hi * 2 + y_lo), z: 4, core: 2. Of those that a mesh axis runs over, the one named last changes fastest.
Arguments:
- adjoint_state: float32 [2, 32, 256, 1024], P('comp', None, 'lat', 'lon'), may hold values from -6 to 6
- winds: float32 [2, 2, 32, 256, 1024], P(None, 'comp', None, 'lat', 'lon'), may hold values from -0.3 to 0.3
- block_inverse: float32 [2, 8, 4, 4, 256, 1024], P('comp', None, None, None, 'lat', 'lon'), may hold values from -0.5 to 1.5
- flux_coef: float32 [2, 4, 256, 1024], P('comp', None, 'lat', 'lon'), may hold values from 0.2 to 1
- sea_mask: int32 [256, 1024], P('lat', 'lon'), may hold values 0 or 1
- intersection_cell: int32 [2, 4, 256, 1024], P(None, None, 'lat', 'lon'), may hold values from 0 to 1023, as said below
- intersection_weight: float32 [4, 256, 1024], P(None, 'lat', 'lon'), may hold values from 0.1 to 1
- fold_map: int32 [1024], replicated, may hold values from 0 to 1023, as said below
Outputs:
- adjoint_final: float32 [2, 32, 256, 1024], P('comp', None, 'lat', 'lon')
Inputs may be any that keep to these rules, and one draw needn't show every extreme that they name: intersection_cell[0, k, i, j] lies within one row of i, intersection_cell[1, k, i, j] within one column of j counted periodically; entry k = 0 is the cell (i, j) itself. fold_map[j] = (o - j) mod 1024 for one offset o of 0 to 1023, the same for every j; so fold_map[fold_map[j]] = j.
All inputs are finite; a program needn't handle non-finite values. No bound on the sum of `sea_mask` on one device may be relied on, other than what follows from the above.
Results may differ from a plain program's by a relative error of at most 0.0001.
Values sent between devices are 32-bit elements; how exact they have to be, the bound alone decides.
No kernel may reach another device: no remote copies, remote signals or barrier semaphores. Data moves between devices by JAX's collectives and lax.ppermute only.
A program may use at most 128 MiB of HBM per device.

v0:
```python
import functools

import jax
import jax.numpy as jnp
from jax import lax
from jax.experimental import pallas as pl
from jax.experimental.pallas import tpu as pltpu
from jax.sharding import PartitionSpec as P

DIFFUSE = 0.15
ROWS = 32
EXT = 48
COLS = 128
BLOCKS = 8
F32 = jnp.float32
AXES = ("comp", "lat", "lon")
LAT, LON = 8, 8
VMEM = pl.BlockSpec(memory_space=pltpu.VMEM)
ANY = pl.BlockSpec(memory_space=pl.ANY)
HBM = pl.BlockSpec(memory_space=pltpu.HBM)
SMEM = pl.BlockSpec(memory_space=pltpu.SMEM)
PARAMS = pltpu.CompilerParams(vmem_limit_bytes=16 * 1024 * 1024)
FULL = pltpu.CompilerParams(vmem_limit_bytes=63 * 1024 * 1024)


def places():
    comp, lat, lon = (lax.axis_index(name) for name in AXES)
    return comp, lat, lon, lat == LAT - 1


def first_pieces():
    pieces = []
    for a in range(4):
        pieces.append((0, 0, a, 8 * a, 8))
        pieces.append((1, 0, a, 32 + 8 * a, 8))
        pieces.append((2, 0, a, 64 + 7 * a, 7))
    for b in range(4):
        pieces.append((3 + b, 0, 0, 92 + 5 * b, 5))
        for a in range(1, 4):
            pieces.append((3 + b, 0, a, 120 + 4 * (4 * (a - 1) + b), 4))
    return pieces


def rest_pieces():
    pieces = []
    for n in range(1, BLOCKS):
        at = 240 + 32 * (n - 1)
        for a in range(4):
            pieces.append((0, n, a, at + 3 * a, 3))
            pieces.append((1, n, a, at + 12 + 3 * a, 3))
            pieces.append((2, n, a, at + 24 + 2 * a, 2))
    return pieces


ROW_BUFFER = 240 + 32 * (BLOCKS - 1)
SINGLES = (
    [(0, f, 168 + 5 * f, 5) for f in range(4)]
    + [(1 + s // 4, s % 4, 188 + 4 * s, 4) for s in range(9)]
    + [(3, 1, 112, 8), (3, 2, 224, 8)]
)


def mirrored_single(quad, member):
    if quad in (1, 2) or (quad == 3 and member == 0):
        s = 8 - (4 * (quad - 1) + member)
        return 1 + s // 4, s % 4
    return quad, member


def copy_all(pairs, sem):
    copies = [pltpu.make_async_copy(a, b, sem.at[k]) for k, (a, b) in enumerate(pairs)]
    for copy in copies:
        copy.start()
    for copy in copies:
        copy.wait()


def reverse(tile):
    flip = 7 - lax.broadcasted_iota(jnp.int32, (8, COLS), 0)
    return jnp.take_along_axis(tile, flip, axis=0, mode="promise_in_bounds")


def put_piece(store, ref, other, at, count, mirrored_sign):
    end = ref.shape[0]
    store[0, at : at + count, :] = ref[end - count : end, :]
    store[1, at : at + count, :] = ref[0:count, :]
    turned = reverse(other[end - 8 : end, :])
    if mirrored_sign < 0:
        turned = -turned
    store[2, at : at + count, :] = turned[0:count, :]


def field_ref(lam, winds, inv, field, n, a):
    if field == 0:
        return lam.at[4 * n + a]
    if field <= 2:
        return winds.at[2 - field, 4 * n + a]
    return inv.at[n, a, field - 3]


def sign_of(field):
    return -1 if field in (1, 2) else 1


def hand_over(store, first_out, second_out, mirror_out):
    _, lat, _, _ = places()
    odd = lat % 2
    first_out[...] = store[odd]
    second_out[...] = store[1 - odd]
    mirror_out[...] = store[2]


def start_rows_kernel(
    fold, lam_in, winds_in, inv_in, fc_in, mask_in, cell_in, weight_in,
    x_out, first_out, second_out, mirror_out, turn_out,
    store, lam, winds, inv, fc, mask, cell, weight, sem,
):
    comp, lat_pos, lon_pos, _ = places()
    turn_out[0] = fold[0] // COLS
    pairs = [(fc_in, fc), (mask_in, mask), (cell_in, cell), (weight_in, weight)]
    for half, rows in enumerate((pl.ds(0, 8), pl.ds(ROWS - 8, 8))):
        at = pl.ds(8 * half, 8)
        pairs.append((lam_in.at[:, rows], lam.at[:, at]))
        pairs.append((winds_in.at[:, :, rows], winds.at[:, :, at]))
        pairs.append((inv_in.at[pl.ds(0, 1), :, :, rows], inv.at[:, :, :, at]))
    copy_all(pairs, sem)
    wet = mask[...].astype(F32)
    x_out[3, 1] = wet
    x_out[3, 2] = jnp.where(comp == 1, wet, jnp.ones_like(wet))
    x_out[3, 3] = jnp.zeros_like(wet)
    for f in range(4):
        x_out[0, f] = fc[f]
    rows = lat_pos * ROWS + lax.broadcasted_iota(jnp.int32, (ROWS, COLS), 0)
    cols = lon_pos * COLS + lax.broadcasted_iota(jnp.int32, (ROWS, COLS), 1)
    row_shift = [cell[0, k] - rows for k in range(4)]
    col_shift = []
    for k in range(4):
        d = cell[1, k] - cols
        d = jnp.where(d > 1, d - LON * COLS, d)
        col_shift.append(jnp.where(d < -1, d + LON * COLS, d))
    code = [3 * row_shift[k] + col_shift[k] + 4 for k in range(4)]
    weights = [weight[k] for k in range(4)]
    for s in range(9):
        total = jnp.where(code[0] == s, weights[0], 0.0)
        for k in range(1, 4):
            total = total + jnp.where(code[k] == s, weights[k], 0.0)
        x_out[1 + s // 4, s % 4] = total
    for field, n, a, at, count in first_pieces() + rest_pieces():
        ref = field_ref(lam, winds, inv, field, n, a)
        put_piece(store, ref, ref, at, count, sign_of(field))
    for quad, member, at, count in SINGLES:
        put_piece(store, x_out.at[quad, member], x_out.at[mirrored_single(quad, member)], at, count, 1)
    hand_over(store, first_out, second_out, mirror_out)


def lanes():
    return lax.broadcasted_iota(jnp.int32, (8, COLS), 1)


def roll_lanes(x, by):
    by = by % COLS
    return x if by == 0 else pltpu.roll(x, by, axis=1)


def roll_rows(x, by):
    by = by % x.shape[0]
    return x if by == 0 else pltpu.roll(x, by, axis=0)


def pack_columns(slots, own, own_at, to_west, to_east, buffer_at, row_count):
    rows = row_count
    used = [k for k, members in enumerate(slots) if members is not None]
    zero = jnp.zeros((rows, COLS), F32)
    lane = lax.broadcasted_iota(jnp.int32, (len(used) * rows, COLS), 1)
    pair = jnp.zeros((len(used) * rows, COLS), F32)
    for a in range(4):
        values = [zero if slots[k][a] is None else slots[k][a] for k in used]
        moved = roll_lanes(jnp.concatenate(values, axis=0), 32 * a + 8)
        pair = jnp.where((lane >= 32 * a) & (lane < 32 * a + 16), moved, pair)
    strips = jnp.where(lane % 32 < 16, pair, roll_lanes(pair, 16))
    group = lax.broadcasted_iota(jnp.int32, (rows, COLS), 1) % 32
    buffers = -(-len(slots) // 4)
    west, east = [zero] * buffers, [zero] * buffers
    for i, k in enumerate(used):
        own[own_at + k] = strips[i * rows : (i + 1) * rows]
        mine = pair[i * rows : (i + 1) * rows]
        buffer, slot = k // 4, k % 4
        here = (group >= 8 * slot) & (group < 8 * slot + 8)
        west[buffer] = jnp.where(here, roll_lanes(mine, 8 * slot - 8), west[buffer])
        east[buffer] = jnp.where(here, roll_lanes(mine, 8 * slot), east[buffer])
    for buffer in range(buffers):
        to_west[buffer_at + buffer, 0:rows, :] = west[buffer]
        to_east[buffer_at + buffer, 0:rows, :] = east[buffer]


def block_slots(read, extra):
    slots = [[read(field, a) for a in range(4)] for field in range(3)] + [extra]
    return slots + [[read(3 + (a + d) % 4, a) for a in range(4)] for d in range(4)]


def single_slots(read):
    return [[None if q == 3 and a == 3 else read(q, a) for a in range(4)] for q in range(1, 4)]


def own_first_kernel(lam_in, winds_in, inv_in, x_in, own, to_west, to_east, lam, winds, inv, x, sem):
    four = pl.ds(0, 4)
    copy_all(
        [
            (inv_in.at[pl.ds(0, 1)], inv),
            (winds_in.at[:, four], winds),
            (lam_in.at[four], lam),
            (x_in, x),
        ],
        sem,
    )

    def read(field, a):
        return field_ref(lam, winds, inv, field, 0, a)[...]

    slots = block_slots(read, [x[0, f] for f in range(4)])
    slots += single_slots(lambda q, a: x[q, a])
    pack_columns(slots, own, 0, to_west, to_east, 0, ROWS)


def own_rest_kernel(lam, winds, inv, own, to_west, to_east):
    def step(n, carry):
        def read(field, a):
            return field_ref(lam, winds, inv, field, n, a)[...]

        pack_columns(block_slots(read, None), own, 8 * (n - 1), to_west, to_east, 2 * (n - 1), ROWS)
        return carry

    lax.fori_loop(1, BLOCKS, step, 0)


def settle_rows(first_in, second_in, south, north, beyond_fold):
    _, lat, _, is_top = places()
    even = lat % 2 == 0

    @pl.when(even)
    def _():
        south[...] = second_in[...]
        north[...] = first_in[...]

    @pl.when(jnp.logical_not(even))
    def _():
        south[...] = first_in[...]

    @pl.when(jnp.logical_not(even) & jnp.logical_not(is_top))
    def _():
        north[...] = second_in[...]

    pl.when(is_top)(beyond_fold)


def pick(values, at):
    tiles = [
        jnp.take_along_axis(values[8 * t : 8 * t + 8], at, axis=1, mode="promise_in_bounds")
        for t in range(values.shape[0] // 8)
    ]
    return jnp.concatenate(tiles, axis=0)


def halo_first_kernel(
    fold, first_in, second_in, fold_a, fold_b, mid_west, mid_east,
    south, north, h, hx, own, to_west, to_east,
):
    def beyond_fold():
        turn, lane = fold[0] % COLS, lanes()
        source = jnp.where(turn >= lane, turn - lane, turn - lane + COLS)
        keep = lax.broadcasted_iota(jnp.int32, (ROW_BUFFER, COLS), 1) <= turn
        north[...] = jnp.where(keep, pick(fold_a[...], source), pick(fold_b[...], source))

    settle_rows(first_in, second_in, south, north, beyond_fold)
    for field, _, a, at, count in first_pieces():
        h[field, a, 8 - count : 8, :] = south[at : at + count, :]
        h[field, a, 8 : 8 + count, :] = north[at : at + count, :]
    for quad, member, at, count in SINGLES:
        hx[quad, member, 8 - count : 8, :] = south[at : at + count, :]
        hx[quad, member, 8 : 8 + count, :] = north[at : at + count, :]
    slots = block_slots(lambda field, a: h[field, a], [hx[0, f] for f in range(4)])
    slots += single_slots(lambda q, a: hx[q, a])
    pack_columns(slots, own, 0, to_west, to_east, 0, 16)
    to_west[:, 16:EXT, :] = mid_west[...]
    to_east[:, 16:EXT, :] = mid_east[...]


REST = BLOCKS - 1
COL_BUFFER = REST * (EXT + ROWS)


def halo_rest_kernel(south, north, mid_west, mid_east, h, own, to_west, to_east, west, east):
    for field, n, a, at, count in rest_pieces():
        h[n - 1, field, a, 8 - count : 8, :] = south[at : at + count, :]
        h[n - 1, field, a, 8 : 8 + count, :] = north[at : at + count, :]

    def step(n, carry):
        slots = [[h[n, field, a] for a in range(4)] for field in range(3)]
        pack_columns(slots, own, 3 * n, west, east, n, 16)
        return carry

    lax.fori_loop(0, REST, step, 0)
    for out, halo, mid in ((to_west, west, mid_west), (to_east, east, mid_east)):
        for n in range(REST):
            out[EXT * n : EXT * n + 16, :] = halo[n]
            out[EXT * n + 16 : EXT * (n + 1), :] = mid[2 * n]
            at = EXT * REST + ROWS * n
            out[at : at + ROWS, :] = mid[2 * n + 1]


def ext_lanes():
    return lax.broadcasted_iota(jnp.int32, (EXT, COLS), 1)


def barrier_masks():
    comp, _, _, is_top = places()
    row = lax.broadcasted_iota(jnp.int32, (EXT, COLS), 0)
    apart = is_top & (comp == 0)
    keep_c = jnp.where(apart & (row == 40), 0.0, 1.0).astype(F32)
    keep_d = jnp.where(apart & (row == 39), 0.0, 1.0).astype(F32)
    return stack([keep_c] * 5), stack([keep_d] * 5)


def assemble_strip(slot, west, east, mid, halo=None):
    group = lax.broadcasted_iota(jnp.int32, west.shape, 1) % 32
    edge = jnp.where(group < 8, roll_lanes(west, -8 * slot), roll_lanes(east, 24 - 8 * slot))
    inner = (group >= 8) & (group < 24)
    if halo is None:
        return jnp.where(inner, mid, edge)
    return jnp.concatenate(
        [
            jnp.where(inner[0:8], halo[0:8], edge[0:8]),
            jnp.where(inner[0:32], mid, edge[16:48]),
            jnp.where(inner[0:8], halo[8:16], edge[8:16]),
        ],
        axis=0,
    )


class First:
    def __init__(self, lam, winds, inv, h, own, own_halo, from_west, from_east, x_in, hx):
        self.lam, self.winds, self.inv, self.h = lam, winds, inv, h
        self.own, self.own_halo, self.from_west, self.from_east = own, own_halo, from_west, from_east
        self.x_in, self.hx = x_in, hx

    def main(self, field, n, a):
        halo = self.h[field, a]
        mid = field_ref(self.lam, self.winds, self.inv, field, 0, a)[...]
        return jnp.concatenate([halo[0:8], mid, halo[8:16]], axis=0)

    def single(self, quad, a):
        halo = self.hx[quad, a]
        return jnp.concatenate([halo[0:8], self.x_in[quad, a], halo[8:16]], axis=0)

    def strip(self, n, which, slot):
        at = 4 * which + slot
        return assemble_strip(slot, self.from_west[which], self.from_east[which], self.own[at], self.own_halo[at])

    def single_strip(self, quad):
        return self.strip(0, 0, 3) if quad == 0 else self.strip(0, 2, quad - 1)


class Rest:
    def __init__(self, lam, winds, inv, h, own, own_halo, from_west, from_east):
        self.lam, self.winds, self.inv, self.h = lam, winds, inv, h
        self.own, self.own_halo, self.from_west, self.from_east = own, own_halo, from_west, from_east

    def main(self, field, n, a):
        mid = field_ref(self.lam, self.winds, self.inv, field, n, a)[...]
        if field >= 3:
            return mid
        halo = self.h[n - 1, field, a]
        return jnp.concatenate([halo[0:8], mid, halo[8:16]], axis=0)

    def strip(self, n, which, slot):
        mid = self.own[8 * (n - 1) + 4 * which + slot]
        if which == 1:
            rows = pl.ds(pl.multiple_of(EXT * REST + ROWS * (n - 1), 8), ROWS)
            return assemble_strip(slot, self.from_west[rows, :], self.from_east[rows, :], mid)
        rows = pl.ds(pl.multiple_of(EXT * (n - 1), 8), EXT)
        halo = self.own_halo[3 * (n - 1) + slot]
        return assemble_strip(slot, self.from_west[rows, :], self.from_east[rows, :], mid, halo)


def stack(values):
    return jnp.concatenate(values, axis=0)


def unstack(value):
    return [value[EXT * k : EXT * (k + 1)] for k in range(value.shape[0] // EXT)]


def replicate(strip, a):
    lane = ext_lanes()
    out = roll_lanes(strip, -32 * a)
    base = jnp.where(lane < 32, out, 0.0)
    for g in range(1, 4):
        base = jnp.where((lane >= 32 * g) & (lane < 32 * g + 32), roll_lanes(out, 32 * g), base)
    return base


def advect(tracer, coefs, land):
    to_south, to_north, to_west = coefs
    for _ in range(3):
        a = to_west[...] * tracer
        b = (2 * DIFFUSE) * tracer - a
        east, west = roll_lanes(a, -1), roll_lanes(b, 1)
        new = (1.0 - 4 * DIFFUSE) * tracer
        new = new + roll_rows(to_south[...] * tracer, -1) + roll_rows(to_north[...] * tracer, 1)
        tracer = (new + (east + west)) * land[...]
    return tracer


def coefficients(fields, n, masks):
    merid = stack([fields.main(1, n, a) for a in range(4)] + [fields.strip(n, 0, 1)])
    zonal = stack([fields.main(2, n, a) for a in range(4)] + [fields.strip(n, 0, 2)])
    to_south = (DIFFUSE + 0.5 * merid) * masks[0]
    to_north = (DIFFUSE - 0.5 * merid) * masks[1]
    return to_south, to_north, DIFFUSE + 0.5 * zonal


def solve(inverse, strip_inverse, old):
    moved = [old[4]] + [roll_lanes(old[4], -32 * d) for d in range(1, 4)]
    new = []
    for a in range(4):
        total = inverse(a, 0) * old[0]
        for b in range(1, 4):
            total = total + inverse(a, b) * old[b]
        new.append(total)
    total = strip_inverse(0) * moved[0]
    for d in range(1, 4):
        total = total + strip_inverse(d) * moved[d]
    return new + [total]


def solve_first(fields, tracer):
    return solve(lambda a, b: fields.main(3 + b, 0, a), lambda d: fields.strip(0, 1, d), unstack(tracer))


def main_from_strip(main, strip, a, width):
    lane = lax.broadcasted_iota(jnp.int32, main.shape, 1)
    main = jnp.where(lane < width, roll_lanes(strip, -(32 * a + 8)), main)
    return jnp.where(lane >= COLS - width, roll_lanes(strip, 104 - 32 * a), main)


def merge(state):
    strip = state[4]
    lane = lax.broadcasted_iota(jnp.int32, strip.shape, 1)
    new_strip = strip
    mains = [main_from_strip(state[a], strip, a, 3) for a in range(4)]
    for a in range(4):
        west = (lane >= 32 * a + 11) & (lane < 32 * a + 16)
        east = (lane >= 32 * a + 16) & (lane < 32 * a + 21)
        new_strip = jnp.where(west, roll_lanes(state[a], 32 * a + 8), new_strip)
        new_strip = jnp.where(east, roll_lanes(state[a], 32 * a + 24), new_strip)
    return mains + [new_strip]


def load_block(fields, n):
    return [fields.main(0, n, a) for a in range(4)] + [fields.strip(n, 0, 0)]


def fluxes_out(fields, state, payload, strip_coefs):
    surface = state[0] * fields.single(3, 1)
    for f in range(4):
        payload[f] = fields.single(0, f) * surface
    wet_strip = roll_lanes(fields.single_strip(3), -32)
    payload[4] = strip_coefs * replicate(state[4] * wet_strip, 0)


def couple(fields, received, strip_coefs, strip_weights, land_strip):
    sources = [received[f] for f in range(4)] + [roll_lanes(received[4], -32 * f) for f in range(4)]
    coefs = [fields.single(0, f) for f in range(4)] + [strip_coefs[f] for f in range(4)]
    weights = [fields.single(1 + s // 4, s % 4) for s in range(9)]
    moved = {dc: [roll_lanes(source, -dc) for source in sources] for dc in (-1, 0, 1)}
    totals = []
    for table, parts in ((weights, range(4)), ([strip_weights[s] for s in range(9)], range(4, 8))):
        total = None
        for k in parts:
            part = None
            for dr in (-1, 0, 1):
                across = None
                for dc in (-1, 0, 1):
                    term = table[3 * (dr + 1) + dc + 1] * roll_rows(moved[dc][k], -dr)
                    across = term if across is None else across + term
                part = across if part is None else part + across
            total = coefs[k] * part if total is None else total + coefs[k] * part
        totals.append(total)
    return totals[0] * fields.single(3, 2), totals[1] * land_strip


INPUTS = 8


def first_kernel(*refs):
    fields = First(*refs[: INPUTS + 2])
    payload, state, land, to_south, to_north, to_west, strip_coefs, strip_weights = refs[INPUTS + 2 :]
    quads = [fields.single_strip(q) for q in range(4)]
    main_land = fields.single(3, 2)
    land[...] = stack([main_land] * 4 + [replicate(quads[3], 2)])
    coefs = (to_south, to_north, to_west)
    for ref, value in zip(coefs, coefficients(fields, 0, barrier_masks()), strict=True):
        ref[...] = value
    tracer = advect(stack(load_block(fields, 0)), coefs, land)
    merged = merge(solve_first(fields, tracer))
    for a in range(5):
        state[a] = merged[a]
    fluxes_out(fields, merged, payload, quads[0])
    for f in range(4):
        strip_coefs[f] = roll_lanes(quads[0], -32 * f)
    for k in range(9):
        strip_weights[k] = roll_lanes(quads[1 + k // 4], -32 * (k % 4))


def own_rows(tracer):
    return [value[8:40] for value in unstack(tracer)]


def rest_first_kernel(*refs):
    fields = Rest(*refs[:INPUTS])
    land, state, coefs, strip_inverse, first_out, second_out, mirror_out, edges, store, mask_c, mask_d = refs[INPUTS:]
    mask_c[...], mask_d[...] = barrier_masks()

    def block(n, carry):
        mine = tuple(coefs.at[n - 1, k] for k in range(3))
        for ref, value in zip(mine, coefficients(fields, n, (mask_c[...], mask_d[...])), strict=True):
            ref[...] = value
        tracer = advect(stack(load_block(fields, n)), mine, land)
        for d in range(4):
            strip_inverse[n - 1, d] = fields.strip(n, 1, d)
        merged = merge(
            solve(lambda a, b: fields.main(3 + b, n, a), lambda d: strip_inverse[n - 1, d], own_rows(tracer))
        )
        for a in range(5):
            state[n - 1, a] = merged[a]
            edges[0, n - 1, a] = merged[a][24:32]
            edges[1, n - 1, a] = merged[a][0:8]
            edges[2, n - 1, a] = reverse(merged[a][24:32])
        return carry

    lax.fori_loop(1, BLOCKS, block, 0)
    for n in range(REST):
        for a in range(5):
            at = 24 * a + 3 * n
            store[0, at : at + 3, :] = edges[0, n, a, 5:8, :]
            store[1, at : at + 3, :] = edges[1, n, a, 0:3, :]
            store[2, at : at + 3, :] = edges[2, n, a, 0:3, :]
    for k in range(3):
        for a in range(5):
            store[k, 24 * a + 21 : 24 * a + 24, :] = jnp.zeros((3, COLS), F32)
    hand_over(store, first_out, second_out, mirror_out)


def rest_second_kernel(*refs):
    fold, inv, strip_inverse, land, state, coefs, first_in, second_in, fold_a, fold_b, before = refs[:11]
    out, result, south, north, halo, sem = refs[11:]
    del before

    def beyond_fold():
        turn, lane = fold[0] % COLS, lanes()
        source = jnp.where(turn >= lane, turn - lane, turn - lane + COLS)
        keep = lax.broadcasted_iota(jnp.int32, (24, COLS), 1) <= turn
        group, in_group = lane // 32, lane % 32
        column = jnp.where(in_group < 16, in_group - 8, in_group + 104)
        at_a = turn - column
        at_b = at_a + COLS
        main_a, main_b = jnp.clip(at_a, 0, COLS - 1), jnp.clip(at_b, 0, COLS - 1)
        strip_a = 32 * group + jnp.clip(at_a - 104, 0, 31)
        strip_b = 32 * group + jnp.clip(at_b + 8, 0, 31)
        wide_a = stack([at_a] * 3)
        wide_b = stack([at_b] * 3)
        wide_group = stack([group] * 3)
        strip = jnp.where(wide_a >= COLS, pick(fold_a[96:120, :], strip_a), pick(fold_b[96:120, :], strip_b))
        for a in range(4):
            values_a, values_b = fold_a[24 * a : 24 * a + 24, :], fold_b[24 * a : 24 * a + 24, :]
            north[24 * a : 24 * a + 24, :] = jnp.where(keep, pick(values_a, source), pick(values_b, source))
            inside = (wide_group == a) & (wide_a < COLS) & (wide_b >= 0)
            strip = jnp.where(inside, jnp.where(wide_a >= 0, pick(values_a, main_a), pick(values_b, main_b)), strip)
        north[96:120, :] = strip

    settle_rows(first_in, second_in, south, north, beyond_fold)
    for n in range(REST):
        for a in range(5):
            at = 24 * a + 3 * n
            halo[n, a, 5:8, :] = south[at : at + 3, :]
            halo[n, a, 8:11, :] = north[at : at + 3, :]

    def block(n, carry):
        mine = tuple(coefs.at[n - 1, k] for k in range(3))
        parts = []
        for a in range(5):
            edge = halo[n - 1, a]
            parts += [edge[0:8], state[n - 1, a], edge[8:16]]
        tracer = advect(stack(parts), mine, land)
        solved = solve(lambda a, b: inv[n, a, b], lambda d: strip_inverse[n - 1, d], own_rows(tracer))
        for a in range(4):
            result[4 * (n - 1) + a] = main_from_strip(solved[a], solved[4], a, 3)
        return carry

    lax.fori_loop(1, BLOCKS, block, 0)
    copy_all([(result, out.at[pl.ds(4, 4 * REST)])], sem)


def second_kernel(*refs):
    fields = First(None, None, *refs[:INPUTS])
    land, to_south, to_north, to_west, strip_coefs, strip_weights, received, state_in = refs[INPUTS : INPUTS + 8]
    payload, state = refs[INPUTS + 8 :]
    added, added_strip = couple(fields, received, strip_coefs, strip_weights, land[4 * EXT :])
    lane = ext_lanes()
    strip = state_in[4] + jnp.where(lane < 32, added_strip, 0.0)
    top = main_from_strip(state_in[0] + added, strip, 0, 1)
    tracer = stack([top] + [state_in[a] for a in range(1, 4)] + [strip])
    solved = solve_first(fields, advect(tracer, (to_south, to_north, to_west), land))
    merged = [main_from_strip(solved[a], solved[4], a, 3) for a in range(4)] + [solved[4]]
    for a in range(5):
        state[a] = merged[a]
    fluxes_out(fields, merged, payload, fields.single_strip(0))


def last_kernel(x_in, hx, land, strip_coefs, strip_weights, received, state, out, result, sem):
    fields = First(*[None] * 8, x_in, hx)
    added, added_strip = couple(fields, received, strip_coefs, strip_weights, land[4 * EXT :])
    strip = state[4] + added_strip
    result[0] = main_from_strip(state[0] + added, strip, 0, 1)[8:40]
    for a in range(1, 4):
        result[a] = state[a][8:40]
    copy_all([(result, out.at[pl.ds(0, 4)])], sem)


MICROSECONDS = {
    "start_rows_kernel": 3.2,
    "own_first_kernel": 2.0,
    "own_rest_kernel": 2.5,
    "halo_first_kernel": 1.7,
    "halo_rest_kernel": 1.3,
    "first_kernel": 1.0,
    "rest_first_kernel": 4.3,
    "second_kernel": 1.0,
    "last_kernel": 0.5,
    "rest_second_kernel": 4.6,
}


def call(kernel, outs, args, specs, scratch=(), params=PARAMS, **more):
    cost = int(MICROSECONDS[kernel.__name__] * 3.5e6)
    return pl.pallas_call(
        kernel,
        out_shape=[jax.ShapeDtypeStruct(s, jnp.int32 if spec is SMEM else F32) for s, spec in outs],
        in_specs=specs,
        out_specs=[spec for _, spec in outs],
        scratch_shapes=list(scratch),
        compiler_params=params,
        cost_estimate=pl.CostEstimate(flops=0, bytes_accessed=cost, transcendentals=0),
        **more,
    )(*args)


def index(c, a, o):
    return (c * LAT + a) * LON + o % LON


def lon_pairs(do):
    return [(index(c, a, o), index(c, a, o + do)) for c in range(2) for a in range(LAT) for o in range(LON)]


def swap_pairs(start):
    pairs = []
    for c in range(2):
        for a in range(start, LAT - 1, 2):
            for o in range(LON):
                pairs += [(index(c, a, o), index(c, a + 1, o)), (index(c, a + 1, o), index(c, a, o))]
    return pairs


def fold_pairs(total, comps):
    return [(index(c, LAT - 1, o), index(c, LAT - 1, total - o)) for c in comps for o in range(LON)]


def body(
    adjoint_state,
    winds,
    block_inverse,
    flux_coef,
    sea_mask,
    intersection_cell,
    intersection_weight,
    fold_map,
):
    lam = adjoint_state[0]
    wind = winds[:, 0]
    inv = block_inverse[0]
    rows = (ROW_BUFFER, COLS)
    x, first, second, mirror, turn = call(
        start_rows_kernel,
        [((4, 4, ROWS, COLS), VMEM)] + [(rows, VMEM)] * 3 + [((1,), SMEM)],
        (fold_map, lam, wind, inv, flux_coef[0], sea_mask, intersection_cell, intersection_weight),
        [SMEM] + [HBM] * 7,
        [
            pltpu.VMEM((3, *rows), F32),
            pltpu.VMEM((32, 16, COLS), F32),
            pltpu.VMEM((2, 32, 16, COLS), F32),
            pltpu.VMEM((1, 4, 4, 16, COLS), F32),
            pltpu.VMEM((4, ROWS, COLS), F32),
            pltpu.VMEM((ROWS, COLS), jnp.int32),
            pltpu.VMEM((2, 4, ROWS, COLS), jnp.int32),
            pltpu.VMEM((4, ROWS, COLS), F32),
            pltpu.SemaphoreType.DMA((10,)),
        ],
        FULL,
    )
    def swap(first, second):
        return lax.ppermute(first, AXES, swap_pairs(0)), lax.ppermute(second, AXES, swap_pairs(1))

    def around(to_west, to_east):
        return lax.ppermute(to_east, AXES, lon_pairs(1)), lax.ppermute(to_west, AXES, lon_pairs(-1))

    def across(value):
        return lax.ppermute(value, AXES, [(i, (i + LAT * LON) % (2 * LAT * LON)) for i in range(2 * LAT * LON)])

    def vmem(*shape):
        return ((*shape, COLS), VMEM)

    state_in = (lam, wind, inv)
    swapped = swap(first, second)

    def across_fold(total, mirror, lam, wind, inv, x):
        folded = [lax.ppermute(mirror, AXES, fold_pairs(total - k, (0, 1))) for k in range(2)]
        own = call(
            own_first_kernel,
            [vmem(12, ROWS), vmem(3, ROWS), vmem(3, ROWS)],
            (lam, wind, inv, x),
            [HBM] * 4,
            [
                pltpu.VMEM((4, ROWS, COLS), F32),
                pltpu.VMEM((2, 4, ROWS, COLS), F32),
                pltpu.VMEM((1, 4, 4, ROWS, COLS), F32),
                pltpu.VMEM((4, 4, ROWS, COLS), F32),
                pltpu.SemaphoreType.DMA((4,)),
            ],
        )
        rest_own = call(
            own_rest_kernel,
            [vmem(8 * REST, ROWS), vmem(2 * REST, ROWS), vmem(2 * REST, ROWS)],
            (lam, wind, inv),
            [VMEM] * 3,
        )
        return *folded, *own, *rest_own

    *folded, own, mid_west, mid_east, rest_own, rest_mid_west, rest_mid_east = lax.switch(
        turn[0], [functools.partial(across_fold, total) for total in range(LON)], mirror, lam, wind, inv, x
    )
    moved = (*swapped, *folded)
    south, north, h, hx, own_halo, to_west, to_east = call(
        halo_first_kernel,
        [vmem(ROW_BUFFER)] * 2 + [vmem(7, 4, 16), vmem(4, 4, 16), vmem(12, 16), vmem(3, EXT), vmem(3, EXT)],
        (fold_map, *moved, mid_west, mid_east),
        [SMEM] + [VMEM] * 6,
    )
    rest_h, rest_own_halo, rest_to_west, rest_to_east = call(
        halo_rest_kernel,
        [vmem(REST, 3, 4, 16), vmem(3 * REST, 16), vmem(COL_BUFFER), vmem(COL_BUFFER)],
        (south, north, rest_mid_west, rest_mid_east),
        [VMEM] * 4,
        [pltpu.VMEM((REST, 16, COLS), F32)] * 2,
    )
    h, rest_to_west, rest_to_east = lax.optimization_barrier((h, rest_to_west, rest_to_east))
    args = (inv, h, own, own_halo, *around(to_west, to_east), x, hx)
    five = vmem(5, EXT)
    tall = vmem(5 * EXT)
    payload, state, land, *tables = call(
        first_kernel,
        [five, five] + [tall] * 4 + [vmem(4, EXT), vmem(9, EXT)],
        (lam, wind, *args),
        [VMEM] * (INPUTS + 2),
    )
    received = across(payload)
    rest_args = (*state_in, rest_h, rest_own, rest_own_halo, *around(rest_to_west, rest_to_east))
    whole = ((32, ROWS, COLS), HBM)
    done = pltpu.SemaphoreType.DMA((1,))
    rest_state, rest_coefs, strip_inverse, *rest_rows = call(
        rest_first_kernel,
        [vmem(REST, 5, ROWS), vmem(REST, 3, 5 * EXT), vmem(REST, 4, ROWS)] + [vmem(120)] * 3,
        (*rest_args, land),
        [VMEM] * (INPUTS + 1),
        [pltpu.VMEM((3, REST, 5, 8, COLS), F32), pltpu.VMEM((3, 120, COLS), F32)]
        + [pltpu.VMEM((5 * EXT, COLS), F32)] * 2,
    )
    rest_swapped = swap(*rest_rows[:2])
    received, rest_mirror = lax.optimization_barrier((received, rest_rows[2]))
    payload, state = call(
        second_kernel, [five, five], (*args, land, *tables, received, state), [VMEM] * (INPUTS + 8)
    )

    def finish(total, mirror, payload, last_args, rest_args, swapped):
        folded = [lax.ppermute(mirror, AXES, fold_pairs(total - k, (1,))) for k in range(2)]
        x, hx, land, strip_coefs, strip_weights, state = last_args
        (out,) = call(
            last_kernel,
            [whole],
            (x, hx, land, strip_coefs, strip_weights, across(payload), state),
            [VMEM] * 7,
            [pltpu.VMEM((4, ROWS, COLS), F32), done],
        )
        return call(
            rest_second_kernel,
            [whole],
            (*rest_args, *swapped, *folded, out),
            [SMEM] + [VMEM] * 9 + [HBM],
            [
                pltpu.VMEM((4 * REST, ROWS, COLS), F32),
                pltpu.VMEM((120, COLS), F32),
                pltpu.VMEM((120, COLS), F32),
                pltpu.VMEM((REST, 5, 16, COLS), F32),
                done,
            ],
            input_output_aliases={10: 0},
        )[0]

    out = lax.switch(
        turn[0],
        [functools.partial(finish, total) for total in range(LON)],
        rest_mirror,
        payload,
        (x, hx, land, *tables[3:], state),
        (fold_map, inv, strip_inverse, land, rest_state, rest_coefs),
        rest_swapped,
    )
    return out[None]


def solution(mesh):
    return jax.shard_map(
        body,
        mesh=mesh,
        in_specs=(
            P("comp", None, "lat", "lon"),
            P(None, "comp", None, "lat", "lon"),
            P("comp", None, None, None, "lat", "lon"),
            P("comp", None, "lat", "lon"),
            P("lat", "lon"),
            P(None, None, "lat", "lon"),
            P(None, "lat", "lon"),
            P(),
        ),
        out_specs=P("comp", None, "lat", "lon"),
        check_vma=False,
    )
```

profile of v0, /device:TPU:16, one launch (start us, length us, event | category | flops | bytes accessed | tf_op | source)
XLA Modules:
  0.0 60.7 jit_solution(9423691392798790748)
XLA Ops:
  0.0 3.3 %shard_map.90 = (f32[4,4,32,128]{3,2,1,0:T(8,128)S(1)}, f32[464,128]{1,0:T(8,128)}, f32[464,128]{1,0:T(8,128)}, f32[464,128]{1,0:T(8,128)}, s32[1]{0:T(128)}) custom-call(s32[1024]{0:T(1024)} %fold.3, f32[32,32,128]{2,1,0:T(8,128)} %bitcast.44, f32[2,32,32,128]{3,2,1,0:T(8,128)} %bitcast.33, f32[8,4,4,32,128]{4,3,2,1,0:T(8,128)} %bitcast.13, ...), custom_call_target="tpu_custom_call" | custom-call | bytes 11200000 | tf_op jit(solution)/shard_map/pallas_call | solution.py:646
  3.4 2.0 %collective-permute-start.40 = (f32[464,128]{1,0:T(8,128)}, f32[464,128]{1,0:T(8,128)S(1)}, u32[]{:S(2)}, u32[]{:S(2)}) collective-permute-start(f32[464,128]{1,0:T(8,128)} %get-tuple-element.589), channel_id=1, source_target_pairs={{0,8},{8,0},{1,9},{9,1},{2,10},{10,2},{3,11},{11,3},{4,12},{12,4},... | collective-permute-start | bytes 712712 | tf_op jit(solution)/shard_map/ppermute | solution.py:712
  5.4 4.2 %collective-permute-start.41 = (f32[464,128]{1,0:T(8,128)}, f32[464,128]{1,0:T(8,128)S(1)}, u32[]{:S(2)}, u32[]{:S(2)}) collective-permute-start(f32[464,128]{1,0:T(8,128)} %get-tuple-element.590), channel_id=1, source_target_pairs={{8,16},{16,8},{9,17},{17,9},{10,18},{18,10},{11,19},{19,11},{12,20... | collective-permute-start | bytes 712712 | tf_op jit(solution)/shard_map/ppermute | solution.py:712
  10.2 0.0 copy-start.19
  10.2 8.2 %conditional.2 = (f32[464,128]{1,0:T(8,128)}, f32[464,128]{1,0:T(8,128)}, f32[12,32,128]{2,1,0:T(8,128)S(1)}, f32[3,32,128]{2,1,0:T(8,128)S(1)}, f32[3,32,128]{2...) conditional(s32[]{:T(128)} %bitcast.12, ...), branch_computations={%region_0.0_spmd, %region_1.0_spmd, %region_2.0_spmd, %region_3.0_... | conditional | bytes 30233656 | solution.py:749
  10.3 0.0 copy-start.1
  10.3 0.0 copy-start.10
  10.3 1.5 %collective-permute-start.1 = (f32[464,128]{1,0:T(8,128)}, f32[464,128]{1,0:T(8,128)}, u32[]{:S(2)}, u32[]{:S(2)}) collective-permute-start(f32[464,128]{1,0:T(8,128)} %get-tuple-element.273), channel_id=1, source_target_pairs={{56,63},{57,62},{58,61},{59,60},{60,59},{61,58},{62,57},{63,56},{1... | collective-permute-start | bytes 712712 | tf_op jit(solution)/shard_map/cond/branch_0_fun/ppermute | solution.py:727
  11.8 1.3 %collective-permute-start = (f32[464,128]{1,0:T(8,128)}, f32[464,128]{1,0:T(8,128)}, u32[]{:S(2)}, u32[]{:S(2)}) collective-permute-start(f32[464,128]{1,0:T(8,128)} %get-tuple-element.273), channel_id=1, source_target_pairs={{56,56},{57,63},{58,62},{59,61},{60,60},{61,59},{62,58},{63,57},{1... | collective-permute-start | bytes 712712 | tf_op jit(solution)/shard_map/cond/branch_0_fun/ppermute | solution.py:727
  13.1 4.7 %branch_0_fun.5 = (f32[56,32,128]{2,1,0:T(8,128)S(1)}, f32[14,32,128]{2,1,0:T(8,128)}, f32[14,32,128]{2,1,0:T(8,128)}) custom-call(f32[32,32,128]{2,1,0:T(8,128)S(1)} %get-tuple-element.274.lam_in.lam, f32[2,32,32,128]{3,2,1,0:T(8,128)} %get-tuple-element.304.winds_in.winds, f32[8,4,4,32,128]{4,3,2,1,0:T(8,128)} %get-tuple-element.336.inv_in.inv), custom_call_target="tpu_custom_call" | custom-call | bytes 8750000 | tf_op jit(solution)/shard_map/cond/branch_0_fun/pallas_call | solution.py:646
  17.8 0.6 %branch_0_fun.4 = (f32[12,32,128]{2,1,0:T(8,128)S(1)}, f32[3,32,128]{2,1,0:T(8,128)S(1)}, f32[3,32,128]{2,1,0:T(8,128)S(1)}) custom-call(f32[32,32,128]{2,1,0:T(8,128)S(1)} %get-tuple-element.274.lam_in.lam, f32[2,32,32,128]{3,2,1,0:T(8,128)S(1)} %copy-done.10, f32[8,4,4,32,128]{4,3,2,1,0:T(8,128)S(1)} %copy-done.1, ...), custom_call_target="tpu_custom_call" | custom-call | bytes 7000000 | tf_op jit(solution)/shard_map/cond/branch_0_fun/pallas_call | solution.py:646
  18.5 0.0 copy-start.9
  18.5 1.5 %shard_map.91 = (f32[464,128]{1,0:T(8,128)S(1)}, f32[464,128]{1,0:T(8,128)S(1)}, f32[7,4,16,128]{3,2,1,0:T(8,128)S(1)}, f32[4,4,16,128]{3,2,1,0:T(8,128)S(1)}, f...) custom-call(s32[1024]{0:T(1024)S(1)} %copy-done.19, ...), custom_call_target="tpu_custom_call" | custom-call | bytes 5950000 | tf_op jit(solution)/shard_map/pallas_call | solution.py:646
  20.0 2.3 %shard_map.92 = (f32[7,3,4,16,128]{4,3,2,1,0:T(8,128)S(1)}, f32[21,16,128]{2,1,0:T(8,128)S(1)}, f32[560,128]{1,0:T(8,128)S(1)}, f32[560,128]{1,0:T(8,128)S(1)}) custom-call(f32[464,128]{1,0:T(8,128)S(1)} %get-tuple-element.598.south, f32[464,128]{1,0:T(8,128)S(1)} %get-tuple-element.599.north, f32[14,32,128]{2,1,0:T(8,128)} %get-tuple-element.600.mid_west, ...), custom_call_target="tpu_custom_call" | custom-call | bytes 4550000 | tf_op jit(solution)/shard_map/pallas_call | solution.py:646
  22.3 0.0 collective-permute-start.45
  22.4 2.9 %collective-permute-start.46 = (f32[560,128]{1,0:T(8,128)S(1)}, f32[560,128]{1,0:T(8,128)S(1)}, u32[]{:S(2)}, u32[]{:S(2)}) collective-permute-start(f32[560,128]{1,0:T(8,128)S(1)} %get-tuple-element.615), channel_id=1, source_target_pairs={{0,7},{1,0},{2,1},{3,2},{4,3},{5,4},{6,5},{7,6},{8,15},{9,8},{10,9... | collective-permute-start | bytes 860168 | tf_op jit(solution)/shard_map/ppermute | solution.py:715
  25.3 3.0 %collective-permute-start.43 = (f32[3,48,128]{2,1,0:T(8,128)S(1)}, f32[3,48,128]{2,1,0:T(8,128)S(1)}, u32[]{:S(2)}, u32[]{:S(2)}) collective-permute-start(f32[3,48,128]{2,1,0:T(8,128)S(1)} %get-tuple-element.608), channel_id=1, source_target_pairs={{0,7},{1,0},{2,1},{3,2},{4,3},{5,4},{6,5},{7,6},{8,15},{9,8},{10,9... | collective-permute-start | bytes 221192 | tf_op jit(solution)/shard_map/ppermute | solution.py:715
  28.3 2.1 %collective-permute-done.42.refs_6_.refs_4_ = f32[3,48,128]{2,1,0:T(8,128)S(1)} collective-permute-done((f32[3,48,128]{2,1,0:T(8,128)S(1)}, f32[3,48,128]{2,1,0:T(8,128)S(1)}, u32[]{:S(2)}, u32[]{:S(2)}) %collective-permute-start.42) | collective-permute-done | bytes 73760 | tf_op jit(solution)/shard_map/ppermute | solution.py:715
  30.4 2.5 %shard_map.93 = (f32[5,48,128]{2,1,0:T(8,128)S(1)}, f32[5,48,128]{2,1,0:T(8,128)S(1)}, f32[240,128]{1,0:T(8,128)S(1)}, f32[240,128]{1,0:T(8,128)S(1)}, f32[240,1...) custom-call(f32[32,32,128]{2,1,0:T(8,128)S(1)} %bitcast.53, ...), custom_call_target="tpu_custom_call" | custom-call | bytes 3500000 | tf_op jit(solution)/shard_map/pallas_call | solution.py:646
  33.0 2.3 %collective-permute-start.44 = (f32[5,48,128]{2,1,0:T(8,128)S(1)}, f32[5,48,128]{2,1,0:T(8,128)S(1)}, u32[]{:S(2)}, u32[]{:S(2)}) collective-permute-start(f32[5,48,128]{2,1,0:T(8,128)S(1)} %get-tuple-element.610), channel_id=1, source_target_pairs={{0,64},{1,65},{2,66},{3,67},{4,68},{5,69},{6,70},{7,71},{8,72},{9,... | collective-permute-start | bytes 368648 | tf_op jit(solution)/shard_map/ppermute | solution.py:718
  35.3 4.3 %shard_map.94 = (f32[7,5,32,128]{3,2,1,0:T(8,128)S(1)}, f32[7,3,240,128]{3,2,1,0:T(8,128)S(1)}, f32[7,4,32,128]{3,2,1,0:T(8,128)S(1)}, f32[120,128]{1,0:T(8,128)...) custom-call(f32[32,32,128]{2,1,0:T(8,128)S(1)} %bitcast.54, f32[2,32,32,128]{3,2,1,0:T(8,128)S(1)} %bitcast.43, ...), custom_call_target="tpu_custom_call" | custom-call | bytes 15050000 | tf_op jit(solution)/shard_map/pallas_call | solution.py:646
  39.5 0.4 collective-permute-start.47
  40.0 3.4 %collective-permute-start.48 = (f32[120,128]{1,0:T(8,128)S(1)}, f32[120,128]{1,0:T(8,128)S(1)}, u32[]{:S(2)}, u32[]{:S(2)}) collective-permute-start(f32[120,128]{1,0:T(8,128)S(1)} %get-tuple-element.632), channel_id=1, source_target_pairs={{8,16},{16,8},{9,17},{17,9},{10,18},{18,10},{11,19},{19,11},{12,20... | collective-permute-start | bytes 184328 | tf_op jit(solution)/shard_map/ppermute | solution.py:712
  43.4 0.9 %shard_map.95 = (f32[5,48,128]{2,1,0:T(8,128)S(1)}, f32[5,48,128]{2,1,0:T(8,128)S(1)}) custom-call(f32[8,4,4,32,128]{4,3,2,1,0:T(8,128)S(1)} %bitcast.24, f32[7,4,16,128]{3,2,1,0:T(8,128)S(1)} %get-tuple-element.604.refs_3_.refs_1_, f32[12,32,128]{2,1,0:T(8,128)S(1)} %get-tuple-element.605.refs_4_.refs_2_, ...), custom_call_target="tpu_custom_call" | custom-call | bytes 3500000 | tf_op jit(solution)/shard_map/pallas_call | solution.py:646
  44.4 5.3 %collective-permute-done.48 = f32[120,128]{1,0:T(8,128)S(1)} collective-permute-done((f32[120,128]{1,0:T(8,128)S(1)}, f32[120,128]{1,0:T(8,128)S(1)}, u32[]{:S(2)}, u32[]{:S(2)}) %collective-permute-start.48) | collective-permute-done | bytes 61472 | tf_op jit(solution)/shard_map/ppermute | solution.py:712
  49.7 10.9 %conditional.3 = (f32[1,32,32,128]{3,2,1,0:T(8,128)}) conditional(s32[]{:T(128)} %bitcast.12, (f32[120,128]{1,0:T(8,128)S(1)}, f32[5,48,128]{2,1,0:T(8,128)S(1)}, f32[4,4,32,128]{3,2,1,0:T(8,128)S(1)}, f32[4,4,16,128]{3,2,1,0:T(8,128)S(1)}, f32[240,128]{1,0:T(8,128)S(1)}, /*index=5*/f32[4,48,128]{2,1,0:T(8,128)S(1)}, ...), branch_computations={%region_8.0_spmd, %region_9.0_spmd, %region_10.0_spmd, %region_11.... | conditional | bytes 18833168 | solution.py:819
  49.7 0.7 %collective-permute-start.18 = (f32[5,48,128]{2,1,0:T(8,128)S(1)}, f32[5,48,128]{2,1,0:T(8,128)S(1)}, u32[]{:S(2)}, u32[]{:S(2)}) collective-permute-start(f32[5,48,128]{2,1,0:T(8,128)S(1)} %get-tuple-element.436), channel_id=1, source_target_pairs={{0,64},{1,65},{2,66},{3,67},{4,68},{5,69},{6,70},{7,71},{8,72},{9,... | collective-permute-start | bytes 368648 | tf_op jit(solution)/shard_map/cond/branch_0_fun/ppermute | solution.py:718
  50.4 0.7 %collective-permute-start.17 = (f32[120,128]{1,0:T(8,128)S(1)}, f32[120,128]{1,0:T(8,128)S(1)}, u32[]{:S(2)}, u32[]{:S(2)}) collective-permute-start(f32[120,128]{1,0:T(8,128)S(1)} %get-tuple-element.431), channel_id=1, source_target_pairs={{120,127},{121,126},{122,125},{123,124},{124,123},{125,122},{126,1... | collective-permute-start | bytes 184328 | tf_op jit(solution)/shard_map/cond/branch_0_fun/ppermute | solution.py:795
  51.1 0.7 %collective-permute-start.16 = (f32[120,128]{1,0:T(8,128)S(1)}, f32[120,128]{1,0:T(8,128)S(1)}, u32[]{:S(2)}, u32[]{:S(2)}) collective-permute-start(f32[120,128]{1,0:T(8,128)S(1)} %get-tuple-element.431), channel_id=1, source_target_pairs={{120,120},{121,127},{122,126},{123,125},{124,124},{125,123},{126,1... | collective-permute-start | bytes 184328 | tf_op jit(solution)/shard_map/cond/branch_0_fun/ppermute | solution.py:795
  51.8 2.8 %collective-permute-done.18.received = f32[5,48,128]{2,1,0:T(8,128)S(1)} collective-permute-done((f32[5,48,128]{2,1,0:T(8,128)S(1)}, f32[5,48,128]{2,1,0:T(8,128)S(1)}, u32[]{:S(2)}, u32[]{:S(2)}) %collective-permute-start.18) | collective-permute-done | bytes 122912 | tf_op jit(solution)/shard_map/cond/branch_0_fun/ppermute | solution.py:718
  54.6 0.9 %branch_0_fun.6.refs_10_ = f32[32,32,128]{2,1,0:T(8,128)} custom-call(f32[4,4,32,128]{3,2,1,0:T(8,128)S(1)} %get-tuple-element.432.x_in, f32[4,4,16,128]{3,2,1,0:T(8,128)S(1)} %get-tuple-element.433.hx, f32[240,128]{1,0:T(8,128)S(1)} %get-tuple-element.426.land.refs_3_, f32[4,48,128]{2,1,0:T(8,128)S(1)} %get-tuple-element.434.strip_coefs, ...), custom_call_target="tpu_custom_call" | custom-call | bytes 1750000 | tf_op jit(solution)/shard_map/cond/branch_0_fun/pallas_call | solution.py:646
  55.5 4.9 %branch_0_fun.7 = f32[32,32,128]{2,1,0:T(8,128)} custom-call(s32[1024]{0:T(1024)S(1)} %get-tuple-element.423.refs_0_, f32[8,4,4,32,128]{4,3,2,1,0:T(8,128)S(1)} %get-tuple-element.424.refs_1_, f32[7,4,32,128]{3,2,1,0:T(8,128)S(1)} %get-tuple-element.425.refs_2_, f32[240,128]{1,0:T(8,128)S(1)} %get-tuple-element.426.land.refs_3_, ...), custom_call_target="tpu_custom_call", output_to_operand_aliasing={{}: (10, {})} | custom-call | bytes 16099999 | tf_op jit(solution)/shard_map/cond/branch_0_fun/pallas_call | solution.py:646
  (20 shorter events, 0.0 us)
Async XLA Ops:
  0.0 10.2 %copy-start.18 = (f32[1,32,32,128]{3,2,1,0:T(8,128)S(1)}, f32[1,32,32,128]{3,2,1,0:T(8,128)}, u32[]{:S(2)}) copy-start(f32[1,32,32,128]{3,2,1,0:T(8,128)} %param.24) | copy-start | bytes 1572868
  3.4 15.1 %collective-permute-start.40 = (f32[464,128]{1,0:T(8,128)}, f32[464,128]{1,0:T(8,128)S(1)}, u32[]{:S(2)}, u32[]{:S(2)}) collective-permute-start(f32[464,128]{1,0:T(8,128)} %get-tuple-element.589), channel_id=1, source_target_pairs={{0,8},{8,0},{1,9},{9,1},{2,10},{10,2},{3,11},{11,3},{4,12},{12,4},... | collective-permute-start | bytes 712712 | tf_op jit(solution)/shard_map/ppermute | solution.py:712
  5.4 13.2 %collective-permute-start.41 = (f32[464,128]{1,0:T(8,128)}, f32[464,128]{1,0:T(8,128)S(1)}, u32[]{:S(2)}, u32[]{:S(2)}) collective-permute-start(f32[464,128]{1,0:T(8,128)} %get-tuple-element.590), channel_id=1, source_target_pairs={{8,16},{16,8},{9,17},{17,9},{10,18},{18,10},{11,19},{19,11},{12,20... | collective-permute-start | bytes 712712 | tf_op jit(solution)/shard_map/ppermute | solution.py:712
  10.2 8.3 %copy-start.19 = (s32[1024]{0:T(1024)S(1)}, s32[1024]{0:T(1024)}, u32[]{:S(2)}) copy-start(s32[1024]{0:T(1024)} %fold.3) | copy-start | bytes 12292
  10.3 7.5 %copy-start.1 = (f32[8,4,4,32,128]{4,3,2,1,0:T(8,128)S(1)}, f32[8,4,4,32,128]{4,3,2,1,0:T(8,128)}, u32[]{:S(2)}) copy-start(f32[8,4,4,32,128]{4,3,2,1,0:T(8,128)} %get-tuple-element.336.inv_in.inv) | copy-start | bytes 6291460 | tf_op jit(solution)/shard_map/cond
  10.3 7.5 %copy-start.10 = (f32[2,32,32,128]{3,2,1,0:T(8,128)S(1)}, f32[2,32,32,128]{3,2,1,0:T(8,128)}, u32[]{:S(2)}) copy-start(f32[2,32,32,128]{3,2,1,0:T(8,128)} %get-tuple-element.304.winds_in.winds) | copy-start | bytes 3145732 | tf_op jit(solution)/shard_map/cond
  10.3 8.1 %collective-permute-start.1 = (f32[464,128]{1,0:T(8,128)}, f32[464,128]{1,0:T(8,128)}, u32[]{:S(2)}, u32[]{:S(2)}) collective-permute-start(f32[464,128]{1,0:T(8,128)} %get-tuple-element.273), channel_id=1, source_target_pairs={{56,63},{57,62},{58,61},{59,60},{60,59},{61,58},{62,57},{63,56},{1... | collective-permute-start | bytes 712712 | tf_op jit(solution)/shard_map/cond/branch_0_fun/ppermute | solution.py:727
  11.8 6.7 %collective-permute-start = (f32[464,128]{1,0:T(8,128)}, f32[464,128]{1,0:T(8,128)}, u32[]{:S(2)}, u32[]{:S(2)}) collective-permute-start(f32[464,128]{1,0:T(8,128)} %get-tuple-element.273), channel_id=1, source_target_pairs={{56,56},{57,63},{58,62},{59,61},{60,60},{61,59},{62,58},{63,57},{1... | collective-permute-start | bytes 712712 | tf_op jit(solution)/shard_map/cond/branch_0_fun/ppermute | solution.py:727
  18.5 11.9 %copy-start.9 = (f32[2,1,32,32,128]{4,3,2,1,0:T(8,128)S(1)}, f32[2,1,32,32,128]{4,3,2,1,0:T(8,128)}, u32[]{:S(2)}) copy-start(f32[2,1,32,32,128]{4,3,2,1,0:T(8,128)} %param.25) | copy-start | bytes 3145732
  22.3 12.9 %copy-start = (f32[1,8,4,4,32,128]{5,4,3,2,1,0:T(8,128)S(1)}, f32[1,8,4,4,32,128]{5,4,3,2,1,0:T(8,128)}, u32[]{:S(2)}) copy-start(f32[1,8,4,4,32,128]{5,4,3,2,1,0:T(8,128)} %param.26) | copy-start | bytes 6291460
  22.3 12.9 %collective-permute-start.45 = (f32[560,128]{1,0:T(8,128)S(1)}, f32[560,128]{1,0:T(8,128)S(1)}, u32[]{:S(2)}, u32[]{:S(2)}) collective-permute-start(f32[560,128]{1,0:T(8,128)S(1)} %get-tuple-element.614), channel_id=1, source_target_pairs={{0,1},{1,2},{2,3},{3,4},{4,5},{5,6},{6,7},{7,0},{8,9},{9,10},{10,1... | collective-permute-start | bytes 860168 | tf_op jit(solution)/shard_map/ppermute | solution.py:715
  22.4 12.9 %collective-permute-start.46 = (f32[560,128]{1,0:T(8,128)S(1)}, f32[560,128]{1,0:T(8,128)S(1)}, u32[]{:S(2)}, u32[]{:S(2)}) collective-permute-start(f32[560,128]{1,0:T(8,128)S(1)} %get-tuple-element.615), channel_id=1, source_target_pairs={{0,7},{1,0},{2,1},{3,2},{4,3},{5,4},{6,5},{7,6},{8,15},{9,8},{10,9... | collective-permute-start | bytes 860168 | tf_op jit(solution)/shard_map/ppermute | solution.py:715
  25.3 5.1 %collective-permute-start.42 = (f32[3,48,128]{2,1,0:T(8,128)S(1)}, f32[3,48,128]{2,1,0:T(8,128)S(1)}, u32[]{:S(2)}, u32[]{:S(2)}) collective-permute-start(f32[3,48,128]{2,1,0:T(8,128)S(1)} %get-tuple-element.607), channel_id=1, source_target_pairs={{0,1},{1,2},{2,3},{3,4},{4,5},{5,6},{6,7},{7,0},{8,9},{9,10},{10,1... | collective-permute-start | bytes 221192 | tf_op jit(solution)/shard_map/ppermute | solution.py:715
  25.3 5.1 %collective-permute-start.43 = (f32[3,48,128]{2,1,0:T(8,128)S(1)}, f32[3,48,128]{2,1,0:T(8,128)S(1)}, u32[]{:S(2)}, u32[]{:S(2)}) collective-permute-start(f32[3,48,128]{2,1,0:T(8,128)S(1)} %get-tuple-element.608), channel_id=1, source_target_pairs={{0,7},{1,0},{2,1},{3,2},{4,3},{5,4},{6,5},{7,6},{8,15},{9,8},{10,9... | collective-permute-start | bytes 221192 | tf_op jit(solution)/shard_map/ppermute | solution.py:715
  33.0 10.4 %collective-permute-start.44 = (f32[5,48,128]{2,1,0:T(8,128)S(1)}, f32[5,48,128]{2,1,0:T(8,128)S(1)}, u32[]{:S(2)}, u32[]{:S(2)}) collective-permute-start(f32[5,48,128]{2,1,0:T(8,128)S(1)} %get-tuple-element.610), channel_id=1, source_target_pairs={{0,64},{1,65},{2,66},{3,67},{4,68},{5,69},{6,70},{7,71},{8,72},{9,... | collective-permute-start | bytes 368648 | tf_op jit(solution)/shard_map/ppermute | solution.py:718
  39.5 4.8 %collective-permute-start.47 = (f32[120,128]{1,0:T(8,128)S(1)}, f32[120,128]{1,0:T(8,128)S(1)}, u32[]{:S(2)}, u32[]{:S(2)}) collective-permute-start(f32[120,128]{1,0:T(8,128)S(1)} %get-tuple-element.631), channel_id=1, source_target_pairs={{0,8},{8,0},{1,9},{9,1},{2,10},{10,2},{3,11},{11,3},{4,12},{12,4},... | collective-permute-start | bytes 184328 | tf_op jit(solution)/shard_map/ppermute | solution.py:712
  40.0 9.7 %collective-permute-start.48 = (f32[120,128]{1,0:T(8,128)S(1)}, f32[120,128]{1,0:T(8,128)S(1)}, u32[]{:S(2)}, u32[]{:S(2)}) collective-permute-start(f32[120,128]{1,0:T(8,128)S(1)} %get-tuple-element.632), channel_id=1, source_target_pairs={{8,16},{16,8},{9,17},{17,9},{10,18},{18,10},{11,19},{19,11},{12,20... | collective-permute-start | bytes 184328 | tf_op jit(solution)/shard_map/ppermute | solution.py:712
  49.7 4.9 %collective-permute-start.18 = (f32[5,48,128]{2,1,0:T(8,128)S(1)}, f32[5,48,128]{2,1,0:T(8,128)S(1)}, u32[]{:S(2)}, u32[]{:S(2)}) collective-permute-start(f32[5,48,128]{2,1,0:T(8,128)S(1)} %get-tuple-element.436), channel_id=1, source_target_pairs={{0,64},{1,65},{2,66},{3,67},{4,68},{5,69},{6,70},{7,71},{8,72},{9,... | collective-permute-start | bytes 368648 | tf_op jit(solution)/shard_map/cond/branch_0_fun/ppermute | solution.py:718
  50.4 5.1 %collective-permute-start.17 = (f32[120,128]{1,0:T(8,128)S(1)}, f32[120,128]{1,0:T(8,128)S(1)}, u32[]{:S(2)}, u32[]{:S(2)}) collective-permute-start(f32[120,128]{1,0:T(8,128)S(1)} %get-tuple-element.431), channel_id=1, source_target_pairs={{120,127},{121,126},{122,125},{123,124},{124,123},{125,122},{126,1... | collective-permute-start | bytes 184328 | tf_op jit(solution)/shard_map/cond/branch_0_fun/ppermute | solution.py:795
  51.1 4.4 %collective-permute-start.16 = (f32[120,128]{1,0:T(8,128)S(1)}, f32[120,128]{1,0:T(8,128)S(1)}, u32[]{:S(2)}, u32[]{:S(2)}) collective-permute-start(f32[120,128]{1,0:T(8,128)S(1)} %get-tuple-element.431), channel_id=1, source_target_pairs={{120,120},{121,127},{122,126},{123,125},{124,124},{125,123},{126,1... | collective-permute-start | bytes 184328 | tf_op jit(solution)/shard_map/cond/branch_0_fun/ppermute | solution.py:795
where the time goes:
time: 61.2 us; the launch traced here: 60.7 us
  Pallas kernels  25.9 us (42%)
  starting transfers between devices  23.1 us (38%)
  waiting for transfers between devices  10.3 us (17%)
  between operations  0.99 us (2%)
    pallas_call x10, Pallas kernels, call(): pl.pallas_call(kernel, out_shape=[jax.ShapeDtypeStruct(s, jnp.int32 if sp...  25.9 us
    ppermute x2, starting transfers between devices, swap(): lax.ppermute(second, AXES, swap_pairs(1))  7.61 us
    ppermute x2, starting transfers between devices, around(): lax.ppermute(to_west, AXES, lon_pairs(-1))  5.9 us
    ppermute x2, waiting for transfers between devices, swap(): lax.ppermute(second, AXES, swap_pairs(1))  5.32 us
    ppermute x2, starting transfers between devices, across(): lax.ppermute(value, AXES, [(i, (i + LAT * LON) % (2 * LAT * LON)) for i i...  3.03 us
    ppermute x2, starting transfers between devices, across_fold(): lax.ppermute(mirror, AXES, fold_pairs(total - k, (0, 1)))  2.84 us
    ppermute x2, waiting for transfers between devices, across(): lax.ppermute(value, AXES, [(i, (i + LAT * LON) % (2 * LAT * LON)) for i i...  2.81 us
    ppermute x2, starting transfers between devices, swap(): lax.ppermute(first, AXES, swap_pairs(0))  2.42 us
  transfers between devices with their start and end apart: 14, of which 3 were waited for; matrix products, arithmetic and copies ran while one was open for 0% of the time, Pallas kernels for 23%

commit v1 on v0

--- a/solution.py
+++ b/solution.py
@@ -11,6 +11,7 @@
 ROWS = 32
 EXT = 48
 COLS = 128
+HALF = COLS // 2
 BLOCKS = 8
 F32 = jnp.float32
 AXES = ("comp", "lat", "lon")
@@ -80,12 +81,16 @@
     return jnp.take_along_axis(tile, flip, axis=0, mode="promise_in_bounds")
 
 
-def put_piece(store, ref, other, at, count, mirrored_sign):
+def put_piece(store, ref, at, count):
     end = ref.shape[0]
     store[0, at : at + count, :] = ref[end - count : end, :]
     store[1, at : at + count, :] = ref[0:count, :]
-    turned = reverse(other[end - 8 : end, :])
-    if mirrored_sign < 0:
+
+
+def put_mirrored(store, ref, at, count, sign):
+    end = ref.shape[0]
+    turned = reverse(ref[end - 8 : end, :])
+    if sign < 0:
         turned = -turned
     store[2, at : at + count, :] = turned[0:count, :]
 
@@ -112,11 +117,12 @@
 
 def start_rows_kernel(
     fold, lam_in, winds_in, inv_in, fc_in, mask_in, cell_in, weight_in,
-    x_out, first_out, second_out, mirror_out, turn_out,
+    x_out, first_out, second_out, mirror_out, low_out, high_out, turn_out, half_turn_out,
     store, lam, winds, inv, fc, mask, cell, weight, sem,
 ):
     comp, lat_pos, lon_pos, _ = places()
     turn_out[0] = fold[0] // COLS
+    half_turn_out[0] = fold[0] // HALF
     pairs = [(fc_in, fc), (mask_in, mask), (cell_in, cell), (weight_in, weight)]
     for half, rows in enumerate((pl.ds(0, 8), pl.ds(ROWS - 8, 8))):
         at = pl.ds(8 * half, 8)
@@ -145,11 +151,24 @@
         for k in range(1, 4):
             total = total + jnp.where(code[k] == s, weights[k], 0.0)
         x_out[1 + s // 4, s % 4] = total
-    for field, n, a, at, count in first_pieces() + rest_pieces():
-        ref = field_ref(lam, winds, inv, field, n, a)
-        put_piece(store, ref, ref, at, count, sign_of(field))
+    pieces = [(field_ref(lam, winds, inv, f, n, a), at, count, sign_of(f)) for f, n, a, at, count in first_pieces()]
+    pieces += [(field_ref(lam, winds, inv, f, n, a), at, count, sign_of(f)) for f, n, a, at, count in rest_pieces()]
+    for ref, at, count, _ in pieces:
+        put_piece(store, ref, at, count)
     for quad, member, at, count in SINGLES:
-        put_piece(store, x_out.at[quad, member], x_out.at[mirrored_single(quad, member)], at, count, 1)
+        put_piece(store, x_out.at[quad, member], at, count)
+
+    @pl.when(places()[3])
+    def _():
+        for ref, at, count, sign in pieces:
+            put_mirrored(store, ref, at, count, sign)
+        for quad, member, at, count in SINGLES:
+            put_mirrored(store, x_out.at[mirrored_single(quad, member)], at, count, 1)
+        a, b = store[2, 0 : ROW_BUFFER // 2, :], store[2, ROW_BUFFER // 2 : ROW_BUFFER, :]
+        low = lax.broadcasted_iota(jnp.int32, a.shape, 1) < HALF
+        low_out[...] = jnp.where(low, a, roll_lanes(b, HALF))
+        high_out[...] = jnp.where(low, roll_lanes(a, HALF), b)
+
     hand_over(store, first_out, second_out, mirror_out)
 
 
@@ -167,7 +186,7 @@
     return x if by == 0 else pltpu.roll(x, by, axis=0)
 
 
-def pack_columns(slots, own, own_at, to_west, to_east, buffer_at, row_count):
+def pack_columns(slots, strip_at, to_west, to_east, buffer_at, row_count):
     rows = row_count
     used = [k for k, members in enumerate(slots) if members is not None]
     zero = jnp.zeros((rows, COLS), F32)
@@ -182,15 +201,17 @@
     buffers = -(-len(slots) // 4)
     west, east = [zero] * buffers, [zero] * buffers
     for i, k in enumerate(used):
-        own[own_at + k] = strips[i * rows : (i + 1) * rows]
+        ref, at = strip_at[k]
+        ref[at] = strips[i * rows : (i + 1) * rows]
         mine = pair[i * rows : (i + 1) * rows]
         buffer, slot = k // 4, k % 4
         here = (group >= 8 * slot) & (group < 8 * slot + 8)
         west[buffer] = jnp.where(here, roll_lanes(mine, 8 * slot - 8), west[buffer])
         east[buffer] = jnp.where(here, roll_lanes(mine, 8 * slot), east[buffer])
     for buffer in range(buffers):
-        to_west[buffer_at + buffer, 0:rows, :] = west[buffer]
-        to_east[buffer_at + buffer, 0:rows, :] = east[buffer]
+        at = pl.ds(pl.multiple_of(rows * (buffer_at + buffer), 8), rows)
+        to_west[at, :] = west[buffer]
+        to_east[at, :] = east[buffer]
 
 
 def block_slots(read, extra):
@@ -219,15 +240,28 @@
 
     slots = block_slots(read, [x[0, f] for f in range(4)])
     slots += single_slots(lambda q, a: x[q, a])
-    pack_columns(slots, own, 0, to_west, to_east, 0, ROWS)
-
-
-def own_rest_kernel(lam, winds, inv, own, to_west, to_east):
+    pack_columns(slots, [(own, k) for k in range(12)], to_west, to_east, 0, ROWS)
+
+
+def own_rest_kernel(lam_in, winds_in, inv_in, own, to_west, to_east, lam, winds, inv, sem):
+    def fetch(n):
+        levels = pl.ds(4 * n, 4)
+        pairs = ((winds_in.at[:, levels], winds.at[:, levels]), (lam_in.at[levels], lam.at[levels]), (inv_in.at[n], inv.at[n]))
+        return [pltpu.make_async_copy(a, b, sem.at[n - 1, k]) for k, (a, b) in enumerate(pairs)]
+
+    for n in range(1, BLOCKS):
+        for copy in fetch(n):
+            copy.start()
+
     def step(n, carry):
+        for copy in fetch(n):
+            copy.wait()
+
         def read(field, a):
             return field_ref(lam, winds, inv, field, n, a)[...]
 
-        pack_columns(block_slots(read, None), own, 8 * (n - 1), to_west, to_east, 2 * (n - 1), ROWS)
+        strip_at = [(own, 8 * (n - 1) + k) for k in range(8)]
+        pack_columns(block_slots(read, None), strip_at, to_west, to_east, 2 * (n - 1), ROWS)
         return carry
 
     lax.fori_loop(1, BLOCKS, step, 0)
@@ -261,15 +295,35 @@
     return jnp.concatenate(tiles, axis=0)
 
 
-def halo_first_kernel(
-    fold, first_in, second_in, fold_a, fold_b, mid_west, mid_east,
-    south, north, h, hx, own, to_west, to_east,
+REST = BLOCKS - 1
+COL_OWN = 16 * (3 + REST)
+COL_BUFFER = COL_OWN + ROWS * (3 + 2 * REST)
+
+
+def halo_kernel(
+    fold, first_in, second_in, fold_whole, fold_half, mid_west, mid_east, rest_west, rest_east, *refs,
 ):
+    brought_in, (h, hx, own, rest_h, rest_own, to_west, to_east), refs = refs[:BROUGHT], refs[BROUGHT : BROUGHT + 7], refs[BROUGHT + 7 :]
+    brought, (south, north, sem) = refs[:BROUGHT], refs[BROUGHT:]
+    mids = (ROWS * 3, ROWS * 2 * REST)
+    pairs = [(rest_west, to_west.at[pl.ds(COL_OWN + mids[0], mids[1])])]
+    pairs += [(rest_east, to_east.at[pl.ds(COL_OWN + mids[0], mids[1])])]
+    pairs += [(mid_west, to_west.at[pl.ds(COL_OWN, mids[0])]), (mid_east, to_east.at[pl.ds(COL_OWN, mids[0])])]
+    pairs += list(zip(brought_in, brought, strict=True))
+    copies = [pltpu.make_async_copy(a, b, sem.at[k]) for k, (a, b) in enumerate(pairs)]
+    for copy in copies:
+        copy.start()
+
     def beyond_fold():
         turn, lane = fold[0] % COLS, lanes()
         source = jnp.where(turn >= lane, turn - lane, turn - lane + COLS)
-        keep = lax.broadcasted_iota(jnp.int32, (ROW_BUFFER, COLS), 1) <= turn
-        north[...] = jnp.where(keep, pick(fold_a[...], source), pick(fold_b[...], source))
+        in_half = source % HALF
+        few = jnp.concatenate([pick(fold_half[...], in_half), pick(fold_half[...], in_half + HALF)], axis=0)
+        many = pick(fold_whole[...], source)
+        column = lax.broadcasted_iota(jnp.int32, (ROW_BUFFER, COLS), 1)
+        whole_is_first = turn >= HALF
+        first = (column <= turn).astype(jnp.int32)
+        north[...] = jnp.where(first == whole_is_first.astype(jnp.int32), many, few)
 
     settle_rows(first_in, second_in, south, north, beyond_fold)
     for field, _, a, at, count in first_pieces():
@@ -278,34 +332,21 @@
     for quad, member, at, count in SINGLES:
         hx[quad, member, 8 - count : 8, :] = south[at : at + count, :]
         hx[quad, member, 8 : 8 + count, :] = north[at : at + count, :]
+    for field, n, a, at, count in rest_pieces():
+        rest_h[n - 1, field, a, 8 - count : 8, :] = south[at : at + count, :]
+        rest_h[n - 1, field, a, 8 : 8 + count, :] = north[at : at + count, :]
     slots = block_slots(lambda field, a: h[field, a], [hx[0, f] for f in range(4)])
-    slots += single_slots(lambda q, a: hx[q, a])
-    pack_columns(slots, own, 0, to_west, to_east, 0, 16)
-    to_west[:, 16:EXT, :] = mid_west[...]
-    to_east[:, 16:EXT, :] = mid_east[...]
-
-
-REST = BLOCKS - 1
-COL_BUFFER = REST * (EXT + ROWS)
-
-
-def halo_rest_kernel(south, north, mid_west, mid_east, h, own, to_west, to_east, west, east):
-    for field, n, a, at, count in rest_pieces():
-        h[n - 1, field, a, 8 - count : 8, :] = south[at : at + count, :]
-        h[n - 1, field, a, 8 : 8 + count, :] = north[at : at + count, :]
-
-    def step(n, carry):
-        slots = [[h[n, field, a] for a in range(4)] for field in range(3)]
-        pack_columns(slots, own, 3 * n, west, east, n, 16)
-        return carry
-
-    lax.fori_loop(0, REST, step, 0)
-    for out, halo, mid in ((to_west, west, mid_west), (to_east, east, mid_east)):
-        for n in range(REST):
-            out[EXT * n : EXT * n + 16, :] = halo[n]
-            out[EXT * n + 16 : EXT * (n + 1), :] = mid[2 * n]
-            at = EXT * REST + ROWS * n
-            out[at : at + ROWS, :] = mid[2 * n + 1]
+    slots += single_slots(lambda q, a: hx[q, a]) + [None]
+    strip_at = [(own, k) for k in range(11)] + [None]
+    for n in range(REST):
+        slots += [[rest_h[n, field, a] for a in range(4)] for field in range(3)] + [None]
+        strip_at += [(rest_own, 3 * n + k) for k in range(3)] + [None]
+    pack_columns(slots, strip_at, to_west, to_east, 0, 16)
+    for copy in copies:
+        copy.wait()
+
+
+BROUGHT = 5
 
 
 def ext_lanes():
@@ -321,26 +362,28 @@
     return stack([keep_c] * 5), stack([keep_d] * 5)
 
 
-def assemble_strip(slot, west, east, mid, halo=None):
+def edges_of(slot, west, east):
     group = lax.broadcasted_iota(jnp.int32, west.shape, 1) % 32
     edge = jnp.where(group < 8, roll_lanes(west, -8 * slot), roll_lanes(east, 24 - 8 * slot))
-    inner = (group >= 8) & (group < 24)
+    return edge, (group >= 8) & (group < 24)
+
+
+def assemble_strip(slot, sides, buffer, mid, halo_buffer=None, halo=None):
+    rows = pl.ds(pl.multiple_of(COL_OWN + ROWS * buffer, 8), ROWS)
+    edge, inner = edges_of(slot, sides[0][rows, :], sides[1][rows, :])
+    middle = jnp.where(inner, mid, edge)
     if halo is None:
-        return jnp.where(inner, mid, edge)
-    return jnp.concatenate(
-        [
-            jnp.where(inner[0:8], halo[0:8], edge[0:8]),
-            jnp.where(inner[0:32], mid, edge[16:48]),
-            jnp.where(inner[0:8], halo[8:16], edge[8:16]),
-        ],
-        axis=0,
-    )
+        return middle
+    rows = pl.ds(pl.multiple_of(16 * halo_buffer, 8), 16)
+    edge, inner = edges_of(slot, sides[0][rows, :], sides[1][rows, :])
+    outer = jnp.where(inner, halo, edge)
+    return jnp.concatenate([outer[0:8], middle, outer[8:16]], axis=0)
 
 
 class First:
     def __init__(self, lam, winds, inv, h, own, own_halo, from_west, from_east, x_in, hx):
         self.lam, self.winds, self.inv, self.h = lam, winds, inv, h
-        self.own, self.own_halo, self.from_west, self.from_east = own, own_halo, from_west, from_east
+        self.own, self.own_halo, self.sides = own, own_halo, (from_west, from_east)
         self.x_in, self.hx = x_in, hx
 
     def main(self, field, n, a):
@@ -354,7 +397,7 @@
 
     def strip(self, n, which, slot):
         at = 4 * which + slot
-        return assemble_strip(slot, self.from_west[which], self.from_east[which], self.own[at], self.own_halo[at])
+        return assemble_strip(slot, self.sides, which, self.own[at], which, self.own_halo[at])
 
     def single_strip(self, quad):
         return self.strip(0, 0, 3) if quad == 0 else self.strip(0, 2, quad - 1)
@@ -363,7 +406,7 @@
 class Rest:
     def __init__(self, lam, winds, inv, h, own, own_halo, from_west, from_east):
         self.lam, self.winds, self.inv, self.h = lam, winds, inv, h
-        self.own, self.own_halo, self.from_west, self.from_east = own, own_halo, from_west, from_east
+        self.own, self.own_halo, self.sides = own, own_halo, (from_west, from_east)
 
     def main(self, field, n, a):
         mid = field_ref(self.lam, self.winds, self.inv, field, n, a)[...]
@@ -374,12 +417,10 @@
 
     def strip(self, n, which, slot):
         mid = self.own[8 * (n - 1) + 4 * which + slot]
+        buffer = 3 + 2 * (n - 1) + which
         if which == 1:
-            rows = pl.ds(pl.multiple_of(EXT * REST + ROWS * (n - 1), 8), ROWS)
-            return assemble_strip(slot, self.from_west[rows, :], self.from_east[rows, :], mid)
-        rows = pl.ds(pl.multiple_of(EXT * (n - 1), 8), EXT)
-        halo = self.own_halo[3 * (n - 1) + slot]
-        return assemble_strip(slot, self.from_west[rows, :], self.from_east[rows, :], mid, halo)
+            return assemble_strip(slot, self.sides, buffer, mid)
+        return assemble_strip(slot, self.sides, buffer, mid, 2 + n, self.own_halo[3 * (n - 1) + slot])
 
 
 def stack(values):
@@ -433,8 +474,8 @@
     return new + [total]
 
 
-def solve_first(fields, tracer):
-    return solve(lambda a, b: fields.main(3 + b, 0, a), lambda d: fields.strip(0, 1, d), unstack(tracer))
+def solve_first(inverse, strip_inverse, tracer):
+    return solve(lambda a, b: inverse[4 * a + b], lambda d: strip_inverse[d], unstack(tracer))
 
 
 def main_from_strip(main, strip, a, width):
@@ -460,12 +501,11 @@
     return [fields.main(0, n, a) for a in range(4)] + [fields.strip(n, 0, 0)]
 
 
-def fluxes_out(fields, state, payload, strip_coefs):
+def fluxes_out(fields, state, payload, strips):
     surface = state[0] * fields.single(3, 1)
     for f in range(4):
         payload[f] = fields.single(0, f) * surface
-    wet_strip = roll_lanes(fields.single_strip(3), -32)
-    payload[4] = strip_coefs * replicate(state[4] * wet_strip, 0)
+    payload[4] = strips[0] * replicate(state[4] * strips[1], 0)
 
 
 def couple(fields, received, strip_coefs, strip_weights, land_strip):
@@ -494,7 +534,8 @@
 
 def first_kernel(*refs):
     fields = First(*refs[: INPUTS + 2])
-    payload, state, land, to_south, to_north, to_west, strip_coefs, strip_weights = refs[INPUTS + 2 :]
+    payload, state, land, to_south, to_north, to_west, strip_coefs, strip_weights = refs[INPUTS + 2 : INPUTS + 10]
+    inverse, strip_inverse, flux_strips = refs[INPUTS + 10 :]
     quads = [fields.single_strip(q) for q in range(4)]
     main_land = fields.single(3, 2)
     land[...] = stack([main_land] * 4 + [replicate(quads[3], 2)])
@@ -502,10 +543,16 @@
     for ref, value in zip(coefs, coefficients(fields, 0, barrier_masks()), strict=True):
         ref[...] = value
     tracer = advect(stack(load_block(fields, 0)), coefs, land)
-    merged = merge(solve_first(fields, tracer))
+    for a in range(4):
+        for b in range(4):
+            inverse[4 * a + b] = fields.main(3 + b, 0, a)
+        strip_inverse[a] = fields.strip(0, 1, a)
+    flux_strips[0] = quads[0]
+    flux_strips[1] = roll_lanes(quads[3], -32)
+    merged = merge(solve_first(inverse, strip_inverse, tracer))
     for a in range(5):
         state[a] = merged[a]
-    fluxes_out(fields, merged, payload, quads[0])
+    fluxes_out(fields, merged, payload, flux_strips)
     for f in range(4):
         strip_coefs[f] = roll_lanes(quads[0], -32 * f)
     for k in range(9):
@@ -552,9 +599,8 @@
 
 
 def rest_second_kernel(*refs):
-    fold, inv, strip_inverse, land, state, coefs, first_in, second_in, fold_a, fold_b, before = refs[:11]
-    out, result, south, north, halo, sem = refs[11:]
-    del before
+    fold, inv, strip_inverse, land, state, coefs, first_in, second_in, fold_a, fold_b = refs[:10]
+    out, result, south, north, halo, sem = refs[10:]
 
     def beyond_fold():
         turn, lane = fold[0] % COLS, lanes()
@@ -601,23 +647,25 @@
     copy_all([(result, out.at[pl.ds(4, 4 * REST)])], sem)
 
 
-def second_kernel(*refs):
-    fields = First(None, None, *refs[:INPUTS])
-    land, to_south, to_north, to_west, strip_coefs, strip_weights, received, state_in = refs[INPUTS : INPUTS + 8]
-    payload, state = refs[INPUTS + 8 :]
+def second_kernel(
+    x_in, hx, land, to_south, to_north, to_west, strip_coefs, strip_weights, inverse, strip_inverse, flux_strips,
+    received, state_in, payload, state,
+):
+    fields = First(*[None] * 8, x_in, hx)
     added, added_strip = couple(fields, received, strip_coefs, strip_weights, land[4 * EXT :])
     lane = ext_lanes()
     strip = state_in[4] + jnp.where(lane < 32, added_strip, 0.0)
     top = main_from_strip(state_in[0] + added, strip, 0, 1)
     tracer = stack([top] + [state_in[a] for a in range(1, 4)] + [strip])
-    solved = solve_first(fields, advect(tracer, (to_south, to_north, to_west), land))
+    solved = solve_first(inverse, strip_inverse, advect(tracer, (to_south, to_north, to_west), land))
     merged = [main_from_strip(solved[a], solved[4], a, 3) for a in range(4)] + [solved[4]]
     for a in range(5):
         state[a] = merged[a]
-    fluxes_out(fields, merged, payload, fields.single_strip(0))
-
-
-def last_kernel(x_in, hx, land, strip_coefs, strip_weights, received, state, out, result, sem):
+    fluxes_out(fields, merged, payload, flux_strips)
+
+
+def last_kernel(x_in, hx, land, strip_coefs, strip_weights, received, state, rest, out, result, sem):
+    del rest
     fields = First(*[None] * 8, x_in, hx)
     added, added_strip = couple(fields, received, strip_coefs, strip_weights, land[4 * EXT :])
     strip = state[4] + added_strip
@@ -631,8 +679,7 @@
     "start_rows_kernel": 3.2,
     "own_first_kernel": 2.0,
     "own_rest_kernel": 2.5,
-    "halo_first_kernel": 1.7,
-    "halo_rest_kernel": 1.3,
+    "halo_kernel": 2.8,
     "first_kernel": 1.0,
     "rest_first_kernel": 4.3,
     "second_kernel": 1.0,
@@ -690,9 +737,9 @@
     wind = winds[:, 0]
     inv = block_inverse[0]
     rows = (ROW_BUFFER, COLS)
-    x, first, second, mirror, turn = call(
+    x, first, second, mirror, low, high, turn, half_turn = call(
         start_rows_kernel,
-        [((4, 4, ROWS, COLS), VMEM)] + [(rows, VMEM)] * 3 + [((1,), SMEM)],
+        [((4, 4, ROWS, COLS), VMEM)] + [(rows, VMEM)] * 3 + [((ROW_BUFFER // 2, COLS), VMEM)] * 2 + [((1,), SMEM)] * 2,
         (fold_map, lam, wind, inv, flux_coef[0], sea_mask, intersection_cell, intersection_weight),
         [SMEM] + [HBM] * 7,
         [
@@ -723,58 +770,58 @@
     state_in = (lam, wind, inv)
     swapped = swap(first, second)
 
-    def across_fold(total, mirror, lam, wind, inv, x):
-        folded = [lax.ppermute(mirror, AXES, fold_pairs(total - k, (0, 1))) for k in range(2)]
+    def across_fold(step, mirror, low, high, lam, wind, inv, x):
+        total, in_late_half = step // 2, step % 2
+        whole = lax.ppermute(mirror, AXES, fold_pairs(total - 1 + in_late_half, (0, 1)))
+        half = lax.ppermute(high if in_late_half else low, AXES, fold_pairs(total - in_late_half, (0, 1)))
+        folded = (whole, half)
         own = call(
             own_first_kernel,
-            [vmem(12, ROWS), vmem(3, ROWS), vmem(3, ROWS)],
+            [vmem(12, ROWS), vmem(3 * ROWS), vmem(3 * ROWS)]
+            + [vmem(4, ROWS), vmem(2, 4, ROWS), vmem(1, 4, 4, ROWS)],
             (lam, wind, inv, x),
             [HBM] * 4,
-            [
-                pltpu.VMEM((4, ROWS, COLS), F32),
-                pltpu.VMEM((2, 4, ROWS, COLS), F32),
-                pltpu.VMEM((1, 4, 4, ROWS, COLS), F32),
-                pltpu.VMEM((4, 4, ROWS, COLS), F32),
-                pltpu.SemaphoreType.DMA((4,)),
-            ],
+            [pltpu.VMEM((4, 4, ROWS, COLS), F32), pltpu.SemaphoreType.DMA((4,))],
         )
         rest_own = call(
             own_rest_kernel,
-            [vmem(8 * REST, ROWS), vmem(2 * REST, ROWS), vmem(2 * REST, ROWS)],
+            [vmem(8 * REST, ROWS), vmem(2 * REST * ROWS), vmem(2 * REST * ROWS)],
             (lam, wind, inv),
-            [VMEM] * 3,
+            [HBM] * 3,
+            [
+                pltpu.VMEM((32, ROWS, COLS), F32),
+                pltpu.VMEM((2, 32, ROWS, COLS), F32),
+                pltpu.VMEM((BLOCKS, 4, 4, ROWS, COLS), F32),
+                pltpu.SemaphoreType.DMA((REST, 3)),
+            ],
         )
         return *folded, *own, *rest_own
 
-    *folded, own, mid_west, mid_east, rest_own, rest_mid_west, rest_mid_east = lax.switch(
-        turn[0], [functools.partial(across_fold, total) for total in range(LON)], mirror, lam, wind, inv, x
+    *folded, own, mid_west, mid_east, lam0, wind0, inv0, rest_own, rest_mid_west, rest_mid_east = lax.switch(
+        half_turn[0], [functools.partial(across_fold, step) for step in range(2 * LON)], mirror, low, high, lam, wind, inv, x
     )
     moved = (*swapped, *folded)
-    south, north, h, hx, own_halo, to_west, to_east = call(
-        halo_first_kernel,
-        [vmem(ROW_BUFFER)] * 2 + [vmem(7, 4, 16), vmem(4, 4, 16), vmem(12, 16), vmem(3, EXT), vmem(3, EXT)],
-        (fold_map, *moved, mid_west, mid_east),
-        [SMEM] + [VMEM] * 6,
+    brought = (own, lam0, wind0, inv0, rest_own)
+    h, hx, own_halo, rest_h, rest_own_halo, to_west, to_east, own, lam0, wind0, inv0, rest_own = call(
+        halo_kernel,
+        [vmem(7, 4, 16), vmem(4, 4, 16), vmem(12, 16), vmem(REST, 3, 4, 16), vmem(3 * REST, 16)]
+        + [vmem(COL_BUFFER)] * 2
+        + [(value.shape, VMEM) for value in brought],
+        (fold_map, *moved, mid_west, mid_east, rest_mid_west, rest_mid_east, *brought),
+        [SMEM] + [VMEM] * 4 + [HBM] * (4 + BROUGHT),
+        [pltpu.VMEM((ROW_BUFFER, COLS), F32)] * 2 + [pltpu.SemaphoreType.DMA((4 + BROUGHT,))],
     )
-    rest_h, rest_own_halo, rest_to_west, rest_to_east = call(
-        halo_rest_kernel,
-        [vmem(REST, 3, 4, 16), vmem(3 * REST, 16), vmem(COL_BUFFER), vmem(COL_BUFFER)],
-        (south, north, rest_mid_west, rest_mid_east),
-        [VMEM] * 4,
-        [pltpu.VMEM((REST, 16, COLS), F32)] * 2,
-    )
-    h, rest_to_west, rest_to_east = lax.optimization_barrier((h, rest_to_west, rest_to_east))
-    args = (inv, h, own, own_halo, *around(to_west, to_east), x, hx)
+    from_sides = around(to_west, to_east)
     five = vmem(5, EXT)
     tall = vmem(5 * EXT)
     payload, state, land, *tables = call(
         first_kernel,
-        [five, five] + [tall] * 4 + [vmem(4, EXT), vmem(9, EXT)],
-        (lam, wind, *args),
+        [five, five] + [tall] * 4 + [vmem(k, EXT) for k in (4, 9, 16, 4, 2)],
+        (lam0, wind0, inv0, h, own, own_halo, *from_sides, x, hx),
         [VMEM] * (INPUTS + 2),
     )
     received = across(payload)
-    rest_args = (*state_in, rest_h, rest_own, rest_own_halo, *around(rest_to_west, rest_to_east))
+    rest_args = (*state_in, rest_h, rest_own, rest_own_halo, *from_sides)
     whole = ((32, ROWS, COLS), HBM)
     done = pltpu.SemaphoreType.DMA((1,))
     rest_state, rest_coefs, strip_inverse, *rest_rows = call(
@@ -785,27 +832,19 @@
         [pltpu.VMEM((3, REST, 5, 8, COLS), F32), pltpu.VMEM((3, 120, COLS), F32)]
         + [pltpu.VMEM((5 * EXT, COLS), F32)] * 2,
     )
-    rest_swapped = swap(*rest_rows[:2])
-    received, rest_mirror = lax.optimization_barrier((received, rest_rows[2]))
-    payload, state = call(
-        second_kernel, [five, five], (*args, land, *tables, received, state), [VMEM] * (INPUTS + 8)
-    )
-
-    def finish(total, mirror, payload, last_args, rest_args, swapped):
-        folded = [lax.ppermute(mirror, AXES, fold_pairs(total - k, (1,))) for k in range(2)]
-        x, hx, land, strip_coefs, strip_weights, state = last_args
-        (out,) = call(
-            last_kernel,
-            [whole],
-            (x, hx, land, strip_coefs, strip_weights, across(payload), state),
-            [VMEM] * 7,
-            [pltpu.VMEM((4, ROWS, COLS), F32), done],
-        )
-        return call(
+    def finish(total, rest_rows, received, chain, rest_args):
+        folded = [lax.ppermute(rest_rows[2], AXES, fold_pairs(total - k, (1,))) for k in range(2)]
+        swapped = swap(*rest_rows[:2])
+        received, swapped = lax.optimization_barrier((received, swapped))
+        x, hx, land, *tables, state = chain
+        payload, state = call(second_kernel, [five, five], (x, hx, land, *tables, received, state), [VMEM] * 13)
+        payload, folded = lax.optimization_barrier((payload, folded))
+        received = across(payload)
+        (rest,) = call(
             rest_second_kernel,
             [whole],
-            (*rest_args, *swapped, *folded, out),
-            [SMEM] + [VMEM] * 9 + [HBM],
+            (*rest_args, *swapped, *folded),
+            [SMEM] + [VMEM] * 9,
             [
                 pltpu.VMEM((4 * REST, ROWS, COLS), F32),
                 pltpu.VMEM((120, COLS), F32),
@@ -813,17 +852,23 @@
                 pltpu.VMEM((REST, 5, 16, COLS), F32),
                 done,
             ],
-            input_output_aliases={10: 0},
+        )
+        return call(
+            last_kernel,
+            [whole],
+            (x, hx, land, *tables[3:5], received, state, rest),
+            [VMEM] * 7 + [HBM],
+            [pltpu.VMEM((4, ROWS, COLS), F32), done],
+            input_output_aliases={7: 0},
         )[0]
 
     out = lax.switch(
         turn[0],
         [functools.partial(finish, total) for total in range(LON)],
-        rest_mirror,
-        payload,
-        (x, hx, land, *tables[3:], state),
+        rest_rows,
+        received,
+        (x, hx, land, *tables, state),
         (fold_map, inv, strip_inverse, land, rest_state, rest_coefs),
-        rest_swapped,
     )
     return out[None]
 

time: 61.2 us -> 56.6 us (0.925)
  the two profiles are of different devices: /device:TPU:16 before, /device:TPU:112 now
where the time goes in v1:
time: 56.6 us; the launch traced here: 56.5 us
  Pallas kernels  23.9 us (42%)
  starting transfers between devices  21.3 us (38%)
  waiting for transfers between devices  9.4 us (17%)
  between operations  1.58 us (3%)
    pallas_call x9, Pallas kernels, call(): pl.pallas_call(kernel, out_shape=[jax.ShapeDtypeStruct(s, jnp.int32 if sp...  23.9 us
    ppermute x2, starting transfers between devices, across(): lax.ppermute(value, AXES, [(i, (i + LAT * LON) % (2 * LAT * LON)) for i i...  8.47 us
    ppermute x1, waiting for transfers between devices, around(): lax.ppermute(to_east, AXES, lon_pairs(1))  5.1 us
    ppermute x1, starting transfers between devices, across_fold(): lax.ppermute(mirror, AXES, fold_pairs(total - 1 + in_late_half, (0, 1)))  4.44 us
    ppermute x1, starting transfers between devices, around(): lax.ppermute(to_west, AXES, lon_pairs(-1))  2.94 us
    ppermute x1, starting transfers between devices, across_fold(): lax.ppermute(high if in_late_half else low, AXES, fold_pairs(total - in_l...  2.42 us
    ppermute x2, waiting for transfers between devices, swap(): lax.ppermute(first, AXES, swap_pairs(0))  2.19 us
    ppermute x1, waiting for transfers between devices, across_fold(): lax.ppermute(high if in_late_half else low, AXES, fold_pairs(total - in_l...  2.08 us
  transfers between devices with their start and end apart: 12, of which 3 were waited for; matrix products, arithmetic and copies ran while one was open for 0% of the time, Pallas kernels for 28%

profile of v1, /device:TPU:112, one launch (start us, length us, event | category | flops | bytes accessed | tf_op | source)
XLA Modules:
  0.0 56.5 jit_solution(1102078307265008014)
XLA Ops:
  0.0 3.4 %shard_map.90 = (f32[4,4,32,128]{3,2,1,0:T(8,128)S(1)}, f32[464,128]{1,0:T(8,128)}, f32[464,128]{1,0:T(8,128)}, f32[464,128]{1,0:T(8,128)}, f32[232,128]{1,0:T(8...) custom-call(s32[1024]{0:T(1024)} %fold.3, f32[32,32,128]{2,1,0:T(8,128)} %bitcast.58, f32[2,32,32,128]{3,2,1,0:T(8,128)} %bitcast.40, ...), custom_call_target="tpu_custom_call" | custom-call | bytes 11200000 | tf_op jit(solution)/shard_map/pallas_call | solution.py:693
  3.4 0.3 collective-permute-start.72
  3.7 0.7 %collective-permute-start.73 = (f32[464,128]{1,0:T(8,128)}, f32[464,128]{1,0:T(8,128)S(1)}, u32[]{:S(2)}, u32[]{:S(2)}) collective-permute-start(f32[464,128]{1,0:T(8,128)} %get-tuple-element.1065), channel_id=1, source_target_pairs={{8,16},{16,8},{9,17},{17,9},{10,18},{18,10},{11,19},{19,11},{12,20... | collective-permute-start | bytes 712712 | tf_op jit(solution)/shard_map/ppermute | solution.py:759
  5.0 14.7 %conditional.2 = (f32[464,128]{1,0:T(8,128)}, f32[232,128]{1,0:T(8,128)}, f32[12,32,128]{2,1,0:T(8,128)S(1)}, f32[96,128]{1,0:T(8,128)}, f32[96,128]{1,0:T(8,128...) conditional(s32[]{:T(128)} %bitcast.13, ...), branch_computations={%region_0.0_spmd, %region_1.0_spmd, %region_2.0_spmd, %region_3.0_... | conditional | bytes 31855724 | solution.py:800
  5.1 0.0 copy-start.13
  5.1 0.0 copy-start.30
  5.1 0.0 copy-start.47
  5.1 4.4 %collective-permute-start.24 = (f32[464,128]{1,0:T(8,128)}, f32[464,128]{1,0:T(8,128)}, u32[]{:S(2)}, u32[]{:S(2)}) collective-permute-start(f32[464,128]{1,0:T(8,128)} %get-tuple-element.723), channel_id=1, source_target_pairs={{56,61},{57,60},{58,59},{59,58},{60,57},{61,56},{62,63},{63,62},{1... | collective-permute-start | bytes 712712 | tf_op jit(solution)/shard_map/cond/branch_12_fun/ppermute | solution.py:775
  9.6 2.4 %collective-permute-start.25 = (f32[232,128]{1,0:T(8,128)}, f32[232,128]{1,0:T(8,128)}, u32[]{:S(2)}, u32[]{:S(2)}) collective-permute-start(f32[232,128]{1,0:T(8,128)} %get-tuple-element.724), channel_id=1, source_target_pairs={{56,62},{57,61},{58,60},{59,59},{60,58},{61,57},{62,56},{63,63},{1... | collective-permute-start | bytes 356360 | tf_op jit(solution)/shard_map/cond/branch_12_fun/ppermute | solution.py:776
  12.0 4.3 %branch_12_fun.3 = (f32[56,32,128]{2,1,0:T(8,128)}, f32[448,128]{1,0:T(8,128)}, f32[448,128]{1,0:T(8,128)}) custom-call(f32[32,32,128]{2,1,0:T(8,128)} %get-tuple-element.725.lam_in, f32[2,32,32,128]{3,2,1,0:T(8,128)} %get-tuple-element.726.winds_in, f32[8,4,4,32,128]{4,3,2,1,0:T(8,128)} %get-tuple-element.727.inv_in), custom_call_target="tpu_custom_call" | custom-call | bytes 8750000 | tf_op jit(solution)/shard_map/cond/branch_12_fun/pallas_call | solution.py:693
  16.4 1.3 %branch_12_fun.2 = (f32[12,32,128]{2,1,0:T(8,128)S(1)}, f32[96,128]{1,0:T(8,128)}, f32[96,128]{1,0:T(8,128)}, f32[4,32,128]{2,1,0:T(8,128)}, f32[2,4,32,128]{3,2,1,0:T(8,128)}, /*index=5*/f32[1,4,4,32,128]{4,3,2,1,0:T(8,128)}) custom-call(f32[32,32,128]{2,1,0:T(8,128)S(1)} %copy-done.47, f32[2,32,32,128]{3,2,1,0:T(8,128)S(1)} %copy-done.30, ...), custom_call_target="tpu_custom_call" | custom-call | bytes 7000000 | tf_op jit(solution)/shard_map/cond/branch_12_fun/pallas_call | solution.py:693
  17.6 2.1 %collective-permute-done.25 = f32[232,128]{1,0:T(8,128)} collective-permute-done((f32[232,128]{1,0:T(8,128)}, f32[232,128]{1,0:T(8,128)}, u32[]{:S(2)}, u32[]{:S(2)}) %collective-permute-start.25) | collective-permute-done | bytes 118816 | tf_op jit(solution)/shard_map/cond/branch_12_fun/ppermute | solution.py:776
  19.7 0.0 collective-permute-done.24
  19.7 0.0 copy-start.34
  19.8 3.0 %shard_map.91 = (f32[7,4,16,128]{3,2,1,0:T(8,128)S(1)}, f32[4,4,16,128]{3,2,1,0:T(8,128)S(1)}, f32[12,16,128]{2,1,0:T(8,128)S(1)}, f32[7,3,4,16,128]{4,3,2,1,0:T...) custom-call(s32[1024]{0:T(1024)} %fold.3, ...), custom_call_target="tpu_custom_call" | custom-call | bytes 9800000 | tf_op jit(solution)/shard_map/pallas_call | solution.py:693
  22.8 0.0 collective-permute-start.74
  22.8 2.9 %collective-permute-start.75 = (f32[704,128]{1,0:T(8,128)S(1)}, f32[704,128]{1,0:T(8,128)S(1)}, u32[]{:S(2)}, u32[]{:S(2)}) collective-permute-start(f32[704,128]{1,0:T(8,128)S(1)} %get-tuple-element.1086), channel_id=1, source_target_pairs={{0,7},{1,0},{2,1},{3,2},{4,3},{5,4},{6,5},{7,6},{8,15},{9,8},{10,9... | collective-permute-start | bytes 1081352 | tf_op jit(solution)/shard_map/ppermute | solution.py:762
  25.7 5.1 %collective-permute-done.74.refs_6_ = f32[704,128]{1,0:T(8,128)S(1)} collective-permute-done((f32[704,128]{1,0:T(8,128)S(1)}, f32[704,128]{1,0:T(8,128)S(1)}, u32[]{:S(2)}, u32[]{:S(2)}) %collective-permute-start.74) | collective-permute-done | bytes 360480 | tf_op jit(solution)/shard_map/ppermute | solution.py:762
  30.8 0.9 %shard_map.92 = (f32[5,48,128]{2,1,0:T(8,128)S(1)}, f32[5,48,128]{2,1,0:T(8,128)S(1)}, f32[240,128]{1,0:T(8,128)S(1)}, f32[240,128]{1,0:T(8,128)S(1)}, f32[240,1...) custom-call(f32[4,32,128]{2,1,0:T(8,128)S(1)} %get-tuple-element.108, ...), custom_call_target="tpu_custom_call" | custom-call | bytes 3500000 | tf_op jit(solution)/shard_map/pallas_call | solution.py:693
  31.7 1.4 %collective-permute-start.76 = (f32[5,48,128]{2,1,0:T(8,128)S(1)}, f32[5,48,128]{2,1,0:T(8,128)S(1)}, u32[]{:S(2)}, u32[]{:S(2)}) collective-permute-start(f32[5,48,128]{2,1,0:T(8,128)S(1)} %get-tuple-element.1097), channel_id=1, source_target_pairs={{0,64},{1,65},{2,66},{3,67},{4,68},{5,69},{6,70},{7,71},{8,72},{9,... | collective-permute-start | bytes 368648 | tf_op jit(solution)/shard_map/ppermute | solution.py:765
  33.8 0.0 copy-start.51
  33.8 4.2 %shard_map.93 = (f32[7,5,32,128]{3,2,1,0:T(8,128)S(1)}, f32[7,3,240,128]{3,2,1,0:T(8,128)S(1)}, f32[7,4,32,128]{3,2,1,0:T(8,128)S(1)}, f32[120,128]{1,0:T(8,128)...) custom-call(f32[32,32,128]{2,1,0:T(8,128)S(1)} %bitcast.75, f32[2,32,32,128]{3,2,1,0:T(8,128)S(1)} %bitcast.57, ...), custom_call_target="tpu_custom_call" | custom-call | bytes 15050000 | tf_op jit(solution)/shard_map/pallas_call | solution.py:693
  38.0 18.2 %conditional.3 = (f32[1,32,32,128]{3,2,1,0:T(8,128)}) conditional(s32[]{:T(128)} %bitcast.12, (f32[120,128]{1,0:T(8,128)S(1)}, f32[120,128]{1,0:T(8,128)S(1)}, f32[5,48,128]{2,1,0:T(8,128)S(1)}, f32[4,4,32,128]{3,2,1,0:T(8,128)S(1)}, f32[4,4,16,128]{3,2,1,0:T(8,128)S(1)}, /*index=5*/f32[240,128]{1,0:T(8,128)S(1)}, ...), branch_computations={%region_16.0_spmd, %region_17.0_spmd, %region_18.0_spmd, %region_1... | conditional | bytes 22824768 | solution.py:865
  38.1 0.1 collective-permute-start.62
  38.2 0.7 %collective-permute-start.63 = (f32[120,128]{1,0:T(8,128)S(1)}, f32[120,128]{1,0:T(8,128)S(1)}, u32[]{:S(2)}, u32[]{:S(2)}) collective-permute-start(f32[120,128]{1,0:T(8,128)S(1)} %get-tuple-element.970), channel_id=1, source_target_pairs={{8,16},{16,8},{9,17},{17,9},{10,18},{18,10},{11,19},{19,11},{12,20... | collective-permute-start | bytes 184328 | tf_op jit(solution)/shard_map/cond/branch_6_fun/ppermute | solution.py:759
  38.9 0.7 %collective-permute-start.65 = (f32[120,128]{1,0:T(8,128)S(1)}, f32[120,128]{1,0:T(8,128)S(1)}, u32[]{:S(2)}, u32[]{:S(2)}) collective-permute-start(f32[120,128]{1,0:T(8,128)S(1)} %get-tuple-element.974), channel_id=1, source_target_pairs={{120,125},{121,124},{122,123},{123,122},{124,121},{125,120},{126,1... | collective-permute-start | bytes 184328 | tf_op jit(solution)/shard_map/cond/branch_6_fun/ppermute | solution.py:836
  39.5 0.7 %collective-permute-start.64 = (f32[120,128]{1,0:T(8,128)S(1)}, f32[120,128]{1,0:T(8,128)S(1)}, u32[]{:S(2)}, u32[]{:S(2)}) collective-permute-start(f32[120,128]{1,0:T(8,128)S(1)} %get-tuple-element.974), channel_id=1, source_target_pairs={{120,126},{121,125},{122,124},{123,123},{124,122},{125,121},{126,1... | collective-permute-start | bytes 184328 | tf_op jit(solution)/shard_map/cond/branch_6_fun/ppermute | solution.py:836
  40.2 2.2 %collective-permute-done.62.refs_6_ = f32[120,128]{1,0:T(8,128)S(1)} collective-permute-done((f32[120,128]{1,0:T(8,128)S(1)}, f32[120,128]{1,0:T(8,128)S(1)}, u32[]{:S(2)}, u32[]{:S(2)}) %collective-permute-start.62) | collective-permute-done | bytes 61472 | tf_op jit(solution)/shard_map/cond/branch_6_fun/ppermute | solution.py:759
  42.4 0.8 %branch_6_fun.7 = (f32[5,48,128]{2,1,0:T(8,128)S(1)}, f32[5,48,128]{2,1,0:T(8,128)S(1)}) custom-call(f32[4,4,32,128]{3,2,1,0:T(8,128)S(1)} %get-tuple-element.957.x_in, f32[4,4,16,128]{3,2,1,0:T(8,128)S(1)} %get-tuple-element.958.hx, f32[240,128]{1,0:T(8,128)S(1)} %get-tuple-element.959.land.refs_3_, f32[240,128]{1,0:T(8,128)S(1)} %get-tuple-element.962.to_south, ...), custom_call_target="tpu_custom_call" | custom-call | bytes 3500000 | tf_op jit(solution)/shard_map/cond/branch_6_fun/pallas_call | solution.py:693
  43.2 7.1 %collective-permute-start.66 = (f32[5,48,128]{2,1,0:T(8,128)S(1)}, f32[5,48,128]{2,1,0:T(8,128)S(1)}, u32[]{:S(2)}, u32[]{:S(2)}) collective-permute-start(f32[5,48,128]{2,1,0:T(8,128)S(1)} %get-tuple-element.975), channel_id=1, source_target_pairs={{0,64},{1,65},{2,66},{3,67},{4,68},{5,69},{6,70},{7,71},{8,72},{9,... | collective-permute-start | bytes 368648 | tf_op jit(solution)/shard_map/cond/branch_6_fun/ppermute | solution.py:765
  50.4 5.0 %branch_6_fun.8.rest = f32[32,32,128]{2,1,0:T(8,128)} custom-call(s32[1024]{0:T(1024)S(1)} %get-tuple-element.977.refs_0_, f32[8,4,4,32,128]{4,3,2,1,0:T(8,128)S(1)} %get-tuple-element.978.refs_1_, f32[7,4,32,128]{3,2,1,0:T(8,128)S(1)} %get-tuple-element.979.refs_2_, f32[240,128]{1,0:T(8,128)S(1)} %get-tuple-element.959.land.refs_3_, ...), custom_call_target="tpu_custom_call" | custom-call | bytes 16099999 | tf_op jit(solution)/shard_map/cond/branch_6_fun/pallas_call | solution.py:693
  55.4 0.9 %branch_6_fun.9 = f32[32,32,128]{2,1,0:T(8,128)} custom-call(f32[4,4,32,128]{3,2,1,0:T(8,128)S(1)} %get-tuple-element.957.x_in, f32[4,4,16,128]{3,2,1,0:T(8,128)S(1)} %get-tuple-element.958.hx, f32[240,128]{1,0:T(8,128)S(1)} %get-tuple-element.959.land.refs_3_, f32[4,48,128]{2,1,0:T(8,128)S(1)} %get-tuple-element.960.strip_coefs, ...), custom_call_target="tpu_custom_call", output_to_operand_aliasing={{}: (7, {})} | custom-call | bytes 1750000 | tf_op jit(solution)/shard_map/cond/branch_6_fun/pallas_call | solution.py:693
  (17 shorter events, 0.0 us)
Async XLA Ops:
  3.4 16.3 %collective-permute-start.72 = (f32[464,128]{1,0:T(8,128)}, f32[464,128]{1,0:T(8,128)S(1)}, u32[]{:S(2)}, u32[]{:S(2)}) collective-permute-start(f32[464,128]{1,0:T(8,128)} %get-tuple-element.1064), channel_id=1, source_target_pairs={{0,8},{8,0},{1,9},{9,1},{2,10},{10,2},{3,11},{11,3},{4,12},{12,4},... | collective-permute-start | bytes 712712 | tf_op jit(solution)/shard_map/ppermute | solution.py:759
  3.7 16.0 %collective-permute-start.73 = (f32[464,128]{1,0:T(8,128)}, f32[464,128]{1,0:T(8,128)S(1)}, u32[]{:S(2)}, u32[]{:S(2)}) collective-permute-start(f32[464,128]{1,0:T(8,128)} %get-tuple-element.1065), channel_id=1, source_target_pairs={{8,16},{16,8},{9,17},{17,9},{10,18},{18,10},{11,19},{19,11},{12,20... | collective-permute-start | bytes 712712 | tf_op jit(solution)/shard_map/ppermute | solution.py:759
  5.1 11.2 %copy-start.13 = (f32[8,4,4,32,128]{4,3,2,1,0:T(8,128)S(1)}, f32[8,4,4,32,128]{4,3,2,1,0:T(8,128)}, u32[]{:S(2)}) copy-start(f32[8,4,4,32,128]{4,3,2,1,0:T(8,128)} %get-tuple-element.727.inv_in) | copy-start | bytes 6291460 | tf_op jit(solution)/shard_map/cond
  5.1 11.2 %copy-start.30 = (f32[2,32,32,128]{3,2,1,0:T(8,128)S(1)}, f32[2,32,32,128]{3,2,1,0:T(8,128)}, u32[]{:S(2)}) copy-start(f32[2,32,32,128]{3,2,1,0:T(8,128)} %get-tuple-element.726.winds_in) | copy-start | bytes 3145732 | tf_op jit(solution)/shard_map/cond
  5.1 11.2 %copy-start.47 = (f32[32,32,128]{2,1,0:T(8,128)S(1)}, f32[32,32,128]{2,1,0:T(8,128)}, u32[]{:S(2)}) copy-start(f32[32,32,128]{2,1,0:T(8,128)} %get-tuple-element.725.lam_in) | copy-start | bytes 1572868 | tf_op jit(solution)/shard_map/cond
  5.1 14.6 %collective-permute-start.24 = (f32[464,128]{1,0:T(8,128)}, f32[464,128]{1,0:T(8,128)}, u32[]{:S(2)}, u32[]{:S(2)}) collective-permute-start(f32[464,128]{1,0:T(8,128)} %get-tuple-element.723), channel_id=1, source_target_pairs={{56,61},{57,60},{58,59},{59,58},{60,57},{61,56},{62,63},{63,62},{1... | collective-permute-start | bytes 712712 | tf_op jit(solution)/shard_map/cond/branch_12_fun/ppermute | solution.py:775
  9.6 10.2 %collective-permute-start.25 = (f32[232,128]{1,0:T(8,128)}, f32[232,128]{1,0:T(8,128)}, u32[]{:S(2)}, u32[]{:S(2)}) collective-permute-start(f32[232,128]{1,0:T(8,128)} %get-tuple-element.724), channel_id=1, source_target_pairs={{56,62},{57,61},{58,60},{59,59},{60,58},{61,57},{62,56},{63,63},{1... | collective-permute-start | bytes 356360 | tf_op jit(solution)/shard_map/cond/branch_12_fun/ppermute | solution.py:776
  19.7 14.0 %copy-start = (f32[1,8,4,4,32,128]{5,4,3,2,1,0:T(8,128)S(1)}, f32[1,8,4,4,32,128]{5,4,3,2,1,0:T(8,128)}, u32[]{:S(2)}) copy-start(f32[1,8,4,4,32,128]{5,4,3,2,1,0:T(8,128)} %param.34) | copy-start | bytes 6291460
  19.7 14.0 %copy-start.17 = (f32[2,1,32,32,128]{4,3,2,1,0:T(8,128)S(1)}, f32[2,1,32,32,128]{4,3,2,1,0:T(8,128)}, u32[]{:S(2)}) copy-start(f32[2,1,32,32,128]{4,3,2,1,0:T(8,128)} %param.33) | copy-start | bytes 3145732
  19.7 14.0 %copy-start.34 = (f32[1,32,32,128]{3,2,1,0:T(8,128)S(1)}, f32[1,32,32,128]{3,2,1,0:T(8,128)}, u32[]{:S(2)}) copy-start(f32[1,32,32,128]{3,2,1,0:T(8,128)} %param.32) | copy-start | bytes 1572868
  22.8 8.1 %collective-permute-start.74 = (f32[704,128]{1,0:T(8,128)S(1)}, f32[704,128]{1,0:T(8,128)S(1)}, u32[]{:S(2)}, u32[]{:S(2)}) collective-permute-start(f32[704,128]{1,0:T(8,128)S(1)} %get-tuple-element.1085), channel_id=1, source_target_pairs={{0,1},{1,2},{2,3},{3,4},{4,5},{5,6},{6,7},{7,0},{8,9},{9,10},{10,1... | collective-permute-start | bytes 1081352 | tf_op jit(solution)/shard_map/ppermute | solution.py:762
  22.8 8.1 %collective-permute-start.75 = (f32[704,128]{1,0:T(8,128)S(1)}, f32[704,128]{1,0:T(8,128)S(1)}, u32[]{:S(2)}, u32[]{:S(2)}) collective-permute-start(f32[704,128]{1,0:T(8,128)S(1)} %get-tuple-element.1086), channel_id=1, source_target_pairs={{0,7},{1,0},{2,1},{3,2},{4,3},{5,4},{6,5},{7,6},{8,15},{9,8},{10,9... | collective-permute-start | bytes 1081352 | tf_op jit(solution)/shard_map/ppermute | solution.py:762
  31.7 6.3 %collective-permute-start.76 = (f32[5,48,128]{2,1,0:T(8,128)S(1)}, f32[5,48,128]{2,1,0:T(8,128)S(1)}, u32[]{:S(2)}, u32[]{:S(2)}) collective-permute-start(f32[5,48,128]{2,1,0:T(8,128)S(1)} %get-tuple-element.1097), channel_id=1, source_target_pairs={{0,64},{1,65},{2,66},{3,67},{4,68},{5,69},{6,70},{7,71},{8,72},{9,... | collective-permute-start | bytes 368648 | tf_op jit(solution)/shard_map/ppermute | solution.py:765
  33.8 4.3 %copy-start.51 = (s32[1024]{0:T(1024)S(1)}, s32[1024]{0:T(1024)}, u32[]{:S(2)}) copy-start(s32[1024]{0:T(1024)} %fold.3) | copy-start | bytes 12292
  38.1 4.3 %collective-permute-start.62 = (f32[120,128]{1,0:T(8,128)S(1)}, f32[120,128]{1,0:T(8,128)S(1)}, u32[]{:S(2)}, u32[]{:S(2)}) collective-permute-start(f32[120,128]{1,0:T(8,128)S(1)} %get-tuple-element.969), channel_id=1, source_target_pairs={{0,8},{8,0},{1,9},{9,1},{2,10},{10,2},{3,11},{11,3},{4,12},{12,4},... | collective-permute-start | bytes 184328 | tf_op jit(solution)/shard_map/cond/branch_6_fun/ppermute | solution.py:759
  38.2 4.2 %collective-permute-start.63 = (f32[120,128]{1,0:T(8,128)S(1)}, f32[120,128]{1,0:T(8,128)S(1)}, u32[]{:S(2)}, u32[]{:S(2)}) collective-permute-start(f32[120,128]{1,0:T(8,128)S(1)} %get-tuple-element.970), channel_id=1, source_target_pairs={{8,16},{16,8},{9,17},{17,9},{10,18},{18,10},{11,19},{19,11},{12,20... | collective-permute-start | bytes 184328 | tf_op jit(solution)/shard_map/cond/branch_6_fun/ppermute | solution.py:759
  38.9 4.4 %collective-permute-start.65 = (f32[120,128]{1,0:T(8,128)S(1)}, f32[120,128]{1,0:T(8,128)S(1)}, u32[]{:S(2)}, u32[]{:S(2)}) collective-permute-start(f32[120,128]{1,0:T(8,128)S(1)} %get-tuple-element.974), channel_id=1, source_target_pairs={{120,125},{121,124},{122,123},{123,122},{124,121},{125,120},{126,1... | collective-permute-start | bytes 184328 | tf_op jit(solution)/shard_map/cond/branch_6_fun/ppermute | solution.py:836
  39.5 3.7 %collective-permute-start.64 = (f32[120,128]{1,0:T(8,128)S(1)}, f32[120,128]{1,0:T(8,128)S(1)}, u32[]{:S(2)}, u32[]{:S(2)}) collective-permute-start(f32[120,128]{1,0:T(8,128)S(1)} %get-tuple-element.974), channel_id=1, source_target_pairs={{120,126},{121,125},{122,124},{123,123},{124,122},{125,121},{126,1... | collective-permute-start | bytes 184328 | tf_op jit(solution)/shard_map/cond/branch_6_fun/ppermute | solution.py:836
  43.2 12.1 %collective-permute-start.66 = (f32[5,48,128]{2,1,0:T(8,128)S(1)}, f32[5,48,128]{2,1,0:T(8,128)S(1)}, u32[]{:S(2)}, u32[]{:S(2)}) collective-permute-start(f32[5,48,128]{2,1,0:T(8,128)S(1)} %get-tuple-element.975), channel_id=1, source_target_pairs={{0,64},{1,65},{2,66},{3,67},{4,68},{5,69},{6,70},{7,71},{8,72},{9,... | collective-permute-start | bytes 368648 | tf_op jit(solution)/shard_map/cond/branch_6_fun/ppermute | solution.py:765

commit v2 on v1

--- a/solution.py
+++ b/solution.py
@@ -223,35 +223,27 @@
     return [[None if q == 3 and a == 3 else read(q, a) for a in range(4)] for q in range(1, 4)]
 
 
-def own_first_kernel(lam_in, winds_in, inv_in, x_in, own, to_west, to_east, lam, winds, inv, x, sem):
+def own_kernel(
+    lam_in, winds_in, inv_in, x_in,
+    own, to_west, to_east, lam0, winds0, inv0, rest_own, rest_west, rest_east,
+    lam, winds, inv, x, first_sem, sem,
+):
     four = pl.ds(0, 4)
-    copy_all(
-        [
-            (inv_in.at[pl.ds(0, 1)], inv),
-            (winds_in.at[:, four], winds),
-            (lam_in.at[four], lam),
-            (x_in, x),
-        ],
-        sem,
-    )
-
-    def read(field, a):
-        return field_ref(lam, winds, inv, field, 0, a)[...]
-
-    slots = block_slots(read, [x[0, f] for f in range(4)])
-    slots += single_slots(lambda q, a: x[q, a])
-    pack_columns(slots, [(own, k) for k in range(12)], to_west, to_east, 0, ROWS)
-
-
-def own_rest_kernel(lam_in, winds_in, inv_in, own, to_west, to_east, lam, winds, inv, sem):
+    first = [(inv_in.at[pl.ds(0, 1)], inv0), (winds_in.at[:, four], winds0), (lam_in.at[four], lam0), (x_in, x)]
+    first = [pltpu.make_async_copy(a, b, first_sem.at[k]) for k, (a, b) in enumerate(first)]
+
     def fetch(n):
         levels = pl.ds(4 * n, 4)
         pairs = ((winds_in.at[:, levels], winds.at[:, levels]), (lam_in.at[levels], lam.at[levels]), (inv_in.at[n], inv.at[n]))
         return [pltpu.make_async_copy(a, b, sem.at[n - 1, k]) for k, (a, b) in enumerate(pairs)]
 
-    for n in range(1, BLOCKS):
-        for copy in fetch(n):
-            copy.start()
+    for copy in first + [copy for n in range(1, BLOCKS) for copy in fetch(n)]:
+        copy.start()
+    for copy in first:
+        copy.wait()
+    slots = block_slots(lambda field, a: field_ref(lam0, winds0, inv0, field, 0, a)[...], [x[0, f] for f in range(4)])
+    slots += single_slots(lambda q, a: x[q, a])
+    pack_columns(slots, [(own, k) for k in range(12)], to_west, to_east, 0, ROWS)
 
     def step(n, carry):
         for copy in fetch(n):
@@ -260,8 +252,8 @@
         def read(field, a):
             return field_ref(lam, winds, inv, field, n, a)[...]
 
-        strip_at = [(own, 8 * (n - 1) + k) for k in range(8)]
-        pack_columns(block_slots(read, None), strip_at, to_west, to_east, 2 * (n - 1), ROWS)
+        strip_at = [(rest_own, 8 * (n - 1) + k) for k in range(8)]
+        pack_columns(block_slots(read, None), strip_at, rest_west, rest_east, 2 * (n - 1), ROWS)
         return carry
 
     lax.fori_loop(1, BLOCKS, step, 0)
@@ -585,7 +577,7 @@
             edges[2, n - 1, a] = reverse(merged[a][24:32])
         return carry
 
-    lax.fori_loop(1, BLOCKS, block, 0)
+    lax.fori_loop(1, BLOCKS, block, 0, unroll=True)
     for n in range(REST):
         for a in range(5):
             at = 24 * a + 3 * n
@@ -677,8 +669,7 @@
 
 MICROSECONDS = {
     "start_rows_kernel": 3.2,
-    "own_first_kernel": 2.0,
-    "own_rest_kernel": 2.5,
+    "own_kernel": 4.0,
     "halo_kernel": 2.8,
     "first_kernel": 1.0,
     "rest_first_kernel": 4.3,
@@ -776,26 +767,22 @@
         half = lax.ppermute(high if in_late_half else low, AXES, fold_pairs(total - in_late_half, (0, 1)))
         folded = (whole, half)
         own = call(
-            own_first_kernel,
+            own_kernel,
             [vmem(12, ROWS), vmem(3 * ROWS), vmem(3 * ROWS)]
-            + [vmem(4, ROWS), vmem(2, 4, ROWS), vmem(1, 4, 4, ROWS)],
+            + [vmem(4, ROWS), vmem(2, 4, ROWS), vmem(1, 4, 4, ROWS)]
+            + [vmem(8 * REST, ROWS), vmem(2 * REST * ROWS), vmem(2 * REST * ROWS)],
             (lam, wind, inv, x),
             [HBM] * 4,
-            [pltpu.VMEM((4, 4, ROWS, COLS), F32), pltpu.SemaphoreType.DMA((4,))],
-        )
-        rest_own = call(
-            own_rest_kernel,
-            [vmem(8 * REST, ROWS), vmem(2 * REST * ROWS), vmem(2 * REST * ROWS)],
-            (lam, wind, inv),
-            [HBM] * 3,
             [
                 pltpu.VMEM((32, ROWS, COLS), F32),
                 pltpu.VMEM((2, 32, ROWS, COLS), F32),
                 pltpu.VMEM((BLOCKS, 4, 4, ROWS, COLS), F32),
+                pltpu.VMEM((4, 4, ROWS, COLS), F32),
+                pltpu.SemaphoreType.DMA((4,)),
                 pltpu.SemaphoreType.DMA((REST, 3)),
             ],
         )
-        return *folded, *own, *rest_own
+        return *folded, *own
 
     *folded, own, mid_west, mid_east, lam0, wind0, inv0, rest_own, rest_mid_west, rest_mid_east = lax.switch(
         half_turn[0], [functools.partial(across_fold, step) for step in range(2 * LON)], mirror, low, high, lam, wind, inv, x
@@ -835,10 +822,9 @@
     def finish(total, rest_rows, received, chain, rest_args):
         folded = [lax.ppermute(rest_rows[2], AXES, fold_pairs(total - k, (1,))) for k in range(2)]
         swapped = swap(*rest_rows[:2])
-        received, swapped = lax.optimization_barrier((received, swapped))
         x, hx, land, *tables, state = chain
         payload, state = call(second_kernel, [five, five], (x, hx, land, *tables, received, state), [VMEM] * 13)
-        payload, folded = lax.optimization_barrier((payload, folded))
+        payload, swapped, folded = lax.optimization_barrier((payload, swapped, folded))
         received = across(payload)
         (rest,) = call(
             rest_second_kernel,

time: 56.6 us -> 55.5 us (0.981); the launches traced: 56.5 us -> 54.5 us
  Pallas kernels: 23.9 us -> 22.4 us
  starting transfers between devices: 21.3 us -> 19.9 us
  waiting for transfers between devices: 9.4 us -> 10.3 us
    ppermute x1, waiting for transfers between devices: 2.08 us -> 3.85 us  [across_fold(): lax.ppermute(high if in_late_half else low, AXES, fold_pairs(total - in_l...]
    pallas_call x9 -> x8, Pallas kernels: 23.9 us -> 22.4 us  [call(): pl.pallas_call(kernel, out_shape=[jax.ShapeDtypeStruct(s, jnp.int32 if sp...]
    ppermute x2, starting transfers between devices: 8.47 us -> 7.31 us  [across(): lax.ppermute(value, AXES, [(i, (i + LAT * LON) % (2 * LAT * LON)) for i i...]
    ppermute x2, waiting for transfers between devices: 2.19 us -> 1.35 us  [swap(): lax.ppermute(first, AXES, swap_pairs(0))]
  transfers between devices with their start and end apart: 12 -> 12, of which waited for: 3 -> 3; matrix products, arithmetic and copies ran while one was open for 0% -> 0% of each run, Pallas kernels for 28% -> 25%
where the time goes in v2:
time: 55.5 us; the launch traced here: 54.5 us
  Pallas kernels  22.4 us (40%)
  starting transfers between devices  19.9 us (36%)
  waiting for transfers between devices  10.3 us (19%)
  between operations  1.49 us (3%)
    pallas_call x8, Pallas kernels, call(): pl.pallas_call(kernel, out_shape=[jax.ShapeDtypeStruct(s, jnp.int32 if sp...  22.4 us
    ppermute x2, starting transfers between devices, across(): lax.ppermute(value, AXES, [(i, (i + LAT * LON) % (2 * LAT * LON)) for i i...  7.31 us
    ppermute x1, waiting for transfers between devices, around(): lax.ppermute(to_east, AXES, lon_pairs(1))  5.1 us
    ppermute x1, starting transfers between devices, across_fold(): lax.ppermute(mirror, AXES, fold_pairs(total - 1 + in_late_half, (0, 1)))  3.91 us
    ppermute x1, waiting for transfers between devices, across_fold(): lax.ppermute(high if in_late_half else low, AXES, fold_pairs(total - in_l...  3.85 us
    ppermute x1, starting transfers between devices, around(): lax.ppermute(to_west, AXES, lon_pairs(-1))  2.94 us
    ppermute x1, starting transfers between devices, across_fold(): lax.ppermute(high if in_late_half else low, AXES, fold_pairs(total - in_l...  2.68 us
    ppermute x2, waiting for transfers between devices, swap(): lax.ppermute(first, AXES, swap_pairs(0))  1.35 us
  transfers between devices with their start and end apart: 12, of which 3 were waited for; matrix products, arithmetic and copies ran while one was open for 0% of the time, Pallas kernels for 25%

profile of v2, /device:TPU:112, one launch (start us, length us, event | category | flops | bytes accessed | tf_op | source)
XLA Modules:
  0.0 54.5 jit_solution(1389404974069265106)
XLA Ops:
  0.0 3.5 %shard_map.90 = (f32[4,4,32,128]{3,2,1,0:T(8,128)S(1)}, f32[464,128]{1,0:T(8,128)}, f32[464,128]{1,0:T(8,128)}, f32[464,128]{1,0:T(8,128)}, f32[232,128]{1,0:T(8...) custom-call(s32[1024]{0:T(1024)} %fold.3, f32[32,32,128]{2,1,0:T(8,128)} %bitcast.58, f32[2,32,32,128]{3,2,1,0:T(8,128)} %bitcast.40, ...), custom_call_target="tpu_custom_call" | custom-call | bytes 11200000 | tf_op jit(solution)/shard_map/pallas_call | solution.py:684
  3.5 0.3 collective-permute-start.72
  3.8 0.7 %collective-permute-start.73 = (f32[464,128]{1,0:T(8,128)}, f32[464,128]{1,0:T(8,128)S(1)}, u32[]{:S(2)}, u32[]{:S(2)}) collective-permute-start(f32[464,128]{1,0:T(8,128)} %get-tuple-element.1058), channel_id=1, source_target_pairs={{8,16},{16,8},{9,17},{17,9},{10,18},{18,10},{11,19},{19,11},{12,20... | collective-permute-start | bytes 712712 | tf_op jit(solution)/shard_map/ppermute | solution.py:750
  5.1 0.0 copy-start.3
  5.1 14.1 %conditional.2 = (f32[464,128]{1,0:T(8,128)}, f32[232,128]{1,0:T(8,128)}, f32[12,32,128]{2,1,0:T(8,128)S(1)}, f32[96,128]{1,0:T(8,128)S(1)}, f32[96,128]{1,0:T(8...) conditional(s32[]{:T(128)} %bitcast.13, ...), branch_computations={%region_0.0_spmd, %region_1.0_spmd, %region_2.0_spmd, %region_3.0_... | conditional | bytes 15425576 | solution.py:787
  5.1 3.9 %collective-permute-start.30 = (f32[464,128]{1,0:T(8,128)}, f32[464,128]{1,0:T(8,128)}, u32[]{:S(2)}, u32[]{:S(2)}) collective-permute-start(f32[464,128]{1,0:T(8,128)} %get-tuple-element.768), channel_id=1, source_target_pairs={{56,63},{57,62},{58,61},{59,60},{60,59},{61,58},{62,57},{63,56},{1... | collective-permute-start | bytes 712712 | tf_op jit(solution)/shard_map/cond/branch_15_fun/ppermute | solution.py:766
  9.0 2.7 %collective-permute-start.31 = (f32[232,128]{1,0:T(8,128)}, f32[232,128]{1,0:T(8,128)}, u32[]{:S(2)}, u32[]{:S(2)}) collective-permute-start(f32[232,128]{1,0:T(8,128)} %get-tuple-element.769), channel_id=1, source_target_pairs={{56,62},{57,61},{58,60},{59,59},{60,58},{61,57},{62,56},{63,63},{1... | collective-permute-start | bytes 356360 | tf_op jit(solution)/shard_map/cond/branch_15_fun/ppermute | solution.py:767
  11.7 3.6 %branch_15_fun.1 = (f32[12,32,128]{2,1,0:T(8,128)S(1)}, f32[96,128]{1,0:T(8,128)S(1)}, f32[96,128]{1,0:T(8,128)S(1)}, f32[4,32,128]{2,1,0:T(8,128)S(1)}, f32[2,4...) custom-call(f32[32,32,128]{2,1,0:T(8,128)S(1)} %get-tuple-element.77, ...), custom_call_target="tpu_custom_call" | custom-call | bytes 14000000 | tf_op jit(solution)/shard_map/cond/branch_15_fun/pallas_call | solution.py:684
  15.3 3.8 %collective-permute-done.31 = f32[232,128]{1,0:T(8,128)} collective-permute-done((f32[232,128]{1,0:T(8,128)}, f32[232,128]{1,0:T(8,128)}, u32[]{:S(2)}, u32[]{:S(2)}) %collective-permute-start.31) | collective-permute-done | bytes 118816 | tf_op jit(solution)/shard_map/cond/branch_15_fun/ppermute | solution.py:767
  19.2 0.0 collective-permute-done.30
  19.2 0.0 collective-permute-done.72.first_in
  19.2 0.0 collective-permute-done.73.second_in
  19.2 3.7 %shard_map.91 = (f32[7,4,16,128]{3,2,1,0:T(8,128)S(1)}, f32[4,4,16,128]{3,2,1,0:T(8,128)S(1)}, f32[12,16,128]{2,1,0:T(8,128)S(1)}, f32[7,3,4,16,128]{4,3,2,1,0:T...) custom-call(s32[1024]{0:T(1024)S(1)} %copy-done.3, ...), custom_call_target="tpu_custom_call" | custom-call | bytes 9800000 | tf_op jit(solution)/shard_map/pallas_call | solution.py:684
  22.9 0.0 collective-permute-start.74
  22.9 2.9 %collective-permute-start.75 = (f32[704,128]{1,0:T(8,128)S(1)}, f32[704,128]{1,0:T(8,128)S(1)}, u32[]{:S(2)}, u32[]{:S(2)}) collective-permute-start(f32[704,128]{1,0:T(8,128)S(1)} %get-tuple-element.1082), channel_id=1, source_target_pairs={{0,7},{1,0},{2,1},{3,2},{4,3},{5,4},{6,5},{7,6},{8,15},{9,8},{10,9... | collective-permute-start | bytes 1081352 | tf_op jit(solution)/shard_map/ppermute | solution.py:753
  25.9 5.1 %collective-permute-done.74.refs_6_ = f32[704,128]{1,0:T(8,128)S(1)} collective-permute-done((f32[704,128]{1,0:T(8,128)S(1)}, f32[704,128]{1,0:T(8,128)S(1)}, u32[]{:S(2)}, u32[]{:S(2)}) %collective-permute-start.74) | collective-permute-done | bytes 360480 | tf_op jit(solution)/shard_map/ppermute | solution.py:753
  31.0 0.9 %shard_map.92 = (f32[5,48,128]{2,1,0:T(8,128)S(1)}, f32[5,48,128]{2,1,0:T(8,128)S(1)}, f32[240,128]{1,0:T(8,128)S(1)}, f32[240,128]{1,0:T(8,128)S(1)}, f32[240,1...) custom-call(f32[4,32,128]{2,1,0:T(8,128)S(1)} %get-tuple-element.107, ...), custom_call_target="tpu_custom_call" | custom-call | bytes 3500000 | tf_op jit(solution)/shard_map/pallas_call | solution.py:684
  31.9 1.4 %collective-permute-start.76 = (f32[5,48,128]{2,1,0:T(8,128)S(1)}, f32[5,48,128]{2,1,0:T(8,128)S(1)}, u32[]{:S(2)}, u32[]{:S(2)}) collective-permute-start(f32[5,48,128]{2,1,0:T(8,128)S(1)} %get-tuple-element.1092), channel_id=1, source_target_pairs={{0,64},{1,65},{2,66},{3,67},{4,68},{5,69},{6,70},{7,71},{8,72},{9,... | collective-permute-start | bytes 368648 | tf_op jit(solution)/shard_map/ppermute | solution.py:756
  33.9 4.0 %shard_map.93 = (f32[7,5,32,128]{3,2,1,0:T(8,128)S(1)}, f32[7,3,240,128]{3,2,1,0:T(8,128)S(1)}, f32[7,4,32,128]{3,2,1,0:T(8,128)S(1)}, f32[120,128]{1,0:T(8,128)...) custom-call(f32[32,32,128]{2,1,0:T(8,128)S(1)} %bitcast.75, f32[2,32,32,128]{3,2,1,0:T(8,128)S(1)} %bitcast.57, ...), custom_call_target="tpu_custom_call" | custom-call | bytes 15050000 | tf_op jit(solution)/shard_map/pallas_call | solution.py:684
  37.9 0.0 collective-permute-done.76
  37.9 16.5 %conditional.3 = (f32[1,32,32,128]{3,2,1,0:T(8,128)}) conditional(s32[]{:T(128)} %bitcast.12, (f32[4,4,32,128]{3,2,1,0:T(8,128)S(1)}, f32[4,4,16,128]{3,2,1,0:T(8,128)S(1)}, f32[240,128]{1,0:T(8,128)S(1)}, f32[240,128]{1,0:T(8,128)S(1)}, f32[240,128]{1,0:T(8,128)S(1)}, /*index=5*/f32[240,128]{1,0:T(8,128)S(1)}, ...), branch_computations={%region_16.0_spmd, %region_17.0_spmd, %region_18.0_spmd, %region_1... | conditional | bytes 22824768 | solution.py:851
  38.2 0.1 collective-permute-start.67
  38.3 0.7 %collective-permute-start.68 = (f32[120,128]{1,0:T(8,128)S(1)}, f32[120,128]{1,0:T(8,128)S(1)}, u32[]{:S(2)}, u32[]{:S(2)}) collective-permute-start(f32[120,128]{1,0:T(8,128)S(1)} %get-tuple-element.994), channel_id=1, source_target_pairs={{8,16},{16,8},{9,17},{17,9},{10,18},{18,10},{11,19},{19,11},{12,20... | collective-permute-start | bytes 184328 | tf_op jit(solution)/shard_map/cond/branch_7_fun/ppermute | solution.py:750
  38.9 0.7 %collective-permute-start.70 = (f32[120,128]{1,0:T(8,128)S(1)}, f32[120,128]{1,0:T(8,128)S(1)}, u32[]{:S(2)}, u32[]{:S(2)}) collective-permute-start(f32[120,128]{1,0:T(8,128)S(1)} %get-tuple-element.995), channel_id=1, source_target_pairs={{120,126},{121,125},{122,124},{123,123},{124,122},{125,121},{126,1... | collective-permute-start | bytes 184328 | tf_op jit(solution)/shard_map/cond/branch_7_fun/ppermute | solution.py:823
  39.6 0.7 %collective-permute-start.69 = (f32[120,128]{1,0:T(8,128)S(1)}, f32[120,128]{1,0:T(8,128)S(1)}, u32[]{:S(2)}, u32[]{:S(2)}) collective-permute-start(f32[120,128]{1,0:T(8,128)S(1)} %get-tuple-element.995), channel_id=1, source_target_pairs={{120,127},{121,126},{122,125},{123,124},{124,123},{125,122},{126,1... | collective-permute-start | bytes 184328 | tf_op jit(solution)/shard_map/cond/branch_7_fun/ppermute | solution.py:823
  40.3 0.8 %branch_7_fun.5 = (f32[5,48,128]{2,1,0:T(8,128)S(1)}, f32[5,48,128]{2,1,0:T(8,128)S(1)}) custom-call(f32[4,4,32,128]{3,2,1,0:T(8,128)S(1)} %get-tuple-element.979.x_in, f32[4,4,16,128]{3,2,1,0:T(8,128)S(1)} %get-tuple-element.980.hx, f32[240,128]{1,0:T(8,128)S(1)} %get-tuple-element.981.land.refs_3_, f32[240,128]{1,0:T(8,128)S(1)} %get-tuple-element.984.to_south, ...), custom_call_target="tpu_custom_call" | custom-call | bytes 3500000 | tf_op jit(solution)/shard_map/cond/branch_7_fun/pallas_call | solution.py:684
  41.1 1.3 %collective-permute-done.67.refs_6_ = f32[120,128]{1,0:T(8,128)S(1)} collective-permute-done((f32[120,128]{1,0:T(8,128)S(1)}, f32[120,128]{1,0:T(8,128)S(1)}, u32[]{:S(2)}, u32[]{:S(2)}) %collective-permute-start.67) | collective-permute-done | bytes 61472 | tf_op jit(solution)/shard_map/cond/branch_7_fun/ppermute | solution.py:750
  42.5 0.0 collective-permute-done.68.refs_7_
  42.5 6.0 %collective-permute-start.71 = (f32[5,48,128]{2,1,0:T(8,128)S(1)}, f32[5,48,128]{2,1,0:T(8,128)S(1)}, u32[]{:S(2)}, u32[]{:S(2)}) collective-permute-start(f32[5,48,128]{2,1,0:T(8,128)S(1)} %get-tuple-element.996), channel_id=1, source_target_pairs={{0,64},{1,65},{2,66},{3,67},{4,68},{5,69},{6,70},{7,71},{8,72},{9,... | collective-permute-start | bytes 368648 | tf_op jit(solution)/shard_map/cond/branch_7_fun/ppermute | solution.py:756
  48.4 5.0 %branch_7_fun.6.rest = f32[32,32,128]{2,1,0:T(8,128)} custom-call(s32[1024]{0:T(1024)S(1)} %get-tuple-element.998.refs_0_, f32[8,4,4,32,128]{4,3,2,1,0:T(8,128)S(1)} %get-tuple-element.999.refs_1_, f32[7,4,32,128]{3,2,1,0:T(8,128)S(1)} %get-tuple-element.1000.refs_2_, f32[240,128]{1,0:T(8,128)S(1)} %get-tuple-element.981.land.refs_3_, ...), custom_call_target="tpu_custom_call" | custom-call | bytes 16099999 | tf_op jit(solution)/shard_map/cond/branch_7_fun/pallas_call | solution.py:684
  53.4 0.0 collective-permute-done.71.received
  53.4 0.9 %branch_7_fun.7 = f32[32,32,128]{2,1,0:T(8,128)} custom-call(f32[4,4,32,128]{3,2,1,0:T(8,128)S(1)} %get-tuple-element.979.x_in, f32[4,4,16,128]{3,2,1,0:T(8,128)S(1)} %get-tuple-element.980.hx, f32[240,128]{1,0:T(8,128)S(1)} %get-tuple-element.981.land.refs_3_, f32[4,48,128]{2,1,0:T(8,128)S(1)} %get-tuple-element.982.strip_coefs, ...), custom_call_target="tpu_custom_call", output_to_operand_aliasing={{}: (7, {})} | custom-call | bytes 1750000 | tf_op jit(solution)/shard_map/cond/branch_7_fun/pallas_call | solution.py:684
  (10 shorter events, 0.0 us)
Async XLA Ops:
  0.0 5.0 %copy-start.2 = (f32[1,32,32,128]{3,2,1,0:T(8,128)S(1)}, f32[1,32,32,128]{3,2,1,0:T(8,128)}, u32[]{:S(2)}) copy-start(f32[1,32,32,128]{3,2,1,0:T(8,128)} %param.32) | copy-start | bytes 1572868
  3.5 15.7 %collective-permute-start.72 = (f32[464,128]{1,0:T(8,128)}, f32[464,128]{1,0:T(8,128)S(1)}, u32[]{:S(2)}, u32[]{:S(2)}) collective-permute-start(f32[464,128]{1,0:T(8,128)} %get-tuple-element.1057), channel_id=1, source_target_pairs={{0,8},{8,0},{1,9},{9,1},{2,10},{10,2},{3,11},{11,3},{4,12},{12,4},... | collective-permute-start | bytes 712712 | tf_op jit(solution)/shard_map/ppermute | solution.py:750
  3.8 15.4 %collective-permute-start.73 = (f32[464,128]{1,0:T(8,128)}, f32[464,128]{1,0:T(8,128)S(1)}, u32[]{:S(2)}, u32[]{:S(2)}) collective-permute-start(f32[464,128]{1,0:T(8,128)} %get-tuple-element.1058), channel_id=1, source_target_pairs={{8,16},{16,8},{9,17},{17,9},{10,18},{18,10},{11,19},{19,11},{12,20... | collective-permute-start | bytes 712712 | tf_op jit(solution)/shard_map/ppermute | solution.py:750
  5.1 14.2 %copy-start.3 = (s32[1024]{0:T(1024)S(1)}, s32[1024]{0:T(1024)}, u32[]{:S(2)}) copy-start(s32[1024]{0:T(1024)} %fold.3) | copy-start | bytes 12292
  5.1 14.0 %collective-permute-start.30 = (f32[464,128]{1,0:T(8,128)}, f32[464,128]{1,0:T(8,128)}, u32[]{:S(2)}, u32[]{:S(2)}) collective-permute-start(f32[464,128]{1,0:T(8,128)} %get-tuple-element.768), channel_id=1, source_target_pairs={{56,63},{57,62},{58,61},{59,60},{60,59},{61,58},{62,57},{63,56},{1... | collective-permute-start | bytes 712712 | tf_op jit(solution)/shard_map/cond/branch_15_fun/ppermute | solution.py:766
  9.0 10.1 %collective-permute-start.31 = (f32[232,128]{1,0:T(8,128)}, f32[232,128]{1,0:T(8,128)}, u32[]{:S(2)}, u32[]{:S(2)}) collective-permute-start(f32[232,128]{1,0:T(8,128)} %get-tuple-element.769), channel_id=1, source_target_pairs={{56,62},{57,61},{58,60},{59,59},{60,58},{61,57},{62,56},{63,63},{1... | collective-permute-start | bytes 356360 | tf_op jit(solution)/shard_map/cond/branch_15_fun/ppermute | solution.py:767
  19.2 14.7 %copy-start = (f32[1,8,4,4,32,128]{5,4,3,2,1,0:T(8,128)S(1)}, f32[1,8,4,4,32,128]{5,4,3,2,1,0:T(8,128)}, u32[]{:S(2)}) copy-start(f32[1,8,4,4,32,128]{5,4,3,2,1,0:T(8,128)} %param.34) | copy-start | bytes 6291460
  19.2 14.7 %copy-start.1 = (f32[2,1,32,32,128]{4,3,2,1,0:T(8,128)S(1)}, f32[2,1,32,32,128]{4,3,2,1,0:T(8,128)}, u32[]{:S(2)}) copy-start(f32[2,1,32,32,128]{4,3,2,1,0:T(8,128)} %param.33) | copy-start | bytes 3145732
  22.9 8.1 %collective-permute-start.74 = (f32[704,128]{1,0:T(8,128)S(1)}, f32[704,128]{1,0:T(8,128)S(1)}, u32[]{:S(2)}, u32[]{:S(2)}) collective-permute-start(f32[704,128]{1,0:T(8,128)S(1)} %get-tuple-element.1081), channel_id=1, source_target_pairs={{0,1},{1,2},{2,3},{3,4},{4,5},{5,6},{6,7},{7,0},{8,9},{9,10},{10,1... | collective-permute-start | bytes 1081352 | tf_op jit(solution)/shard_map/ppermute | solution.py:753
  22.9 8.1 %collective-permute-start.75 = (f32[704,128]{1,0:T(8,128)S(1)}, f32[704,128]{1,0:T(8,128)S(1)}, u32[]{:S(2)}, u32[]{:S(2)}) collective-permute-start(f32[704,128]{1,0:T(8,128)S(1)} %get-tuple-element.1082), channel_id=1, source_target_pairs={{0,7},{1,0},{2,1},{3,2},{4,3},{5,4},{6,5},{7,6},{8,15},{9,8},{10,9... | collective-permute-start | bytes 1081352 | tf_op jit(solution)/shard_map/ppermute | solution.py:753
  31.9 6.0 %collective-permute-start.76 = (f32[5,48,128]{2,1,0:T(8,128)S(1)}, f32[5,48,128]{2,1,0:T(8,128)S(1)}, u32[]{:S(2)}, u32[]{:S(2)}) collective-permute-start(f32[5,48,128]{2,1,0:T(8,128)S(1)} %get-tuple-element.1092), channel_id=1, source_target_pairs={{0,64},{1,65},{2,66},{3,67},{4,68},{5,69},{6,70},{7,71},{8,72},{9,... | collective-permute-start | bytes 368648 | tf_op jit(solution)/shard_map/ppermute | solution.py:756
  38.2 4.3 %collective-permute-start.67 = (f32[120,128]{1,0:T(8,128)S(1)}, f32[120,128]{1,0:T(8,128)S(1)}, u32[]{:S(2)}, u32[]{:S(2)}) collective-permute-start(f32[120,128]{1,0:T(8,128)S(1)} %get-tuple-element.993), channel_id=1, source_target_pairs={{0,8},{8,0},{1,9},{9,1},{2,10},{10,2},{3,11},{11,3},{4,12},{12,4},... | collective-permute-start | bytes 184328 | tf_op jit(solution)/shard_map/cond/branch_7_fun/ppermute | solution.py:750
  38.3 4.2 %collective-permute-start.68 = (f32[120,128]{1,0:T(8,128)S(1)}, f32[120,128]{1,0:T(8,128)S(1)}, u32[]{:S(2)}, u32[]{:S(2)}) collective-permute-start(f32[120,128]{1,0:T(8,128)S(1)} %get-tuple-element.994), channel_id=1, source_target_pairs={{8,16},{16,8},{9,17},{17,9},{10,18},{18,10},{11,19},{19,11},{12,20... | collective-permute-start | bytes 184328 | tf_op jit(solution)/shard_map/cond/branch_7_fun/ppermute | solution.py:750
  38.9 3.5 %collective-permute-start.70 = (f32[120,128]{1,0:T(8,128)S(1)}, f32[120,128]{1,0:T(8,128)S(1)}, u32[]{:S(2)}, u32[]{:S(2)}) collective-permute-start(f32[120,128]{1,0:T(8,128)S(1)} %get-tuple-element.995), channel_id=1, source_target_pairs={{120,126},{121,125},{122,124},{123,123},{124,122},{125,121},{126,1... | collective-permute-start | bytes 184328 | tf_op jit(solution)/shard_map/cond/branch_7_fun/ppermute | solution.py:823
  39.6 2.9 %collective-permute-start.69 = (f32[120,128]{1,0:T(8,128)S(1)}, f32[120,128]{1,0:T(8,128)S(1)}, u32[]{:S(2)}, u32[]{:S(2)}) collective-permute-start(f32[120,128]{1,0:T(8,128)S(1)} %get-tuple-element.995), channel_id=1, source_target_pairs={{120,127},{121,126},{122,125},{123,124},{124,123},{125,122},{126,1... | collective-permute-start | bytes 184328 | tf_op jit(solution)/shard_map/cond/branch_7_fun/ppermute | solution.py:823
  42.5 10.9 %collective-permute-start.71 = (f32[5,48,128]{2,1,0:T(8,128)S(1)}, f32[5,48,128]{2,1,0:T(8,128)S(1)}, u32[]{:S(2)}, u32[]{:S(2)}) collective-permute-start(f32[5,48,128]{2,1,0:T(8,128)S(1)} %get-tuple-element.996), channel_id=1, source_target_pairs={{0,64},{1,65},{2,66},{3,67},{4,68},{5,69},{6,70},{7,71},{8,72},{9,... | collective-permute-start | bytes 368648 | tf_op jit(solution)/shard_map/cond/branch_7_fun/ppermute | solution.py:756

commit v3 on v2

--- a/solution.py
+++ b/solution.py
@@ -296,15 +296,12 @@
     fold, first_in, second_in, fold_whole, fold_half, mid_west, mid_east, rest_west, rest_east, *refs,
 ):
     brought_in, (h, hx, own, rest_h, rest_own, to_west, to_east), refs = refs[:BROUGHT], refs[BROUGHT : BROUGHT + 7], refs[BROUGHT + 7 :]
-    brought, (south, north, sem) = refs[:BROUGHT], refs[BROUGHT:]
-    mids = (ROWS * 3, ROWS * 2 * REST)
-    pairs = [(rest_west, to_west.at[pl.ds(COL_OWN + mids[0], mids[1])])]
-    pairs += [(rest_east, to_east.at[pl.ds(COL_OWN + mids[0], mids[1])])]
-    pairs += [(mid_west, to_west.at[pl.ds(COL_OWN, mids[0])]), (mid_east, to_east.at[pl.ds(COL_OWN, mids[0])])]
-    pairs += list(zip(brought_in, brought, strict=True))
-    copies = [pltpu.make_async_copy(a, b, sem.at[k]) for k, (a, b) in enumerate(pairs)]
-    for copy in copies:
-        copy.start()
+    brought, (south, north) = refs[:BROUGHT], refs[BROUGHT:]
+    for out, mid, rest_mid in ((to_west, mid_west, rest_west), (to_east, mid_east, rest_east)):
+        out[COL_OWN : COL_OWN + 3 * ROWS, :] = mid[...]
+        out[COL_OWN + 3 * ROWS : COL_BUFFER, :] = rest_mid[...]
+    for source, target in zip(brought_in, brought, strict=True):
+        target[...] = source[...]
 
     def beyond_fold():
         turn, lane = fold[0] % COLS, lanes()
@@ -334,8 +331,6 @@
         slots += [[rest_h[n, field, a] for a in range(4)] for field in range(3)] + [None]
         strip_at += [(rest_own, 3 * n + k) for k in range(3)] + [None]
     pack_columns(slots, strip_at, to_west, to_east, 0, 16)
-    for copy in copies:
-        copy.wait()
 
 
 BROUGHT = 5
@@ -623,6 +618,9 @@
             halo[n, a, 5:8, :] = south[at : at + 3, :]
             halo[n, a, 8:11, :] = north[at : at + 3, :]
 
+    def leave(n):
+        return pltpu.make_async_copy(result.at[pl.ds(4 * (n - 1), 4)], out.at[pl.ds(4 * n, 4)], sem.at[n - 1])
+
     def block(n, carry):
         mine = tuple(coefs.at[n - 1, k] for k in range(3))
         parts = []
@@ -633,10 +631,12 @@
         solved = solve(lambda a, b: inv[n, a, b], lambda d: strip_inverse[n - 1, d], own_rows(tracer))
         for a in range(4):
             result[4 * (n - 1) + a] = main_from_strip(solved[a], solved[4], a, 3)
+        leave(n).start()
         return carry
 
     lax.fori_loop(1, BLOCKS, block, 0)
-    copy_all([(result, out.at[pl.ds(4, 4 * REST)])], sem)
+    for n in range(1, BLOCKS):
+        leave(n).wait()
 
 
 def second_kernel(
@@ -795,8 +795,8 @@
         + [vmem(COL_BUFFER)] * 2
         + [(value.shape, VMEM) for value in brought],
         (fold_map, *moved, mid_west, mid_east, rest_mid_west, rest_mid_east, *brought),
-        [SMEM] + [VMEM] * 4 + [HBM] * (4 + BROUGHT),
-        [pltpu.VMEM((ROW_BUFFER, COLS), F32)] * 2 + [pltpu.SemaphoreType.DMA((4 + BROUGHT,))],
+        [SMEM] + [VMEM] * (8 + BROUGHT),
+        [pltpu.VMEM((ROW_BUFFER, COLS), F32)] * 2,
     )
     from_sides = around(to_west, to_east)
     five = vmem(5, EXT)
@@ -836,7 +836,7 @@
                 pltpu.VMEM((120, COLS), F32),
                 pltpu.VMEM((120, COLS), F32),
                 pltpu.VMEM((REST, 5, 16, COLS), F32),
-                done,
+                pltpu.SemaphoreType.DMA((REST,)),
             ],
         )
         return call(

time: 55.5 us -> 52.6 us (0.948)
  Pallas kernels: 22.4 us -> 20.7 us
  starting transfers between devices: 19.9 us -> 18.9 us
    pallas_call x8, Pallas kernels: 22.4 us -> 20.7 us  [call(): pl.pallas_call(kernel, out_shape=[jax.ShapeDtypeStruct(s, jnp.int32 if sp...]
    ppermute x1, starting transfers between devices: 3.91 us -> 2.64 us  [across_fold(): lax.ppermute(mirror, AXES, fold_pairs(total - 1 + in_late_half, (0, 1)))]
  transfers between devices with their start and end apart: 12 -> 12, of which waited for: 3 -> 3; matrix products, arithmetic and copies ran while one was open for 0% -> 0% of each run, Pallas kernels for 25% -> 26%
where the time goes in v3:
time: 52.6 us; the launch traced here: 51.8 us
  Pallas kernels  20.7 us (39%)
  starting transfers between devices  18.9 us (36%)
  waiting for transfers between devices  10.4 us (20%)
  between operations  1.48 us (3%)
    pallas_call x8, Pallas kernels, call(): pl.pallas_call(kernel, out_shape=[jax.ShapeDtypeStruct(s, jnp.int32 if sp...  20.7 us
    ppermute x2, starting transfers between devices, across(): lax.ppermute(value, AXES, [(i, (i + LAT * LON) % (2 * LAT * LON)) for i i...  7.53 us
    ppermute x1, waiting for transfers between devices, around(): lax.ppermute(to_east, AXES, lon_pairs(1))  5.1 us
    ppermute x1, waiting for transfers between devices, across_fold(): lax.ppermute(high if in_late_half else low, AXES, fold_pairs(total - in_l...  3.9 us
    ppermute x1, starting transfers between devices, around(): lax.ppermute(to_west, AXES, lon_pairs(-1))  2.94 us
    ppermute x1, starting transfers between devices, across_fold(): lax.ppermute(high if in_late_half else low, AXES, fold_pairs(total - in_l...  2.68 us
    ppermute x1, starting transfers between devices, across_fold(): lax.ppermute(mirror, AXES, fold_pairs(total - 1 + in_late_half, (0, 1)))  2.64 us
    ppermute x2, waiting for transfers between devices, swap(): lax.ppermute(first, AXES, swap_pairs(0))  1.35 us
  transfers between devices with their start and end apart: 12, of which 3 were waited for; matrix products, arithmetic and copies ran while one was open for 0% of the time, Pallas kernels for 26%

profile of v3, /device:TPU:112, one launch (start us, length us, event | category | flops | bytes accessed | tf_op | source)
XLA Modules:
  0.0 51.8 jit_solution(10080313576958734495)
XLA Ops:
  0.0 3.5 %shard_map.90 = (f32[4,4,32,128]{3,2,1,0:T(8,128)S(1)}, f32[464,128]{1,0:T(8,128)}, f32[464,128]{1,0:T(8,128)}, f32[464,128]{1,0:T(8,128)}, f32[232,128]{1,0:T(8...) custom-call(s32[1024]{0:T(1024)} %fold.3, f32[32,32,128]{2,1,0:T(8,128)} %bitcast.58, f32[2,32,32,128]{3,2,1,0:T(8,128)} %bitcast.40, ...), custom_call_target="tpu_custom_call" | custom-call | bytes 11200000 | tf_op jit(solution)/shard_map/pallas_call | solution.py:684
  3.5 0.3 collective-permute-start.72
  3.8 0.7 %collective-permute-start.73 = (f32[464,128]{1,0:T(8,128)}, f32[464,128]{1,0:T(8,128)S(1)}, u32[]{:S(2)}, u32[]{:S(2)}) collective-permute-start(f32[464,128]{1,0:T(8,128)} %get-tuple-element.1058), channel_id=1, source_target_pairs={{8,16},{16,8},{9,17},{17,9},{10,18},{18,10},{11,19},{19,11},{12,20... | collective-permute-start | bytes 712712 | tf_op jit(solution)/shard_map/ppermute | solution.py:750
  5.1 0.0 copy-start.3
  5.1 12.9 %conditional.2 = (f32[464,128]{1,0:T(8,128)}, f32[232,128]{1,0:T(8,128)}, f32[12,32,128]{2,1,0:T(8,128)S(1)}, f32[96,128]{1,0:T(8,128)S(1)}, f32[96,128]{1,0:T(8...) conditional(s32[]{:T(128)} %bitcast.13, ...), branch_computations={%region_0.0_spmd, %region_1.0_spmd, %region_2.0_spmd, %region_3.0_... | conditional | bytes 15425576 | solution.py:787
  5.1 2.6 %collective-permute-start.14 = (f32[464,128]{1,0:T(8,128)}, f32[464,128]{1,0:T(8,128)}, u32[]{:S(2)}, u32[]{:S(2)}) collective-permute-start(f32[464,128]{1,0:T(8,128)} %get-tuple-element.648), channel_id=1, source_target_pairs={{56,59},{57,58},{58,57},{59,56},{60,63},{61,62},{62,61},{63,60},{1... | collective-permute-start | bytes 712712 | tf_op jit(solution)/shard_map/cond/branch_7_fun/ppermute | solution.py:766
  7.8 2.7 %collective-permute-start.15 = (f32[232,128]{1,0:T(8,128)}, f32[232,128]{1,0:T(8,128)}, u32[]{:S(2)}, u32[]{:S(2)}) collective-permute-start(f32[232,128]{1,0:T(8,128)} %get-tuple-element.649), channel_id=1, source_target_pairs={{56,58},{57,57},{58,56},{59,63},{60,62},{61,61},{62,60},{63,59},{1... | collective-permute-start | bytes 356360 | tf_op jit(solution)/shard_map/cond/branch_7_fun/ppermute | solution.py:767
  10.5 3.6 %branch_7_fun.4 = (f32[12,32,128]{2,1,0:T(8,128)S(1)}, f32[96,128]{1,0:T(8,128)S(1)}, f32[96,128]{1,0:T(8,128)S(1)}, f32[4,32,128]{2,1,0:T(8,128)S(1)}, f32[2,4,...) custom-call(f32[32,32,128]{2,1,0:T(8,128)S(1)} %get-tuple-element.65, ...), custom_call_target="tpu_custom_call" | custom-call | bytes 14000000 | tf_op jit(solution)/shard_map/cond/branch_7_fun/pallas_call | solution.py:684
  14.1 3.9 %collective-permute-done.15 = f32[232,128]{1,0:T(8,128)} collective-permute-done((f32[232,128]{1,0:T(8,128)}, f32[232,128]{1,0:T(8,128)}, u32[]{:S(2)}, u32[]{:S(2)}) %collective-permute-start.15) | collective-permute-done | bytes 118816 | tf_op jit(solution)/shard_map/cond/branch_7_fun/ppermute | solution.py:767
  18.0 0.0 collective-permute-done.14
  18.0 0.0 collective-permute-done.72.first_in
  18.0 0.0 collective-permute-done.73.second_in
  18.0 2.1 %shard_map.91 = (f32[7,4,16,128]{3,2,1,0:T(8,128)S(1)}, f32[4,4,16,128]{3,2,1,0:T(8,128)S(1)}, f32[12,16,128]{2,1,0:T(8,128)S(1)}, f32[7,3,4,16,128]{4,3,2,1,0:T...) custom-call(s32[1024]{0:T(1024)S(1)} %copy-done.3, ...), custom_call_target="tpu_custom_call" | custom-call | bytes 9800000 | tf_op jit(solution)/shard_map/pallas_call | solution.py:684
  20.1 0.0 collective-permute-start.74
  20.1 2.9 %collective-permute-start.75 = (f32[704,128]{1,0:T(8,128)S(1)}, f32[704,128]{1,0:T(8,128)S(1)}, u32[]{:S(2)}, u32[]{:S(2)}) collective-permute-start(f32[704,128]{1,0:T(8,128)S(1)} %get-tuple-element.1082), channel_id=1, source_target_pairs={{0,7},{1,0},{2,1},{3,2},{4,3},{5,4},{6,5},{7,6},{8,15},{9,8},{10,9... | collective-permute-start | bytes 1081352 | tf_op jit(solution)/shard_map/ppermute | solution.py:753
  23.0 5.1 %collective-permute-done.74.refs_6_ = f32[704,128]{1,0:T(8,128)S(1)} collective-permute-done((f32[704,128]{1,0:T(8,128)S(1)}, f32[704,128]{1,0:T(8,128)S(1)}, u32[]{:S(2)}, u32[]{:S(2)}) %collective-permute-start.74) | collective-permute-done | bytes 360480 | tf_op jit(solution)/shard_map/ppermute | solution.py:753
  28.1 0.9 %shard_map.92 = (f32[5,48,128]{2,1,0:T(8,128)S(1)}, f32[5,48,128]{2,1,0:T(8,128)S(1)}, f32[240,128]{1,0:T(8,128)S(1)}, f32[240,128]{1,0:T(8,128)S(1)}, f32[240,1...) custom-call(f32[4,32,128]{2,1,0:T(8,128)S(1)} %get-tuple-element.107, ...), custom_call_target="tpu_custom_call" | custom-call | bytes 3500000 | tf_op jit(solution)/shard_map/pallas_call | solution.py:684
  29.0 1.4 %collective-permute-start.76 = (f32[5,48,128]{2,1,0:T(8,128)S(1)}, f32[5,48,128]{2,1,0:T(8,128)S(1)}, u32[]{:S(2)}, u32[]{:S(2)}) collective-permute-start(f32[5,48,128]{2,1,0:T(8,128)S(1)} %get-tuple-element.1092), channel_id=1, source_target_pairs={{0,64},{1,65},{2,66},{3,67},{4,68},{5,69},{6,70},{7,71},{8,72},{9,... | collective-permute-start | bytes 368648 | tf_op jit(solution)/shard_map/ppermute | solution.py:756
  31.1 4.0 %shard_map.93 = (f32[7,5,32,128]{3,2,1,0:T(8,128)S(1)}, f32[7,3,240,128]{3,2,1,0:T(8,128)S(1)}, f32[7,4,32,128]{3,2,1,0:T(8,128)S(1)}, f32[120,128]{1,0:T(8,128)...) custom-call(f32[32,32,128]{2,1,0:T(8,128)S(1)} %bitcast.75, f32[2,32,32,128]{3,2,1,0:T(8,128)S(1)} %bitcast.57, ...), custom_call_target="tpu_custom_call" | custom-call | bytes 15050000 | tf_op jit(solution)/shard_map/pallas_call | solution.py:684
  35.0 0.0 collective-permute-done.76
  35.0 16.6 %conditional.3 = (f32[1,32,32,128]{3,2,1,0:T(8,128)}) conditional(s32[]{:T(128)} %bitcast.12, (f32[4,4,32,128]{3,2,1,0:T(8,128)S(1)}, f32[4,4,16,128]{3,2,1,0:T(8,128)S(1)}, f32[240,128]{1,0:T(8,128)S(1)}, f32[240,128]{1,0:T(8,128)S(1)}, f32[240,128]{1,0:T(8,128)S(1)}, /*index=5*/f32[240,128]{1,0:T(8,128)S(1)}, ...), branch_computations={%region_16.0_spmd, %region_17.0_spmd, %region_18.0_spmd, %region_1... | conditional | bytes 22824768 | solution.py:851
  35.1 0.1 collective-permute-start.47
  35.2 0.7 %collective-permute-start.48 = (f32[120,128]{1,0:T(8,128)S(1)}, f32[120,128]{1,0:T(8,128)S(1)}, u32[]{:S(2)}, u32[]{:S(2)}) collective-permute-start(f32[120,128]{1,0:T(8,128)S(1)} %get-tuple-element.882), channel_id=1, source_target_pairs={{8,16},{16,8},{9,17},{17,9},{10,18},{18,10},{11,19},{19,11},{12,20... | collective-permute-start | bytes 184328 | tf_op jit(solution)/shard_map/cond/branch_3_fun/ppermute | solution.py:750
  35.8 0.7 %collective-permute-start.50 = (f32[120,128]{1,0:T(8,128)S(1)}, f32[120,128]{1,0:T(8,128)S(1)}, u32[]{:S(2)}, u32[]{:S(2)}) collective-permute-start(f32[120,128]{1,0:T(8,128)S(1)} %get-tuple-element.883), channel_id=1, source_target_pairs={{120,122},{121,121},{122,120},{123,127},{124,126},{125,125},{126,1... | collective-permute-start | bytes 184328 | tf_op jit(solution)/shard_map/cond/branch_3_fun/ppermute | solution.py:823
  36.5 0.7 %collective-permute-start.49 = (f32[120,128]{1,0:T(8,128)S(1)}, f32[120,128]{1,0:T(8,128)S(1)}, u32[]{:S(2)}, u32[]{:S(2)}) collective-permute-start(f32[120,128]{1,0:T(8,128)S(1)} %get-tuple-element.883), channel_id=1, source_target_pairs={{120,123},{121,122},{122,121},{123,120},{124,127},{125,126},{126,1... | collective-permute-start | bytes 184328 | tf_op jit(solution)/shard_map/cond/branch_3_fun/ppermute | solution.py:823
  37.2 0.8 %branch_3_fun.5 = (f32[5,48,128]{2,1,0:T(8,128)S(1)}, f32[5,48,128]{2,1,0:T(8,128)S(1)}) custom-call(f32[4,4,32,128]{3,2,1,0:T(8,128)S(1)} %get-tuple-element.867.x_in, f32[4,4,16,128]{3,2,1,0:T(8,128)S(1)} %get-tuple-element.868.hx, f32[240,128]{1,0:T(8,128)S(1)} %get-tuple-element.869.land.refs_3_, f32[240,128]{1,0:T(8,128)S(1)} %get-tuple-element.872.to_south, ...), custom_call_target="tpu_custom_call" | custom-call | bytes 3500000 | tf_op jit(solution)/shard_map/cond/branch_3_fun/pallas_call | solution.py:684
  38.0 1.3 %collective-permute-done.47.refs_6_ = f32[120,128]{1,0:T(8,128)S(1)} collective-permute-done((f32[120,128]{1,0:T(8,128)S(1)}, f32[120,128]{1,0:T(8,128)S(1)}, u32[]{:S(2)}, u32[]{:S(2)}) %collective-permute-start.47) | collective-permute-done | bytes 61472 | tf_op jit(solution)/shard_map/cond/branch_3_fun/ppermute | solution.py:750
  39.4 0.0 collective-permute-done.48.refs_7_
  39.4 0.0 collective-permute-done.50.refs_9_
  39.4 6.2 %collective-permute-start.51 = (f32[5,48,128]{2,1,0:T(8,128)S(1)}, f32[5,48,128]{2,1,0:T(8,128)S(1)}, u32[]{:S(2)}, u32[]{:S(2)}) collective-permute-start(f32[5,48,128]{2,1,0:T(8,128)S(1)} %get-tuple-element.884), channel_id=1, source_target_pairs={{0,64},{1,65},{2,66},{3,67},{4,68},{5,69},{6,70},{7,71},{8,72},{9,... | collective-permute-start | bytes 368648 | tf_op jit(solution)/shard_map/cond/branch_3_fun/ppermute | solution.py:756
  45.6 4.9 %branch_3_fun.6.rest = f32[32,32,128]{2,1,0:T(8,128)} custom-call(s32[1024]{0:T(1024)S(1)} %get-tuple-element.886.refs_0_, f32[8,4,4,32,128]{4,3,2,1,0:T(8,128)S(1)} %get-tuple-element.887.refs_1_, f32[7,4,32,128]{3,2,1,0:T(8,128)S(1)} %get-tuple-element.888.refs_2_, f32[240,128]{1,0:T(8,128)S(1)} %get-tuple-element.869.land.refs_3_, ...), custom_call_target="tpu_custom_call" | custom-call | bytes 16099999 | tf_op jit(solution)/shard_map/cond/branch_3_fun/pallas_call | solution.py:684
  50.5 0.9 %branch_3_fun.7 = f32[32,32,128]{2,1,0:T(8,128)} custom-call(f32[4,4,32,128]{3,2,1,0:T(8,128)S(1)} %get-tuple-element.867.x_in, f32[4,4,16,128]{3,2,1,0:T(8,128)S(1)} %get-tuple-element.868.hx, f32[240,128]{1,0:T(8,128)S(1)} %get-tuple-element.869.land.refs_3_, f32[4,48,128]{2,1,0:T(8,128)S(1)} %get-tuple-element.870.strip_coefs, ...), custom_call_target="tpu_custom_call", output_to_operand_aliasing={{}: (7, {})} | custom-call | bytes 1750000 | tf_op jit(solution)/shard_map/cond/branch_3_fun/pallas_call | solution.py:684
  (10 shorter events, 0.0 us)
Async XLA Ops:
  0.0 5.0 %copy-start.2 = (f32[1,32,32,128]{3,2,1,0:T(8,128)S(1)}, f32[1,32,32,128]{3,2,1,0:T(8,128)}, u32[]{:S(2)}) copy-start(f32[1,32,32,128]{3,2,1,0:T(8,128)} %param.32) | copy-start | bytes 1572868
  3.5 14.4 %collective-permute-start.72 = (f32[464,128]{1,0:T(8,128)}, f32[464,128]{1,0:T(8,128)S(1)}, u32[]{:S(2)}, u32[]{:S(2)}) collective-permute-start(f32[464,128]{1,0:T(8,128)} %get-tuple-element.1057), channel_id=1, source_target_pairs={{0,8},{8,0},{1,9},{9,1},{2,10},{10,2},{3,11},{11,3},{4,12},{12,4},... | collective-permute-start | bytes 712712 | tf_op jit(solution)/shard_map/ppermute | solution.py:750
  3.8 14.2 %collective-permute-start.73 = (f32[464,128]{1,0:T(8,128)}, f32[464,128]{1,0:T(8,128)S(1)}, u32[]{:S(2)}, u32[]{:S(2)}) collective-permute-start(f32[464,128]{1,0:T(8,128)} %get-tuple-element.1058), channel_id=1, source_target_pairs={{8,16},{16,8},{9,17},{17,9},{10,18},{18,10},{11,19},{19,11},{12,20... | collective-permute-start | bytes 712712 | tf_op jit(solution)/shard_map/ppermute | solution.py:750
  5.1 12.9 %copy-start.3 = (s32[1024]{0:T(1024)S(1)}, s32[1024]{0:T(1024)}, u32[]{:S(2)}) copy-start(s32[1024]{0:T(1024)} %fold.3) | copy-start | bytes 12292
  5.1 12.8 %collective-permute-start.14 = (f32[464,128]{1,0:T(8,128)}, f32[464,128]{1,0:T(8,128)}, u32[]{:S(2)}, u32[]{:S(2)}) collective-permute-start(f32[464,128]{1,0:T(8,128)} %get-tuple-element.648), channel_id=1, source_target_pairs={{56,59},{57,58},{58,57},{59,56},{60,63},{61,62},{62,61},{63,60},{1... | collective-permute-start | bytes 712712 | tf_op jit(solution)/shard_map/cond/branch_7_fun/ppermute | solution.py:766
  7.8 10.2 %collective-permute-start.15 = (f32[232,128]{1,0:T(8,128)}, f32[232,128]{1,0:T(8,128)}, u32[]{:S(2)}, u32[]{:S(2)}) collective-permute-start(f32[232,128]{1,0:T(8,128)} %get-tuple-element.649), channel_id=1, source_target_pairs={{56,58},{57,57},{58,56},{59,63},{60,62},{61,61},{62,60},{63,59},{1... | collective-permute-start | bytes 356360 | tf_op jit(solution)/shard_map/cond/branch_7_fun/ppermute | solution.py:767
  18.0 13.1 %copy-start = (f32[1,8,4,4,32,128]{5,4,3,2,1,0:T(8,128)S(1)}, f32[1,8,4,4,32,128]{5,4,3,2,1,0:T(8,128)}, u32[]{:S(2)}) copy-start(f32[1,8,4,4,32,128]{5,4,3,2,1,0:T(8,128)} %param.34) | copy-start | bytes 6291460
  18.0 13.1 %copy-start.1 = (f32[2,1,32,32,128]{4,3,2,1,0:T(8,128)S(1)}, f32[2,1,32,32,128]{4,3,2,1,0:T(8,128)}, u32[]{:S(2)}) copy-start(f32[2,1,32,32,128]{4,3,2,1,0:T(8,128)} %param.33) | copy-start | bytes 3145732
  20.1 8.1 %collective-permute-start.74 = (f32[704,128]{1,0:T(8,128)S(1)}, f32[704,128]{1,0:T(8,128)S(1)}, u32[]{:S(2)}, u32[]{:S(2)}) collective-permute-start(f32[704,128]{1,0:T(8,128)S(1)} %get-tuple-element.1081), channel_id=1, source_target_pairs={{0,1},{1,2},{2,3},{3,4},{4,5},{5,6},{6,7},{7,0},{8,9},{9,10},{10,1... | collective-permute-start | bytes 1081352 | tf_op jit(solution)/shard_map/ppermute | solution.py:753
  20.1 8.1 %collective-permute-start.75 = (f32[704,128]{1,0:T(8,128)S(1)}, f32[704,128]{1,0:T(8,128)S(1)}, u32[]{:S(2)}, u32[]{:S(2)}) collective-permute-start(f32[704,128]{1,0:T(8,128)S(1)} %get-tuple-element.1082), channel_id=1, source_target_pairs={{0,7},{1,0},{2,1},{3,2},{4,3},{5,4},{6,5},{7,6},{8,15},{9,8},{10,9... | collective-permute-start | bytes 1081352 | tf_op jit(solution)/shard_map/ppermute | solution.py:753
  29.0 6.0 %collective-permute-start.76 = (f32[5,48,128]{2,1,0:T(8,128)S(1)}, f32[5,48,128]{2,1,0:T(8,128)S(1)}, u32[]{:S(2)}, u32[]{:S(2)}) collective-permute-start(f32[5,48,128]{2,1,0:T(8,128)S(1)} %get-tuple-element.1092), channel_id=1, source_target_pairs={{0,64},{1,65},{2,66},{3,67},{4,68},{5,69},{6,70},{7,71},{8,72},{9,... | collective-permute-start | bytes 368648 | tf_op jit(solution)/shard_map/ppermute | solution.py:756
  35.1 4.3 %collective-permute-start.47 = (f32[120,128]{1,0:T(8,128)S(1)}, f32[120,128]{1,0:T(8,128)S(1)}, u32[]{:S(2)}, u32[]{:S(2)}) collective-permute-start(f32[120,128]{1,0:T(8,128)S(1)} %get-tuple-element.881), channel_id=1, source_target_pairs={{0,8},{8,0},{1,9},{9,1},{2,10},{10,2},{3,11},{11,3},{4,12},{12,4},... | collective-permute-start | bytes 184328 | tf_op jit(solution)/shard_map/cond/branch_3_fun/ppermute | solution.py:750
  35.2 4.2 %collective-permute-start.48 = (f32[120,128]{1,0:T(8,128)S(1)}, f32[120,128]{1,0:T(8,128)S(1)}, u32[]{:S(2)}, u32[]{:S(2)}) collective-permute-start(f32[120,128]{1,0:T(8,128)S(1)} %get-tuple-element.882), channel_id=1, source_target_pairs={{8,16},{16,8},{9,17},{17,9},{10,18},{18,10},{11,19},{19,11},{12,20... | collective-permute-start | bytes 184328 | tf_op jit(solution)/shard_map/cond/branch_3_fun/ppermute | solution.py:750
  35.8 3.5 %collective-permute-start.50 = (f32[120,128]{1,0:T(8,128)S(1)}, f32[120,128]{1,0:T(8,128)S(1)}, u32[]{:S(2)}, u32[]{:S(2)}) collective-permute-start(f32[120,128]{1,0:T(8,128)S(1)} %get-tuple-element.883), channel_id=1, source_target_pairs={{120,122},{121,121},{122,120},{123,127},{124,126},{125,125},{126,1... | collective-permute-start | bytes 184328 | tf_op jit(solution)/shard_map/cond/branch_3_fun/ppermute | solution.py:823
  36.5 2.9 %collective-permute-start.49 = (f32[120,128]{1,0:T(8,128)S(1)}, f32[120,128]{1,0:T(8,128)S(1)}, u32[]{:S(2)}, u32[]{:S(2)}) collective-permute-start(f32[120,128]{1,0:T(8,128)S(1)} %get-tuple-element.883), channel_id=1, source_target_pairs={{120,123},{121,122},{122,121},{123,120},{124,127},{125,126},{126,1... | collective-permute-start | bytes 184328 | tf_op jit(solution)/shard_map/cond/branch_3_fun/ppermute | solution.py:823
  39.4 11.1 %collective-permute-start.51 = (f32[5,48,128]{2,1,0:T(8,128)S(1)}, f32[5,48,128]{2,1,0:T(8,128)S(1)}, u32[]{:S(2)}, u32[]{:S(2)}) collective-permute-start(f32[5,48,128]{2,1,0:T(8,128)S(1)} %get-tuple-element.884), channel_id=1, source_target_pairs={{0,64},{1,65},{2,66},{3,67},{4,68},{5,69},{6,70},{7,71},{8,72},{9,... | collective-permute-start | bytes 368648 | tf_op jit(solution)/shard_map/cond/branch_3_fun/ppermute | solution.py:756

commit v4 on v3

--- a/solution.py
+++ b/solution.py
@@ -572,7 +572,7 @@
             edges[2, n - 1, a] = reverse(merged[a][24:32])
         return carry
 
-    lax.fori_loop(1, BLOCKS, block, 0, unroll=True)
+    lax.fori_loop(1, BLOCKS, block, 0)
     for n in range(REST):
         for a in range(5):
             at = 24 * a + 3 * n
@@ -807,7 +807,6 @@
         (lam0, wind0, inv0, h, own, own_halo, *from_sides, x, hx),
         [VMEM] * (INPUTS + 2),
     )
-    received = across(payload)
     rest_args = (*state_in, rest_h, rest_own, rest_own_halo, *from_sides)
     whole = ((32, ROWS, COLS), HBM)
     done = pltpu.SemaphoreType.DMA((1,))
@@ -819,7 +818,8 @@
         [pltpu.VMEM((3, REST, 5, 8, COLS), F32), pltpu.VMEM((3, 120, COLS), F32)]
         + [pltpu.VMEM((5 * EXT, COLS), F32)] * 2,
     )
-    def finish(total, rest_rows, received, chain, rest_args):
+    def finish(total, rest_rows, payload, chain, rest_args):
+        received = across(payload)
         folded = [lax.ppermute(rest_rows[2], AXES, fold_pairs(total - k, (1,))) for k in range(2)]
         swapped = swap(*rest_rows[:2])
         x, hx, land, *tables, state = chain
@@ -852,7 +852,7 @@
         turn[0],
         [functools.partial(finish, total) for total in range(LON)],
         rest_rows,
-        received,
+        payload,
         (x, hx, land, *tables, state),
         (fold_map, inv, strip_inverse, land, rest_state, rest_coefs),
     )

time: 52.6 us -> 53.9 us (1.025)
  the two profiles are of different devices: /device:TPU:112 before, /device:TPU:114 now
where the time goes in v4:
time: 53.9 us; the launch traced here: 53.4 us
  Pallas kernels  21.1 us (39%)
  starting transfers between devices  21 us (39%)
  waiting for transfers between devices  9.41 us (17%)
  between operations  1.42 us (3%)
    pallas_call x8, Pallas kernels, call(): pl.pallas_call(kernel, out_shape=[jax.ShapeDtypeStruct(s, jnp.int32 if sp...  21.1 us
    ppermute x2, starting transfers between devices, across(): lax.ppermute(value, AXES, [(i, (i + LAT * LON) % (2 * LAT * LON)) for i i...  10.4 us
    ppermute x1, waiting for transfers between devices, around(): lax.ppermute(to_east, AXES, lon_pairs(1))  4.54 us
    ppermute x1, starting transfers between devices, across_fold(): lax.ppermute(mirror, AXES, fold_pairs(total - 1 + in_late_half, (0, 1)))  4.03 us
    ppermute x1, waiting for transfers between devices, across_fold(): lax.ppermute(high if in_late_half else low, AXES, fold_pairs(total - in_l...  2.8 us
    ppermute x2, waiting for transfers between devices, across(): lax.ppermute(value, AXES, [(i, (i + LAT * LON) % (2 * LAT * LON)) for i i...  2.05 us
    ppermute x1, starting transfers between devices, across_fold(): lax.ppermute(high if in_late_half else low, AXES, fold_pairs(total - in_l...  1.92 us
    ppermute x1, starting transfers between devices, around(): lax.ppermute(to_west, AXES, lon_pairs(-1))  1.67 us
  transfers between devices with their start and end apart: 12, of which 3 were waited for; matrix products, arithmetic and copies ran while one was open for 0% of the time, Pallas kernels for 18%

profile of v4, /device:TPU:114, one launch (start us, length us, event | category | flops | bytes accessed | tf_op | source)
XLA Modules:
  0.0 53.4 jit_solution(7349241003312202088)
XLA Ops:
  0.0 3.5 %shard_map.90 = (f32[4,4,32,128]{3,2,1,0:T(8,128)S(1)}, f32[464,128]{1,0:T(8,128)}, f32[464,128]{1,0:T(8,128)}, f32[464,128]{1,0:T(8,128)}, f32[232,128]{1,0:T(8...) custom-call(s32[1024]{0:T(1024)} %fold.3, f32[32,32,128]{2,1,0:T(8,128)} %bitcast.58, ...), custom_call_target="tpu_custom_call" | custom-call | bytes 11200000 | tf_op jit(solution)/shard_map/pallas_call | solution.py:684
  3.5 0.3 collective-permute-start.80
  3.8 0.7 %collective-permute-start.81 = (f32[464,128]{1,0:T(8,128)}, f32[464,128]{1,0:T(8,128)S(1)}, u32[]{:S(2)}, u32[]{:S(2)}) collective-permute-start(f32[464,128]{1,0:T(8,128)} %get-tuple-element.1057), channel_id=1, source_target_pairs={{8,16},{16,8},{9,17},{17,9},{10,18},{18,10},{11,19},{19,11},{12,20... | collective-permute-start | bytes 712712 | tf_op jit(solution)/shard_map/ppermute | solution.py:750
  5.1 0.0 copy-start.3
  5.1 12.4 %conditional.2 = (f32[464,128]{1,0:T(8,128)}, f32[232,128]{1,0:T(8,128)}, f32[12,32,128]{2,1,0:T(8,128)S(1)}, f32[96,128]{1,0:T(8,128)S(1)}, f32[96,128]{1,0:T(8...) conditional(s32[]{:T(128)} %bitcast.13, ...), branch_computations={%region_0.0_spmd, %region_1.0_spmd, %region_2.0_spmd, %region_3.0_... | conditional | bytes 15425576 | solution.py:787
  5.1 4.0 %collective-permute-start.2 = (f32[464,128]{1,0:T(8,128)}, f32[464,128]{1,0:T(8,128)}, u32[]{:S(2)}, u32[]{:S(2)}) collective-permute-start(f32[464,128]{1,0:T(8,128)} %get-tuple-element.558), channel_id=1, source_target_pairs={{56,56},{57,63},{58,62},{59,61},{60,60},{61,59},{62,58},{63,57},{1... | collective-permute-start | bytes 712712 | tf_op jit(solution)/shard_map/cond/branch_1_fun/ppermute | solution.py:766
  9.2 1.9 %collective-permute-start.3 = (f32[232,128]{1,0:T(8,128)}, f32[232,128]{1,0:T(8,128)}, u32[]{:S(2)}, u32[]{:S(2)}) collective-permute-start(f32[232,128]{1,0:T(8,128)} %get-tuple-element.559), channel_id=1, source_target_pairs={{56,63},{57,62},{58,61},{59,60},{60,59},{61,58},{62,57},{63,56},{1... | collective-permute-start | bytes 356360 | tf_op jit(solution)/shard_map/cond/branch_1_fun/ppermute | solution.py:767
  11.1 3.6 %branch_1_fun.4 = (f32[12,32,128]{2,1,0:T(8,128)S(1)}, f32[96,128]{1,0:T(8,128)S(1)}, f32[96,128]{1,0:T(8,128)S(1)}, f32[4,32,128]{2,1,0:T(8,128)S(1)}, f32[2,4,...) custom-call(f32[32,32,128]{2,1,0:T(8,128)S(1)} %get-tuple-element.56, ...), custom_call_target="tpu_custom_call" | custom-call | bytes 14000000 | tf_op jit(solution)/shard_map/cond/branch_1_fun/pallas_call | solution.py:684
  14.7 2.8 %collective-permute-done.3 = f32[232,128]{1,0:T(8,128)} collective-permute-done((f32[232,128]{1,0:T(8,128)}, f32[232,128]{1,0:T(8,128)}, u32[]{:S(2)}, u32[]{:S(2)}) %collective-permute-start.3) | collective-permute-done | bytes 118816 | tf_op jit(solution)/shard_map/cond/branch_1_fun/ppermute | solution.py:767
  17.5 0.0 collective-permute-done.2
  17.5 0.0 collective-permute-done.80.first_in
  17.5 0.0 collective-permute-done.81.second_in
  17.5 2.1 %shard_map.91 = (f32[7,4,16,128]{3,2,1,0:T(8,128)S(1)}, f32[4,4,16,128]{3,2,1,0:T(8,128)S(1)}, f32[12,16,128]{2,1,0:T(8,128)S(1)}, f32[7,3,4,16,128]{4,3,2,1,0:T...) custom-call(s32[1024]{0:T(1024)S(1)} %copy-done.3, ...), custom_call_target="tpu_custom_call" | custom-call | bytes 9800000 | tf_op jit(solution)/shard_map/pallas_call | solution.py:684
  19.6 0.1 collective-permute-start.82
  19.7 1.7 %collective-permute-start.83 = (f32[704,128]{1,0:T(8,128)S(1)}, f32[704,128]{1,0:T(8,128)S(1)}, u32[]{:S(2)}, u32[]{:S(2)}) collective-permute-start(f32[704,128]{1,0:T(8,128)S(1)} %get-tuple-element.1081), channel_id=1, source_target_pairs={{0,7},{1,0},{2,1},{3,2},{4,3},{5,4},{6,5},{7,6},{8,15},{9,8},{10,9... | collective-permute-start | bytes 1081352 | tf_op jit(solution)/shard_map/ppermute | solution.py:753
  21.9 4.5 %collective-permute-done.82.refs_6_ = f32[704,128]{1,0:T(8,128)S(1)} collective-permute-done((f32[704,128]{1,0:T(8,128)S(1)}, f32[704,128]{1,0:T(8,128)S(1)}, u32[]{:S(2)}, u32[]{:S(2)}) %collective-permute-start.82) | collective-permute-done | bytes 360480 | tf_op jit(solution)/shard_map/ppermute | solution.py:753
  26.5 0.0 collective-permute-done.83.refs_7_
  26.5 0.9 %shard_map.92 = (f32[5,48,128]{2,1,0:T(8,128)S(1)}, f32[5,48,128]{2,1,0:T(8,128)S(1)}, f32[240,128]{1,0:T(8,128)S(1)}, f32[240,128]{1,0:T(8,128)S(1)}, f32[240,1...) custom-call(f32[4,32,128]{2,1,0:T(8,128)S(1)} %get-tuple-element.107, ...), custom_call_target="tpu_custom_call" | custom-call | bytes 3500000 | tf_op jit(solution)/shard_map/pallas_call | solution.py:684
  27.4 4.3 %shard_map.93 = (f32[7,5,32,128]{3,2,1,0:T(8,128)S(1)}, f32[7,3,240,128]{3,2,1,0:T(8,128)S(1)}, f32[7,4,32,128]{3,2,1,0:T(8,128)S(1)}, f32[120,128]{1,0:T(8,128)...) custom-call(f32[32,32,128]{2,1,0:T(8,128)S(1)} %bitcast.75, f32[2,32,32,128]{3,2,1,0:T(8,128)S(1)} %bitcast.57, ...), custom_call_target="tpu_custom_call" | custom-call | bytes 15050000 | tf_op jit(solution)/shard_map/pallas_call | solution.py:684
  31.7 21.5 %conditional.3 = (f32[1,32,32,128]{3,2,1,0:T(8,128)}) conditional(s32[]{:T(128)} %bitcast.12, (f32[5,48,128]{2,1,0:T(8,128)S(1)}, f32[4,4,32,128]{3,2,1,0:T(8,128)S(1)}, f32[4,4,16,128]{3,2,1,0:T(8,128)S(1)}, f32[240,128]{1,0:T(8,128)S(1)}, f32[240,128]{1,0:T(8,128)S(1)}, /*index=5*/f32[240,128]{1,0:T(8,128)S(1)}, ...), branch_computations={%region_16.0_spmd, %region_17.0_spmd, %region_18.0_spmd, %region_1... | conditional | bytes 23316328 | solution.py:851
  31.7 1.4 %collective-permute-start.32 = (f32[5,48,128]{2,1,0:T(8,128)S(1)}, f32[5,48,128]{2,1,0:T(8,128)S(1)}, u32[]{:S(2)}, u32[]{:S(2)}) collective-permute-start(f32[5,48,128]{2,1,0:T(8,128)S(1)} %get-tuple-element.794), channel_id=1, source_target_pairs={{0,64},{1,65},{2,66},{3,67},{4,68},{5,69},{6,70},{7,71},{8,72},{9,... | collective-permute-start | bytes 368648 | tf_op jit(solution)/shard_map/cond/branch_0_fun/ppermute | solution.py:756
  33.1 0.0 collective-permute-start.33
  33.1 0.7 %collective-permute-start.34 = (f32[120,128]{1,0:T(8,128)S(1)}, f32[120,128]{1,0:T(8,128)S(1)}, u32[]{:S(2)}, u32[]{:S(2)}) collective-permute-start(f32[120,128]{1,0:T(8,128)S(1)} %get-tuple-element.798), channel_id=1, source_target_pairs={{8,16},{16,8},{9,17},{17,9},{10,18},{18,10},{11,19},{19,11},{12,20... | collective-permute-start | bytes 184328 | tf_op jit(solution)/shard_map/cond/branch_0_fun/ppermute | solution.py:750
  33.8 0.7 %collective-permute-start.36 = (f32[120,128]{1,0:T(8,128)S(1)}, f32[120,128]{1,0:T(8,128)S(1)}, u32[]{:S(2)}, u32[]{:S(2)}) collective-permute-start(f32[120,128]{1,0:T(8,128)S(1)} %get-tuple-element.799), channel_id=1, source_target_pairs={{120,127},{121,126},{122,125},{123,124},{124,123},{125,122},{126,1... | collective-permute-start | bytes 184328 | tf_op jit(solution)/shard_map/cond/branch_0_fun/ppermute | solution.py:823
  34.4 0.7 %collective-permute-start.35 = (f32[120,128]{1,0:T(8,128)S(1)}, f32[120,128]{1,0:T(8,128)S(1)}, u32[]{:S(2)}, u32[]{:S(2)}) collective-permute-start(f32[120,128]{1,0:T(8,128)S(1)} %get-tuple-element.799), channel_id=1, source_target_pairs={{120,120},{121,127},{122,126},{123,125},{124,124},{125,123},{126,1... | collective-permute-start | bytes 184328 | tf_op jit(solution)/shard_map/cond/branch_0_fun/ppermute | solution.py:823
  35.1 2.1 %collective-permute-done.32.received = f32[5,48,128]{2,1,0:T(8,128)S(1)} collective-permute-done((f32[5,48,128]{2,1,0:T(8,128)S(1)}, f32[5,48,128]{2,1,0:T(8,128)S(1)}, u32[]{:S(2)}, u32[]{:S(2)}) %collective-permute-start.32) | collective-permute-done | bytes 122912 | tf_op jit(solution)/shard_map/cond/branch_0_fun/ppermute | solution.py:756
  37.2 0.9 %branch_0_fun.5 = (f32[5,48,128]{2,1,0:T(8,128)S(1)}, f32[5,48,128]{2,1,0:T(8,128)S(1)}) custom-call(f32[4,4,32,128]{3,2,1,0:T(8,128)S(1)} %get-tuple-element.783.x_in, f32[4,4,16,128]{3,2,1,0:T(8,128)S(1)} %get-tuple-element.784.hx, f32[240,128]{1,0:T(8,128)S(1)} %get-tuple-element.785.land.refs_3_, f32[240,128]{1,0:T(8,128)S(1)} %get-tuple-element.788.to_south, ...), custom_call_target="tpu_custom_call" | custom-call | bytes 3500000 | tf_op jit(solution)/shard_map/cond/branch_0_fun/pallas_call | solution.py:684
  38.0 0.0 collective-permute-done.33.refs_6_
  38.0 0.0 collective-permute-done.34.refs_7_
  38.1 9.0 %collective-permute-start.37 = (f32[5,48,128]{2,1,0:T(8,128)S(1)}, f32[5,48,128]{2,1,0:T(8,128)S(1)}, u32[]{:S(2)}, u32[]{:S(2)}) collective-permute-start(f32[5,48,128]{2,1,0:T(8,128)S(1)} %get-tuple-element.800), channel_id=1, source_target_pairs={{0,64},{1,65},{2,66},{3,67},{4,68},{5,69},{6,70},{7,71},{8,72},{9,... | collective-permute-start | bytes 368648 | tf_op jit(solution)/shard_map/cond/branch_0_fun/ppermute | solution.py:756
  47.1 4.9 %branch_0_fun.6.rest = f32[32,32,128]{2,1,0:T(8,128)} custom-call(s32[1024]{0:T(1024)S(1)} %get-tuple-element.802.refs_0_, f32[8,4,4,32,128]{4,3,2,1,0:T(8,128)S(1)} %get-tuple-element.803.refs_1_, f32[7,4,32,128]{3,2,1,0:T(8,128)S(1)} %get-tuple-element.804.refs_2_, f32[240,128]{1,0:T(8,128)S(1)} %get-tuple-element.785.land.refs_3_, ...), custom_call_target="tpu_custom_call" | custom-call | bytes 16099999 | tf_op jit(solution)/shard_map/cond/branch_0_fun/pallas_call | solution.py:684
  52.1 0.9 %branch_0_fun.7 = f32[32,32,128]{2,1,0:T(8,128)} custom-call(f32[4,4,32,128]{3,2,1,0:T(8,128)S(1)} %get-tuple-element.783.x_in, f32[4,4,16,128]{3,2,1,0:T(8,128)S(1)} %get-tuple-element.784.hx, f32[240,128]{1,0:T(8,128)S(1)} %get-tuple-element.785.land.refs_3_, f32[4,48,128]{2,1,0:T(8,128)S(1)} %get-tuple-element.786.strip_coefs, ...), custom_call_target="tpu_custom_call", output_to_operand_aliasing={{}: (7, {})} | custom-call | bytes 1750000 | tf_op jit(solution)/shard_map/cond/branch_0_fun/pallas_call | solution.py:684
  (10 shorter events, 0.0 us)
Async XLA Ops:
  0.0 5.1 %copy-start.2 = (f32[1,32,32,128]{3,2,1,0:T(8,128)S(1)}, f32[1,32,32,128]{3,2,1,0:T(8,128)}, u32[]{:S(2)}) copy-start(f32[1,32,32,128]{3,2,1,0:T(8,128)} %param.32) | copy-start | bytes 1572868
  3.5 14.0 %collective-permute-start.80 = (f32[464,128]{1,0:T(8,128)}, f32[464,128]{1,0:T(8,128)S(1)}, u32[]{:S(2)}, u32[]{:S(2)}) collective-permute-start(f32[464,128]{1,0:T(8,128)} %get-tuple-element.1056), channel_id=1, source_target_pairs={{0,8},{8,0},{1,9},{9,1},{2,10},{10,2},{3,11},{11,3},{4,12},{12,4},... | collective-permute-start | bytes 712712 | tf_op jit(solution)/shard_map/ppermute | solution.py:750
  3.8 13.7 %collective-permute-start.81 = (f32[464,128]{1,0:T(8,128)}, f32[464,128]{1,0:T(8,128)S(1)}, u32[]{:S(2)}, u32[]{:S(2)}) collective-permute-start(f32[464,128]{1,0:T(8,128)} %get-tuple-element.1057), channel_id=1, source_target_pairs={{8,16},{16,8},{9,17},{17,9},{10,18},{18,10},{11,19},{19,11},{12,20... | collective-permute-start | bytes 712712 | tf_op jit(solution)/shard_map/ppermute | solution.py:750
  5.1 12.4 %copy-start.3 = (s32[1024]{0:T(1024)S(1)}, s32[1024]{0:T(1024)}, u32[]{:S(2)}) copy-start(s32[1024]{0:T(1024)} %fold.3) | copy-start | bytes 12292
  5.1 12.4 %collective-permute-start.2 = (f32[464,128]{1,0:T(8,128)}, f32[464,128]{1,0:T(8,128)}, u32[]{:S(2)}, u32[]{:S(2)}) collective-permute-start(f32[464,128]{1,0:T(8,128)} %get-tuple-element.558), channel_id=1, source_target_pairs={{56,56},{57,63},{58,62},{59,61},{60,60},{61,59},{62,58},{63,57},{1... | collective-permute-start | bytes 712712 | tf_op jit(solution)/shard_map/cond/branch_1_fun/ppermute | solution.py:766
  9.2 8.3 %collective-permute-start.3 = (f32[232,128]{1,0:T(8,128)}, f32[232,128]{1,0:T(8,128)}, u32[]{:S(2)}, u32[]{:S(2)}) collective-permute-start(f32[232,128]{1,0:T(8,128)} %get-tuple-element.559), channel_id=1, source_target_pairs={{56,63},{57,62},{58,61},{59,60},{60,59},{61,58},{62,57},{63,56},{1... | collective-permute-start | bytes 356360 | tf_op jit(solution)/shard_map/cond/branch_1_fun/ppermute | solution.py:767
  17.5 9.9 %copy-start = (f32[1,8,4,4,32,128]{5,4,3,2,1,0:T(8,128)S(1)}, f32[1,8,4,4,32,128]{5,4,3,2,1,0:T(8,128)}, u32[]{:S(2)}) copy-start(f32[1,8,4,4,32,128]{5,4,3,2,1,0:T(8,128)} %param.34) | copy-start | bytes 6291460
  17.5 9.9 %copy-start.1 = (f32[2,1,32,32,128]{4,3,2,1,0:T(8,128)S(1)}, f32[2,1,32,32,128]{4,3,2,1,0:T(8,128)}, u32[]{:S(2)}) copy-start(f32[2,1,32,32,128]{4,3,2,1,0:T(8,128)} %param.33) | copy-start | bytes 3145732
  19.6 6.9 %collective-permute-start.82 = (f32[704,128]{1,0:T(8,128)S(1)}, f32[704,128]{1,0:T(8,128)S(1)}, u32[]{:S(2)}, u32[]{:S(2)}) collective-permute-start(f32[704,128]{1,0:T(8,128)S(1)} %get-tuple-element.1080), channel_id=1, source_target_pairs={{0,1},{1,2},{2,3},{3,4},{4,5},{5,6},{6,7},{7,0},{8,9},{9,10},{10,1... | collective-permute-start | bytes 1081352 | tf_op jit(solution)/shard_map/ppermute | solution.py:753
  19.7 6.8 %collective-permute-start.83 = (f32[704,128]{1,0:T(8,128)S(1)}, f32[704,128]{1,0:T(8,128)S(1)}, u32[]{:S(2)}, u32[]{:S(2)}) collective-permute-start(f32[704,128]{1,0:T(8,128)S(1)} %get-tuple-element.1081), channel_id=1, source_target_pairs={{0,7},{1,0},{2,1},{3,2},{4,3},{5,4},{6,5},{7,6},{8,15},{9,8},{10,9... | collective-permute-start | bytes 1081352 | tf_op jit(solution)/shard_map/ppermute | solution.py:753
  31.7 5.4 %collective-permute-start.32 = (f32[5,48,128]{2,1,0:T(8,128)S(1)}, f32[5,48,128]{2,1,0:T(8,128)S(1)}, u32[]{:S(2)}, u32[]{:S(2)}) collective-permute-start(f32[5,48,128]{2,1,0:T(8,128)S(1)} %get-tuple-element.794), channel_id=1, source_target_pairs={{0,64},{1,65},{2,66},{3,67},{4,68},{5,69},{6,70},{7,71},{8,72},{9,... | collective-permute-start | bytes 368648 | tf_op jit(solution)/shard_map/cond/branch_0_fun/ppermute | solution.py:756
  33.1 4.9 %collective-permute-start.33 = (f32[120,128]{1,0:T(8,128)S(1)}, f32[120,128]{1,0:T(8,128)S(1)}, u32[]{:S(2)}, u32[]{:S(2)}) collective-permute-start(f32[120,128]{1,0:T(8,128)S(1)} %get-tuple-element.797), channel_id=1, source_target_pairs={{0,8},{8,0},{1,9},{9,1},{2,10},{10,2},{3,11},{11,3},{4,12},{12,4},... | collective-permute-start | bytes 184328 | tf_op jit(solution)/shard_map/cond/branch_0_fun/ppermute | solution.py:750
  33.1 4.9 %collective-permute-start.34 = (f32[120,128]{1,0:T(8,128)S(1)}, f32[120,128]{1,0:T(8,128)S(1)}, u32[]{:S(2)}, u32[]{:S(2)}) collective-permute-start(f32[120,128]{1,0:T(8,128)S(1)} %get-tuple-element.798), channel_id=1, source_target_pairs={{8,16},{16,8},{9,17},{17,9},{10,18},{18,10},{11,19},{19,11},{12,20... | collective-permute-start | bytes 184328 | tf_op jit(solution)/shard_map/cond/branch_0_fun/ppermute | solution.py:750
  33.8 4.3 %collective-permute-start.36 = (f32[120,128]{1,0:T(8,128)S(1)}, f32[120,128]{1,0:T(8,128)S(1)}, u32[]{:S(2)}, u32[]{:S(2)}) collective-permute-start(f32[120,128]{1,0:T(8,128)S(1)} %get-tuple-element.799), channel_id=1, source_target_pairs={{120,127},{121,126},{122,125},{123,124},{124,123},{125,122},{126,1... | collective-permute-start | bytes 184328 | tf_op jit(solution)/shard_map/cond/branch_0_fun/ppermute | solution.py:823
  34.4 3.6 %collective-permute-start.35 = (f32[120,128]{1,0:T(8,128)S(1)}, f32[120,128]{1,0:T(8,128)S(1)}, u32[]{:S(2)}, u32[]{:S(2)}) collective-permute-start(f32[120,128]{1,0:T(8,128)S(1)} %get-tuple-element.799), channel_id=1, source_target_pairs={{120,120},{121,127},{122,126},{123,125},{124,124},{125,123},{126,1... | collective-permute-start | bytes 184328 | tf_op jit(solution)/shard_map/cond/branch_0_fun/ppermute | solution.py:823
  38.1 14.0 %collective-permute-start.37 = (f32[5,48,128]{2,1,0:T(8,128)S(1)}, f32[5,48,128]{2,1,0:T(8,128)S(1)}, u32[]{:S(2)}, u32[]{:S(2)}) collective-permute-start(f32[5,48,128]{2,1,0:T(8,128)S(1)} %get-tuple-element.800), channel_id=1, source_target_pairs={{0,64},{1,65},{2,66},{3,67},{4,68},{5,69},{6,70},{7,71},{8,72},{9,... | collective-permute-start | bytes 368648 | tf_op jit(solution)/shard_map/cond/branch_0_fun/ppermute | solution.py:756
